TPU v7x, 128 devices: a whole 4x4x4 slice. The times are simulated.
128 devices in a mesh: replica: 8 (over x_hi, z), fsdp: 16 (over y, x_lo, core).
Axes of the slice: x: 4 (x_hi: 2, x_lo: 2; x = x_hi * 2 + x_lo), y: 4, z: 4, core: 2. Of those that a mesh axis runs over, the one named last changes fastest.
Arguments:
- inner_weight: float32 [8, 4608, 2048], P('replica', 'fsdp'), may hold values from -6 to 6
- first_moment: float32 [8, 4608, 2048], P('replica', 'fsdp'), may hold values from -4 to 4
- second_moment: float32 [8, 4608, 2048], P('replica', 'fsdp'), may hold values from 0.01 to 2
- outer_weight: float32 [4608, 2048], P('fsdp', 'replica'), may hold values from -6 to 6
- outer_momentum: float32 [4608, 2048], P('fsdp', 'replica'), may hold values from -4 to 4
- activations: bfloat16 [8, 8192, 4608], P('replica', 'fsdp'), may hold values from -6 to 6
- out_grads: bfloat16 [8, 8192, 2048], P('replica', 'fsdp'), may hold values from -0.0625 to 0.0625
Outputs:
- inner_next: float32 [8, 4608, 2048], P('replica', 'fsdp')
- first_next: float32 [8, 4608, 2048], P('replica', 'fsdp')
- second_next: float32 [8, 4608, 2048], P('replica', 'fsdp')
- outer_next: float32 [4608, 2048], P('fsdp', 'replica')
- momentum_next: float32 [4608, 2048], P('fsdp', 'replica')
All inputs are finite; a program needn't handle non-finite values.
Results may differ from a plain program's by a relative error of at most 0.0003.
Values may be sent and summed in bfloat16 or wider, within the bound.
No kernel may reach another device: no remote copies, remote signals or barrier semaphores. Data moves between devices by JAX's collectives and lax.ppermute only.
A program may use at most 128 MiB of HBM per device.

v0:
```python
import jax
import jax.numpy as jnp
from jax import lax
from jax.sharding import PartitionSpec as P

outer_rate = 0.7
outer_decay = 0.9
mix_share = 0.5
beta_one = 0.9
beta_two = 0.95
inner_rate = 0.05
weight_decay = 0.1
epsilon = 1e-08
step_count = 200.0


def local(
    inner_weight, first_moment, second_moment, outer_weight, outer_momentum, activations, out_grads
):
    replicas = lax.axis_size("replica")
    summed = lax.psum_scatter(inner_weight[0], "replica", scatter_dimension=1, tiled=True)
    average = outer_weight - summed / replicas
    momentum_next = outer_decay * outer_momentum + average
    outer_next = outer_weight - outer_rate * (average + outer_decay * momentum_next)
    full_outer = lax.all_gather(outer_next, "replica", axis=1, tiled=True)
    blended = mix_share * full_outer + (1.0 - mix_share) * inner_weight[0]
    inputs = activations[0]
    cotangents = out_grads[0]
    grad = lax.psum_scatter(
        lax.dot_general(
            inputs, cotangents, (((0,), (0,)), ((), ())), preferred_element_type=jnp.float32
        ),
        "fsdp",
        scatter_dimension=0,
        tiled=True,
    )
    first_next = beta_one * first_moment[0] + (1.0 - beta_one) * grad
    second_next = beta_two * second_moment[0] + (1.0 - beta_two) * grad * grad
    corr_one = 1.0 - beta_one**step_count
    corr_two = 1.0 - beta_two**step_count
    update = first_next / corr_one / (jnp.sqrt(second_next / corr_two) + epsilon)
    inner_next = blended - inner_rate * (update + weight_decay * blended)
    return (inner_next[None], first_next[None], second_next[None], outer_next, momentum_next)


def solution(mesh):
    in_specs = (
        P("replica", "fsdp", None),
        P("replica", "fsdp", None),
        P("replica", "fsdp", None),
        P("fsdp", "replica"),
        P("fsdp", "replica"),
        P("replica", "fsdp", None),
        P("replica", "fsdp", None),
    )
    out_specs = (
        P("replica", "fsdp", None),
        P("replica", "fsdp", None),
        P("replica", "fsdp", None),
        P("fsdp", "replica"),
        P("fsdp", "replica"),
    )
    return jax.shard_map(local, mesh=mesh, in_specs=in_specs, out_specs=out_specs, check_vma=False)
```

profile of v0, /device:TPU:0, one launch (start us, length us, event | category | flops | bytes accessed | tf_op | source)
XLA Modules:
  0.0 533.3 jit_solution(4996034587574248067)
XLA Ops:
  8.0 0.0 copy-start
  8.0 0.0 copy-start.1
  8.0 0.0 copy-start.2
  8.0 0.0 reduce-scatter.3.cloned.1.call-start
  8.1 0.7 reduce-scatter.3.cloned.1.call-update
  8.8 0.0 all-gather.2.cloned.1.call-start
  8.8 83.0 %reduce-scatter.3.cloned.1.call-done = f32[288,256]{1,0:T(8,128)} async-done(((f32[288,2048]{1,0:T(8,128)}), f32[288,256]{1,0:T(8,128)}) %reduce-scatter.3.cloned.1.call-update) | async-done | bytes 294928 | tf_op jit(solution)/shard_map/reduce_scatter | solution.py:21
  91.8 0.0 copy-done.1
  91.8 0.0 copy-done.2
  91.8 1.9 multiply_subtract_fusion
  93.7 0.0 all-gather.2.cloned.1.call-update
  93.7 0.0 reduce-scatter.5.cloned.1.call-start
  93.7 0.0 copy-done
  93.7 18.1 %fusion = f32[4608,2048]{1,0:T(8,128)} fusion(bf16[1,512,4608]{2,1,0:T(8,128)(2,1)} %param.12, bf16[1,512,2048]{2,1,0:T(8,128)(2,1)S(1)} %copy-done), kind=kOutput, calls=%fused_computation | convolution fusion | flops 9663676416 | bytes 44564480 | tf_op jit(solution)/shard_map/dot_general | solution.py:30
  111.9 0.0 reduce-scatter.5.cloned.1.call-update
  111.9 43.2 %all-gather.2.cloned.1.call-done = f32[288,2048]{1,0:T(8,128)} async-done(((f32[288,256]{1,0:T(8,128)}), f32[288,2048]{1,0:T(8,128)}) %all-gather.2.cloned.1.call-update) | async-done | bytes 2359312 | tf_op jit(solution)/shard_map/all_gather | solution.py:25
  155.1 361.1 %reduce-scatter.5.cloned.1.call-done = f32[288,2048]{1,0:T(8,128)} async-done(((f32[4608,2048]{1,0:T(8,128)}), f32[288,2048]{1,0:T(8,128)}) %reduce-scatter.5.cloned.1.call-update) | async-done | bytes 2359312 | tf_op jit(solution)/shard_map/reduce_scatter | solution.py:29
  516.2 9.6 %fusion.5 = (f32[1,288,2048]{2,1,0:T(8,128)}, f32[1,288,2048]{2,1,0:T(8,128)}, f32[1,288,2048]{2,1,0:T(8,128)}) fusion(f32[288,2048]{1,0:T(8,128)} %reduce-scatter.5.cloned.1.call-done, f32[1,288,2048]{2,1,0:T(8,128)} %param.9, f32[1,288,2048]{2,1,0:T(8,128)} %param.8, f32[288,2048]{1,0:T(8,128)} %all-gather.2.cloned.1.call-done, f32[1,288,2048]{2,1,0:T(8,128)} %param.7), kind=kLoop, calls=%fused_computation.8 | loop fusion | flops 9437184 | bytes 18874368 | tf_op jit(solution)/shard_map/broadcast_in_dim | solution.py:43
Async XLA Ops:
  8.0 85.7 %copy-start = (bf16[1,512,2048]{2,1,0:T(8,128)(2,1)S(1)}, bf16[1,512,2048]{2,1,0:T(8,128)(2,1)}, u32[]{:S(2)}) copy-start(bf16[1,512,2048]{2,1,0:T(8,128)(2,1)} %param.13) | copy-start | bytes 6291460
  8.0 83.8 %copy-start.1 = (f32[288,256]{1,0:T(8,128)S(1)}, f32[288,256]{1,0:T(8,128)}, u32[]{:S(2)}) copy-start(f32[288,256]{1,0:T(8,128)} %param.10) | copy-start | bytes 884740
  8.0 83.8 %copy-start.2 = (f32[288,256]{1,0:T(8,128)S(1)}, f32[288,256]{1,0:T(8,128)}, u32[]{:S(2)}) copy-start(f32[288,256]{1,0:T(8,128)} %param.11) | copy-start | bytes 884740
  8.0 83.8 %reduce-scatter.3.cloned.1.call-start = ((), (), s32[]{:S(2)}) async-start(), calls=%async_computation.2 | async-start | bytes 2654208 | tf_op jit(solution)/shard_map/reduce_scatter | solution.py:21
  8.8 146.3 %all-gather.2.cloned.1.call-start = ((), (), s32[]{:S(2)}) async-start(), calls=%async_computation.3 | async-start | bytes 2654208 | tf_op jit(solution)/shard_map/all_gather | solution.py:25
  93.7 422.5 %reduce-scatter.5.cloned.1.call-start = ((), (), s32[]{:S(2)}) async-start(), calls=%async_computation.4 | async-start | bytes 40108032 | tf_op jit(solution)/shard_map/reduce_scatter | solution.py:29
Sparse Core Ops, SparseCore 0:
  12.6 79.1 reduce-scatter.2
  94.6 60.4 all-gather.1
Sparse Core Ops, SparseCore 1:
  112.0 404.1 reduce-scatter.4
where the time goes:
time: 533 us
  waiting for transfers between devices  488 us (92%)
  matrix products  18.1 us (3%)
  between operations  15.5 us (3%)
  other arithmetic  11.5 us (2%)
    reduce_scatter x1, waiting for transfers between devices, local(): lax.psum_scatter(lax.dot_general(inputs, cotangents, (((0,), (0,)), ((),...  361 us
    reduce_scatter x1, waiting for transfers between devices, local(): lax.psum_scatter(inner_weight[0], 'replica', scatter_dimension=1, tiled=T...  83 us
    all_gather x1, waiting for transfers between devices, local(): full_outer = lax.all_gather(outer_next, 'replica', axis=1, tiled=True)  43.2 us
    dot_general x1, matrix products, local(): lax.dot_general(inputs, cotangents, (((0,), (0,)), ((), ())), preferred_e...  18.1 us
  transfers between devices with their start and end apart: 3, of which 3 were waited for; matrix products, arithmetic and copies ran while one was open for 3% of the time, Pallas kernels for 0%

commit v1 on v0

v1 whole, which is shorter than its diff:
```python
import functools

import jax
import jax.numpy as jnp
from jax import lax
from jax.experimental import pallas as pl
from jax.experimental.pallas import tpu as pltpu
from jax.sharding import PartitionSpec as P

outer_rate = 0.7
outer_decay = 0.9
mix_share = 0.5
beta_one = 0.9
beta_two = 0.95
inner_rate = 0.05
weight_decay = 0.1
epsilon = 1e-08
step_count = 200.0
corr_one = 1.0 - beta_one**step_count
corr_two = 1.0 - beta_two**step_count

NY, NX, NC, NZ, NH = 4, 2, 2, 4, 2
WA, B1, B2 = 640, 256, 512
CA, CB = 2 * WA, B1 + B2
ORDER = (2, 1, 3, 0)
VMEM = 40 * 2**20


def along_fsdp(move):
    where = [(y, x, c) for y in range(NY) for x in range(NX) for c in range(NC)]
    number = lambda y, x, c: ((y % NY) * NX + x) * NC + c
    return [(number(*place), number(*move(*place))) for place in where]


def along_replica(move):
    where = [(h, z) for h in range(NH) for z in range(NZ)]
    number = lambda h, z: h * NZ + z % NZ
    return [(number(*place), number(*move(*place))) for place in where]


UP = along_fsdp(lambda y, x, c: (y + 1, x, c))
DOWN = along_fsdp(lambda y, x, c: (y - 1, x, c))
ACROSS = along_fsdp(lambda y, x, c: (y, 1 - x, c))
TWIN = along_fsdp(lambda y, x, c: (y, x, 1 - c))
FAR = along_replica(lambda h, z: (1 - h, z))
AHEAD = [along_replica(lambda h, z, k=k: (h, z + k)) for k in range(NZ)]


def on_fsdp(value, pairs):
    return lax.ppermute(value, "fsdp", pairs)


def on_replica(value, pairs):
    return lax.ppermute(value, "replica", pairs)


def coded(value):
    return (value * jnp.abs(value) * (value * value)).astype(jnp.bfloat16)


def decoded(code):
    code = code.astype(jnp.float32)
    root = lax.rsqrt(lax.rsqrt(jnp.abs(code)))
    return jnp.where(code < 0.0, -root, root)


def coded_outer(value):
    value = value * 4096.0
    square = value * value
    fourth = square * square
    return (value * jnp.abs(value) * square * fourth).astype(jnp.bfloat16)


def decoded_outer(code):
    code = code.astype(jnp.float32)
    root = jnp.sqrt(lax.rsqrt(lax.rsqrt(jnp.abs(code)))) * (1.0 / 4096.0)
    return jnp.where(code < 0.0, -root, root)


def params(vmem=VMEM):
    return pltpu.CompilerParams(vmem_limit_bytes=vmem)


def cost(flops, moved):
    return pl.CostEstimate(flops=int(flops), bytes_accessed=int(moved), transcendentals=0)


def prepare(place, activations, distances):
    tokens, width = activations.shape
    quarter = width // NY
    rows = quarter // (NX * NC)
    first, count = distances

    def distance(i):
        step = first + i
        return jnp.where(step == 0, 2, jnp.where(step == 1, 1, jnp.where(step == 2, 3, 0)))

    def kernel(place_ref, a_ref, own_ref, send_ref, turned):
        turned[...] = a_ref[...].T
        x, core = place_ref[1], place_ref[2]
        for dx in range(NX):
            column = (x + dx) % NX
            own = pl.multiple_of((column * NC + core) * rows, 16)
            other = pl.multiple_of((column * NC + 1 - core) * rows, 16)
            own_ref[dx] = turned[pl.ds(own, rows), :]
            send_ref[dx] = turned[pl.ds(other, rows), :]

    shape = jax.ShapeDtypeStruct((NX * count, rows, tokens), jnp.bfloat16)
    spec = pl.BlockSpec((NX, rows, tokens), lambda i, s: (i, 0, 0))
    return pl.pallas_call(
        kernel,
        out_shape=(shape, shape),
        grid_spec=pltpu.PrefetchScalarGridSpec(
            num_scalar_prefetch=1,
            grid=(count,),
            in_specs=[pl.BlockSpec((tokens, quarter), lambda i, s: (0, (s[0] + distance(i)) % NY))],
            out_specs=(spec, spec),
            scratch_shapes=[pltpu.VMEM((quarter, tokens), jnp.bfloat16)],
        ),
        compiler_params=params(),
        cost_estimate=cost(0, 2 * tokens * quarter * count * 2),
    )(place, activations)


def multiplied(left_own, left_twin, right_own, right_twin):
    return jnp.dot(left_own, right_own, preferred_element_type=jnp.float32) + jnp.dot(
        left_twin, right_twin, preferred_element_type=jnp.float32
    )


def product(lefts, rights, blocks, columns, received=()):
    start, step, count = blocks
    width, place = columns
    rows, depth = lefts[0].shape[1:]

    def kernel(lo, lt, ro, rt, *rest):
        out = rest[-1]
        total = multiplied(lo[0], lt[0], ro[...], rt[...])
        for code in rest[:-1]:
            total = total + decoded(code[0])
        out[0] = coded(total)

    left = pl.BlockSpec((1, rows, depth), lambda i: (start + step * i, 0, 0))
    right = pl.BlockSpec((depth, width), lambda i: (0, place))
    block = pl.BlockSpec((1, rows, width), lambda i: (i, 0, 0))
    return pl.pallas_call(
        kernel,
        out_shape=jax.ShapeDtypeStruct((count, rows, width), jnp.bfloat16),
        grid=(count,),
        in_specs=[left, left, right, right] + [block] * len(received),
        out_specs=block,
        compiler_params=params(),
        cost_estimate=cost(
            4 * count * rows * width * depth,
            4 * depth * (count * rows + width) + 2 * count * rows * width * (1 + len(received)),
        ),
    )(*lefts, *rights, *received)


def narrow(lefts, rights, blocks):
    start, step, count = blocks
    rows, depth = lefts[0].shape[1:]

    def kernel(lo, lt, ro1, rt1, ro2, rt2, out):
        out[0, :, :B1] = coded(multiplied(lo[0], lt[0], ro1[...], rt1[...]))
        out[0, :, B1:] = coded(multiplied(lo[0], lt[0], ro2[...], rt2[...]))

    left = pl.BlockSpec((1, rows, depth), lambda i: (start + step * i, 0, 0))
    near = pl.BlockSpec((depth, B1), lambda i: (0, CA // B1))
    far = pl.BlockSpec((depth, B2), lambda i: (0, (CA + B1) // B2))
    return pl.pallas_call(
        kernel,
        out_shape=jax.ShapeDtypeStruct((count, rows, CB), jnp.bfloat16),
        grid=(count,),
        in_specs=[left, left, near, near, far, far],
        out_specs=pl.BlockSpec((1, rows, CB), lambda i: (i, 0, 0)),
        compiler_params=params(),
        cost_estimate=cost(
            4 * count * rows * CB * depth, 4 * depth * (count * rows + CB) + 2 * count * rows * CB
        ),
    )(*lefts, *rights, *rights)


def middle(lefts, rights, block, columns, inner_half, across, received=()):
    rows, depth = lefts[0].shape[1:]
    width, place = columns
    row_block, = inner_half

    def kernel(lo, lt, ro, rt, code, *rest):
        out = rest[-1]
        total = multiplied(lo[0], lt[0], ro[...], rt[...])
        sent = code[0, :, :B1] if width == B1 else code[0, :, B1:]
        total = total + decoded(sent)
        for more in rest[:-1]:
            total = total + decoded(more[...])
        out[...] = coded(total)

    left = pl.BlockSpec((1, rows, depth), lambda i: (block, 0, 0))
    right = pl.BlockSpec((depth, width), lambda i: (0, place))
    whole = pl.BlockSpec((rows, width), lambda i: (0, 0))
    return pl.pallas_call(
        kernel,
        out_shape=jax.ShapeDtypeStruct((rows, width), jnp.bfloat16),
        grid=(1,),
        in_specs=[left, left, right, right, pl.BlockSpec((1, rows, CB), lambda i: (row_block, 0, 0))]
        + [whole] * len(received),
        out_specs=whole,
        compiler_params=params(),
        cost_estimate=cost(4 * rows * width * depth, 4 * depth * (rows + width) + 8 * rows * width),
    )(*lefts, *rights, across, *received)


def turn(lefts, rights, received):
    rows, depth = lefts[0].shape[1:]
    block = lefts[0].shape[0] - 1

    def kernel(lo, lt, ro, rt, *rest):
        out = rest[-1]
        total = multiplied(lo[0], lt[0], ro[...], rt[...])
        first, second = rest[0], rest[1]
        half = pl.program_id(0)

        @pl.when(half == 0)
        def _():
            out[...] = coded(total + decoded(rest[0][0]) + decoded(rest[1][0]))

        @pl.when(half == 1)
        def _():
            out[...] = coded(total + decoded(rest[2][0]) + decoded(rest[3][0]))

    left = pl.BlockSpec((1, rows, depth), lambda i: (block, 0, 0))
    right = pl.BlockSpec((depth, WA), lambda i: (0, i))
    code = pl.BlockSpec((1, rows, WA), lambda i: (1, 0, 0))
    return pl.pallas_call(
        kernel,
        out_shape=jax.ShapeDtypeStruct((rows, CA), jnp.bfloat16),
        grid=(2,),
        in_specs=[left, left, right, right] + [code] * 4,
        out_specs=pl.BlockSpec((rows, WA), lambda i: (0, i)),
        compiler_params=params(),
        cost_estimate=cost(4 * rows * CA * depth, 4 * depth * (rows + CA) + 10 * rows * CA),
    )(*lefts, *rights, *received)


def adam(total, blended, first, second, inner_out, first_out, second_out):
    first_next = beta_one * first + (1.0 - beta_one) * total
    second_next = beta_two * second + (1.0 - beta_two) * total * total
    update = first_next / corr_one / (jnp.sqrt(second_next / corr_two) + epsilon)
    inner_out[...] = blended - inner_rate * (update + weight_decay * blended)
    first_out[...] = first_next
    second_out[...] = second_next


def finish(lefts, rights, columns, codes, states, outs):
    rows, depth = lefts[0].shape[1:]
    block = lefts[0].shape[0] - 2
    width, place = columns
    cuts = 3
    part = rows // cuts
    n = len(codes)

    def kernel(lo, lt, ro, rt, *rest):
        total = multiplied(lo[0], lt[0], ro[...], rt[...])
        for code in rest[:n]:
            value = code[0] if len(code.shape) == 3 else code[...]
            total = total + decoded(value)
        blended, first, second = rest[n : n + 3]
        adam(total, blended[...], first[...], second[...], *rest[-3:])

    left = pl.BlockSpec((1, part, depth), lambda i: (block, i, 0))
    right = pl.BlockSpec((depth, width), lambda i: (0, place))
    state = pl.BlockSpec((part, width), lambda i: (i, place))
    specs = []
    for array, at in codes:
        if array.ndim == 3:
            specs.append(pl.BlockSpec((1, part, width), lambda i, at=at: (at[0], i, at[1])))
        else:
            specs.append(pl.BlockSpec((part, width), lambda i, at=at: (i, at[1])))
    arrays = [array for array, _ in codes]
    shape = jax.ShapeDtypeStruct(states[0].shape, jnp.float32)
    operands = [*lefts, *rights, *arrays, *states]
    aliases = {}
    if outs is not None:
        aliases = {len(operands) + i: i for i in range(3)}
        operands += list(outs)
    return pl.pallas_call(
        (lambda *refs: kernel(*refs[: 7 + n], *refs[-3:])),
        out_shape=(shape,) * 3,
        grid=(cuts,),
        in_specs=[left, left, right, right]
        + specs
        + [state] * 3
        + ([pl.BlockSpec(memory_space=pl.ANY)] * 3 if outs is not None else []),
        out_specs=(state,) * 3,
        input_output_aliases=aliases,
        compiler_params=params(),
        cost_estimate=cost(4 * rows * width * depth, 4 * depth * (rows + width) + 32 * rows * width),
    )(*operands)


def scatter_blocks(place, inner):
    rows, width = inner.shape
    block = width // (NZ * NH)

    def kernel(place_ref, *refs):
        for source, target in zip(refs[: NZ - 1], refs[NZ - 1 :]):
            target[0] = source[...]

    def source(k):
        return pl.BlockSpec(
            (rows, block), lambda i, s: (0, ((s[4] + i) % NH) * NZ + (s[3] + k) % NZ)
        )

    shape = jax.ShapeDtypeStruct((NH, rows, block), jnp.float32)
    target = pl.BlockSpec((1, rows, block), lambda i, s: (i, 0, 0))
    return pl.pallas_call(
        kernel,
        out_shape=(shape,) * (NZ - 1),
        grid_spec=pltpu.PrefetchScalarGridSpec(
            num_scalar_prefetch=1,
            grid=(NH,),
            in_specs=[source(k) for k in range(1, NZ)],
            out_specs=(target,) * (NZ - 1),
        ),
        compiler_params=params(),
        cost_estimate=cost(0, 8 * (NZ - 1) * NH * rows * block),
    )(place, inner, inner, inner)


def sum_far(place, inner, received):
    rows, width = inner.shape
    block = width // (NZ * NH)

    def kernel(place_ref, own, a, b, c, out):
        out[...] = own[...] + a[0] + b[0] + c[0]

    code = pl.BlockSpec((1, rows, block), lambda i, s: (1, 0, 0))
    return pl.pallas_call(
        kernel,
        out_shape=jax.ShapeDtypeStruct((rows, block), jnp.float32),
        grid_spec=pltpu.PrefetchScalarGridSpec(
            num_scalar_prefetch=1,
            grid=(1,),
            in_specs=[pl.BlockSpec((rows, block), lambda i, s: (0, ((s[4] + 1) % NH) * NZ + s[3]))]
            + [code] * 3,
            out_specs=pl.BlockSpec((rows, block), lambda i, s: (0, 0)),
        ),
        compiler_params=params(),
        cost_estimate=cost(0, 20 * rows * block),
    )(place, inner, *received)


def outer_step(place, inner, received, far, outer_weight, outer_momentum):
    rows, width = inner.shape
    block = width // (NZ * NH)

    def kernel(place_ref, own, a, b, c, far_ref, weight, momentum, next_ref, momentum_ref, code_ref):
        summed = own[...] + a[0] + b[0] + c[0] + far_ref[...]
        average = weight[...] - summed / (NZ * NH)
        momentum_next = outer_decay * momentum[...] + average
        outer_next = weight[...] - outer_rate * (average + outer_decay * momentum_next)
        next_ref[...] = outer_next
        momentum_ref[...] = momentum_next
        code_ref[...] = coded_outer(outer_next)

    code = pl.BlockSpec((1, rows, block), lambda i, s: (0, 0, 0))
    whole = pl.BlockSpec((rows, block), lambda i, s: (0, 0))
    shape = jax.ShapeDtypeStruct((rows, block), jnp.float32)
    return pl.pallas_call(
        kernel,
        out_shape=(shape, shape, jax.ShapeDtypeStruct((rows, block), jnp.bfloat16)),
        grid_spec=pltpu.PrefetchScalarGridSpec(
            num_scalar_prefetch=1,
            grid=(1,),
            in_specs=[pl.BlockSpec((rows, block), lambda i, s: (0, s[4] * NZ + s[3]))]
            + [code] * 3
            + [whole] * 3,
            out_specs=(whole,) * 3,
        ),
        compiler_params=params(),
        cost_estimate=cost(0, 38 * rows * block),
    )(place, inner, *received, far, outer_weight, outer_momentum)


def blend(place, inner, gathered):
    rows, width = inner.shape
    block = width // (NZ * NH)

    def kernel(place_ref, inner_ref, *refs):
        out = refs[-1]
        j = pl.program_id(0)
        back = (place_ref[3] - j % NZ + NZ) % NZ
        side = (j // NZ + place_ref[4]) % NH
        for k in range(NZ):

            @pl.when(back == k)
            def _():
                outer = decoded_outer(refs[k][side])
                out[...] = mix_share * outer + (1.0 - mix_share) * inner_ref[...]

    whole = pl.BlockSpec((NH, rows, block), lambda j, s: (0, 0, 0))
    state = pl.BlockSpec((rows, block), lambda j, s: (0, j))
    return pl.pallas_call(
        kernel,
        out_shape=jax.ShapeDtypeStruct((rows, width), jnp.float32),
        grid_spec=pltpu.PrefetchScalarGridSpec(
            num_scalar_prefetch=1,
            grid=(NZ * NH,),
            in_specs=[state] + [whole] * NZ,
            out_specs=state,
        ),
        compiler_params=params(),
        cost_estimate=cost(0, 10 * rows * width),
    )(place, inner, *gathered)


def local(
    inner_weight, first_moment, second_moment, outer_weight, outer_momentum, activations, out_grads
):
    inner, first, second = inner_weight[0], first_moment[0], second_moment[0]
    inputs, cotangents = activations[0], out_grads[0]
    replica, member = lax.axis_index("replica"), lax.axis_index("fsdp")
    core, column, row = member % NC, member // NC % NX, member // (NC * NX)
    depth, side = replica % NZ, replica // NZ
    place = jnp.stack([row, column, core, depth, side]).astype(jnp.int32)

    rights = (cotangents, on_fsdp(cotangents, TWIN))
    far_own, far_send = prepare(place, inputs, (0, 1))
    far_left = (far_own, on_fsdp(far_send, TWIN))
    near_own, near_send = prepare(place, inputs, (1, 3))
    near_left = (near_own, on_fsdp(near_send, TWIN))

    blocks = scatter_blocks(place, inner)
    arrived = [on_replica(blocks[k - 1], AHEAD[k]) for k in range(1, NZ)]

    up_far = on_fsdp(product(far_left, rights, (0, 1, 2), (WA, 0)), UP)
    down_far = on_fsdp(product(far_left, rights, (0, 1, 2), (WA, 1)), DOWN)
    across_far = on_fsdp(narrow(far_left, rights, (1, 1, 1)), ACROSS)
    up_own = on_fsdp(product(near_left, rights, (0, 1, 2), (WA, 1)), UP)
    down_own = on_fsdp(product(near_left, rights, (2, 1, 2), (WA, 0)), DOWN)
    across_near = on_fsdp(narrow(near_left, rights, (1, 2, 2)), ACROSS)
    across_here = on_fsdp(narrow(near_left, rights, (5, 1, 1)), ACROSS)

    up_both = on_fsdp(product(near_left, rights, (0, 1, 2), (WA, 0), (up_far,)), UP)
    down_both = on_fsdp(product(near_left, rights, (2, 1, 2), (WA, 1), (down_far,)), DOWN)

    far_sum = on_replica(sum_far(place, inner, arrived), FAR)
    outer_next, momentum_next, code = outer_step(
        place, inner, arrived, far_sum, outer_weight, outer_momentum
    )
    pair = jnp.stack([code, on_replica(code, FAR)])
    gathered = [pair] + [on_replica(pair, AHEAD[k]) for k in range(1, NZ)]

    half_one, half_two = (B1, CA // B1), (B2, (CA + B1) // B2)
    up_first = on_fsdp(middle(far_left, rights, 0, half_one, (0,), across_far), UP)
    down_first = on_fsdp(middle(far_left, rights, 0, half_two, (0,), across_far), DOWN)
    up_second = on_fsdp(middle(near_left, rights, 0, half_two, (0,), across_near), UP)
    down_second = on_fsdp(middle(near_left, rights, 2, half_one, (1,), across_near), DOWN)

    turned = turn(near_left, rights, (up_both, down_own, up_own, down_both))
    across_turned = on_fsdp(turned, ACROSS)

    up_third = on_fsdp(
        middle(near_left, rights, 0, half_one, (0,), across_near, (up_first,)), UP
    )
    down_third = on_fsdp(
        middle(near_left, rights, 2, half_two, (1,), across_near, (down_first,)), DOWN
    )

    blended = blend(place, inner, gathered)
    states = (blended, first, second)
    here_one, here_two = across_here[0, :, :B1], across_here[0, :, B1:]
    outs = finish(
        near_left, rights, half_one,
        [(here_one, (0, 0)), (up_third, (0, 0)), (down_second, (0, 0))], states, None,
    )
    outs = finish(
        near_left, rights, half_two,
        [(here_two, (0, 0)), (up_second, (0, 0)), (down_third, (0, 0))], states, outs,
    )
    outs = finish(
        near_left, rights, (WA, 0),
        [(up_both, (0, 0)), (down_own, (0, 0)), (across_turned, (0, 0))], states, outs,
    )
    outs = finish(
        near_left, rights, (WA, 1),
        [(up_own, (0, 0)), (down_both, (0, 0)), (across_turned, (0, 1))], states, outs,
    )
    inner_next, first_next, second_next = outs
    return (inner_next[None], first_next[None], second_next[None], outer_next, momentum_next)


def solution(mesh):
    in_specs = (
        P("replica", "fsdp", None),
        P("replica", "fsdp", None),
        P("replica", "fsdp", None),
        P("fsdp", "replica"),
        P("fsdp", "replica"),
        P("replica", "fsdp", None),
        P("replica", "fsdp", None),
    )
    out_specs = (
        P("replica", "fsdp", None),
        P("replica", "fsdp", None),
        P("replica", "fsdp", None),
        P("fsdp", "replica"),
        P("fsdp", "replica"),
    )
    return jax.shard_map(local, mesh=mesh, in_specs=in_specs, out_specs=out_specs, check_vma=False)
```

time: 533 us -> 144 us (0.27)
  waiting for transfers between devices: 488 us -> 55.2 us
  Pallas kernels: 0 us -> 44.6 us
  starting transfers between devices: 0.12 us -> 40.1 us
  matrix products: 18.1 us -> 0 us
  between operations: 15.5 us -> 1.04 us
  other arithmetic: 11.5 us -> 0.03 us
    reduce_scatter x2 -> x0, waiting for transfers between devices: 444 us -> none  [the longest x1 361 us: local(): lax.psum_scatter(lax.dot_general(inputs, cotangents, (((0,), (0,)), ((),...]
    ppermute x0 -> x27, waiting for transfers between devices: none -> 55.2 us  [the longest x8 29.7 us: on_replica(): return lax.ppermute(value, 'replica', pairs)]
    pallas_call x0 -> x26, Pallas kernels: none -> 44.6 us  [the longest x4 16.5 us: finish(): pl.pallas_call(lambda *refs: kernel(*refs[:7 + n], *refs[-3:]), out_shape...]
    all_gather x1 -> x0, waiting for transfers between devices: 43.2 us -> none  [local(): full_outer = lax.all_gather(outer_next, 'replica', axis=1, tiled=True)]
    ppermute x0 -> x27, starting transfers between devices: none -> 40.1 us  [the longest x19 20.6 us: on_fsdp(): return lax.ppermute(value, 'fsdp', pairs)]
    dot_general x1 -> x0, matrix products: 18.1 us -> none  [local(): lax.dot_general(inputs, cotangents, (((0,), (0,)), ((), ())), preferred_e...]
    broadcast_in_dim x1 -> x0, other arithmetic: 9.65 us -> none  [local(): second_next[None]]
  transfers between devices with their start and end apart: 3 -> 27, of which waited for: 3 -> 12; matrix products, arithmetic and copies ran while one was open for 3% -> 0% of each run, Pallas kernels for 0% -> 25%
where the time goes in v1:
time: 144 us; the launch traced here: 143 us
  waiting for transfers between devices  55.2 us (38%)
  Pallas kernels  44.6 us (31%)
  starting transfers between devices  40.1 us (28%)
  local copies, waits for them, and re-layouts  1.82 us (1%)
    ppermute x8, waiting for transfers between devices, on_replica(): return lax.ppermute(value, 'replica', pairs)  29.7 us
    ppermute x19, waiting for transfers between devices, on_fsdp(): return lax.ppermute(value, 'fsdp', pairs)  25.5 us
    ppermute x19, starting transfers between devices, on_fsdp(): return lax.ppermute(value, 'fsdp', pairs)  20.6 us
    ppermute x8, starting transfers between devices, on_replica(): return lax.ppermute(value, 'replica', pairs)  19.5 us
    pallas_call x4, Pallas kernels, finish(): pl.pallas_call(lambda *refs: kernel(*refs[:7 + n], *refs[-3:]), out_shape...  16.5 us
    pallas_call x6, Pallas kernels, product(): pl.pallas_call(kernel, out_shape=jax.ShapeDtypeStruct((count, rows, width...  9.19 us
    pallas_call x2, Pallas kernels, prepare(): pl.pallas_call(kernel, out_shape=(shape, shape), grid_spec=pltpu.Prefetch...  4.28 us
    pallas_call x6, Pallas kernels, middle(): pl.pallas_call(kernel, out_shape=jax.ShapeDtypeStruct((rows, width), jnp....  3.03 us
  transfers between devices with their start and end apart: 27, of which 12 were waited for; matrix products, arithmetic and copies ran while one was open for 0% of the time, Pallas kernels for 25%

profile of v1, /device:TPU:0, one launch (start us, length us, event | category | flops | bytes accessed | tf_op | source)
XLA Modules:
  0.0 142.7 jit_solution(7731706964172955969)
XLA Ops:
  3.6 2.1 %collective-permute-start.10 = (f32[2,288,256]{2,1,0:T(8,128)S(1)}, f32[2,288,256]{2,1,0:T(8,128)S(1)}, u32[]{:S(2)}, u32[]{:S(2)}) collective-permute-start(f32[2,288,256]{2,1,0:T(8,128)S(1)} %get-tuple-element.31), channel_id=1, source_target_pairs={{0,16},{16,32},{32,48},{48,0},{64,80},{80,96},{96,112},{112,64},{1... | collective-permute-start | bytes 1769480 | tf_op jit(solution)/shard_map/ppermute | solution.py:54
  5.6 3.3 %shard_map.110 = (bf16[6,288,512]{2,1,0:T(8,128)(2,1)S(1)}, bf16[6,288,512]{2,1,0:T(8,128)(2,1)}) custom-call(s32[5]{0:T(128)S(1)} %stack.32.place_ref, bf16[512,4608]{1,0:T(8,128)(2,1)S(1)} %bitcast.53), custom_call_target="tpu_custom_call" | custom-call | bytes 7077888 | tf_op jit(solution)/shard_map/pallas_call | solution.py:110
  9.1 3.6 %collective-permute-start.11 = (f32[2,288,256]{2,1,0:T(8,128)S(1)}, f32[2,288,256]{2,1,0:T(8,128)S(1)}, u32[]{:S(2)}, u32[]{:S(2)}) collective-permute-start(f32[2,288,256]{2,1,0:T(8,128)S(1)} %get-tuple-element.32), channel_id=1, source_target_pairs={{0,32},{16,48},{32,0},{48,16},{64,96},{80,112},{96,64},{112,80},{1... | collective-permute-start | bytes 1769480 | tf_op jit(solution)/shard_map/ppermute | solution.py:54
  14.7 7.0 %collective-permute-done.10.a = f32[2,288,256]{2,1,0:T(8,128)S(1)} collective-permute-done((f32[2,288,256]{2,1,0:T(8,128)S(1)}, f32[2,288,256]{2,1,0:T(8,128)S(1)}, u32[]{:S(2)}, u32[]{:S(2)}) %collective-permute-start.10) | collective-permute-done | bytes 589856 | tf_op jit(solution)/shard_map/ppermute | solution.py:54
  21.7 13.8 %collective-permute-done.11.b = f32[2,288,256]{2,1,0:T(8,128)S(1)} collective-permute-done((f32[2,288,256]{2,1,0:T(8,128)S(1)}, f32[2,288,256]{2,1,0:T(8,128)S(1)}, u32[]{:S(2)}, u32[]{:S(2)}) %collective-permute-start.11) | collective-permute-done | bytes 589856 | tf_op jit(solution)/shard_map/ppermute | solution.py:54
  35.5 4.1 %collective-permute-done.12.c = f32[2,288,256]{2,1,0:T(8,128)S(1)} collective-permute-done((f32[2,288,256]{2,1,0:T(8,128)S(1)}, f32[2,288,256]{2,1,0:T(8,128)S(1)}, u32[]{:S(2)}, u32[]{:S(2)}) %collective-permute-start.12) | collective-permute-done | bytes 589856 | tf_op jit(solution)/shard_map/ppermute | solution.py:54
  40.2 3.1 %collective-permute-start.13 = (f32[288,256]{1,0:T(8,128)S(1)}, f32[288,256]{1,0:T(8,128)S(1)}, u32[]{:S(2)}, u32[]{:S(2)}) collective-permute-start(f32[288,256]{1,0:T(8,128)S(1)} %shard_map.120), channel_id=1, source_target_pairs={{0,64},{16,80},{32,96},{48,112},{64,0},{80,16},{96,32},{112,48},{1... | collective-permute-start | bytes 884744 | tf_op jit(solution)/shard_map/ppermute | solution.py:54
  51.4 3.0 %collective-permute-start.14 = (bf16[288,256]{1,0:T(8,128)(2,1)S(1)}, bf16[288,256]{1,0:T(8,128)(2,1)S(1)}, u32[]{:S(2)}, u32[]{:S(2)}) collective-permute-start(bf16[288,256]{1,0:T(8,128)(2,1)S(1)} %get-tuple-element.34), channel_id=1, source_target_pairs={{0,64},{16,80},{32,96},{48,112},{64,0},{80,16},{96,32},{112,48},{1... | collective-permute-start | bytes 442376 | tf_op jit(solution)/shard_map/ppermute | solution.py:54
  54.4 3.6 %collective-permute-done.14 = bf16[288,256]{1,0:T(8,128)(2,1)S(1)} collective-permute-done((bf16[288,256]{1,0:T(8,128)(2,1)S(1)}, bf16[288,256]{1,0:T(8,128)(2,1)S(1)}, u32[]{:S(2)}, u32[]{:S(2)}) %collective-permute-start.14) | collective-permute-done | bytes 147488 | tf_op jit(solution)/shard_map/ppermute | solution.py:54
  63.8 3.1 %collective-permute-start.8 = (bf16[2,288,640]{2,1,0:T(8,128)(2,1)S(1)}, bf16[2,288,640]{2,1,0:T(8,128)(2,1)S(1)}, u32[]{:S(2)}, u32[]{:S(2)}) collective-permute-start(bf16[2,288,640]{2,1,0:T(8,128)(2,1)S(1)} %shard_map.117), channel_id=1, source_target_pairs={{0,12},{1,13},{2,14},{3,15},{4,0},{5,1},{6,2},{7,3},{8,4},{9,5},{1... | collective-permute-start | bytes 2211848 | tf_op jit(solution)/shard_map/ppermute | solution.py:50
  72.5 2.9 %collective-permute-start.5 = (bf16[2,288,640]{2,1,0:T(8,128)(2,1)S(1)}, bf16[2,288,640]{2,1,0:T(8,128)(2,1)S(1)}, u32[]{:S(2)}, u32[]{:S(2)}) collective-permute-start(bf16[2,288,640]{2,1,0:T(8,128)(2,1)S(1)} %shard_map.114), channel_id=1, source_target_pairs={{0,12},{1,13},{2,14},{3,15},{4,0},{5,1},{6,2},{7,3},{8,4},{9,5},{1... | collective-permute-start | bytes 2211848 | tf_op jit(solution)/shard_map/ppermute | solution.py:50
  77.6 6.3 %collective-permute-done.8.rest_1_.refs_5_ = bf16[2,288,640]{2,1,0:T(8,128)(2,1)S(1)} collective-permute-done((bf16[2,288,640]{2,1,0:T(8,128)(2,1)S(1)}, bf16[2,288,640]{2,1,0:T(8,128)(2,1)S(1)}, u32[]{:S(2)}, u32[]{:S(2)}) %collective-permute-start.8) | collective-permute-done | bytes 737312 | tf_op jit(solution)/shard_map/ppermute | solution.py:50
  83.8 2.9 %collective-permute-start.16 = (bf16[2,288,256]{2,1,0:T(8,128)(2,1)S(1)}, bf16[2,288,256]{2,1,0:T(8,128)(2,1)S(1)}, u32[]{:S(2)}, u32[]{:S(2)}) collective-permute-start(bf16[2,288,256]{2,1,0:T(8,128)(2,1)S(1)} %pad_maximum_fusion.refs_0_), channel_id=1, source_target_pairs={{0,32},{16,48},{32,0},{48,16},{64,96},{80,112},{96,64},{112,80},{1... | collective-permute-start | bytes 884744 | tf_op jit(solution)/shard_map/ppermute | solution.py:54
  89.6 11.7 %collective-permute-done.7.rest_0_.refs_4_ = bf16[2,288,640]{2,1,0:T(8,128)(2,1)S(1)} collective-permute-done((bf16[2,288,640]{2,1,0:T(8,128)(2,1)S(1)}, bf16[2,288,640]{2,1,0:T(8,128)(2,1)S(1)}, u32[]{:S(2)}, u32[]{:S(2)}) %collective-permute-start.7) | collective-permute-done | bytes 737312 | tf_op jit(solution)/shard_map/ppermute | solution.py:50
  103.8 2.9 %shard_map.118 = bf16[288,1280]{1,0:T(8,128)(2,1)S(1)} custom-call(bf16[6,288,512]{2,1,0:T(8,128)(2,1)S(1)} %get-tuple-element.27.lo.refs_0_, bf16[6,288,512]{2,1,0:T(8,128)(2,1)S(1)} %collective-permute-done.lt.refs_1_, bf16[512,2048]{1,0:T(8,128)(2,1)S(1)} %bitcast.33, bf16[512,2048]{1,0:T(8,128)(2,1)S(1)} %collective-permute-done.1.rt.rt1.rt2.refs_3_, ...), custom_call_target="tpu_custom_call" | custom-call | flops 754974720 | bytes 6897664 | tf_op jit(solution)/shard_map/pallas_call | solution.py:234
  108.0 2.7 %shard_map.122.refs_7_ = f32[288,2048]{1,0:T(8,128)S(1)} custom-call(s32[5]{0:T(128)S(1)} %stack.32.place_ref, f32[288,2048]{1,0:T(8,128)S(1)} %bitcast.48, bf16[2,288,256]{2,1,0:T(8,128)(2,1)S(1)} %pad_maximum_fusion.refs_0_, bf16[2,288,256]{2,1,0:T(8,128)(2,1)S(1)} %collective-permute-done.15.refs_1_, ...), custom_call_target="tpu_custom_call" | custom-call | bytes 5898240 | tf_op jit(solution)/shard_map/pallas_call | solution.py:403
  113.0 2.2 %collective-permute-start.23 = (bf16[288,512]{1,0:T(8,128)(2,1)S(1)}, bf16[288,512]{1,0:T(8,128)(2,1)S(1)}, u32[]{:S(2)}, u32[]{:S(2)}) collective-permute-start(bf16[288,512]{1,0:T(8,128)(2,1)S(1)} %shard_map.128), channel_id=1, source_target_pairs={{0,12},{1,13},{2,14},{3,15},{4,0},{5,1},{6,2},{7,3},{8,4},{9,5},{1... | collective-permute-start | bytes 884744 | tf_op jit(solution)/shard_map/ppermute | solution.py:50
  116.0 3.1 %collective-permute-done.24.rest_0_ = bf16[288,256]{1,0:T(8,128)(2,1)S(1)} collective-permute-done((bf16[288,256]{1,0:T(8,128)(2,1)S(1)}, bf16[288,256]{1,0:T(8,128)(2,1)S(1)}, u32[]{:S(2)}, u32[]{:S(2)}) %collective-permute-start.24) | collective-permute-done | bytes 147488 | tf_op jit(solution)/shard_map/ppermute | solution.py:50
  120.0 3.5 %collective-permute-start.26 = (bf16[288,256]{1,0:T(8,128)(2,1)S(1)}, bf16[288,256]{1,0:T(8,128)(2,1)S(1)}, u32[]{:S(2)}, u32[]{:S(2)}) collective-permute-start(bf16[288,256]{1,0:T(8,128)(2,1)S(1)} %shard_map.131), channel_id=1, source_target_pairs={{0,12},{1,13},{2,14},{3,15},{4,0},{5,1},{6,2},{7,3},{8,4},{9,5},{1... | collective-permute-start | bytes 442376 | tf_op jit(solution)/shard_map/ppermute | solution.py:50
  123.5 2.5 %collective-permute-done.25.refs_5_ = bf16[288,256]{1,0:T(8,128)(2,1)S(1)} collective-permute-done((bf16[288,256]{1,0:T(8,128)(2,1)S(1)}, bf16[288,256]{1,0:T(8,128)(2,1)S(1)}, u32[]{:S(2)}, u32[]{:S(2)}) %collective-permute-start.25) | collective-permute-done | bytes 147488 | tf_op jit(solution)/shard_map/ppermute | solution.py:50
  126.2 3.2 %shard_map.132 = (f32[288,2048]{1,0:T(8,128)}, f32[288,2048]{1,0:T(8,128)}, f32[288,2048]{1,0:T(8,128)}) custom-call(bf16[6,288,512]{2,1,0:T(8,128)(2,1)S(1)} %get-tuple-element.27.lo.refs_0_, bf16[6,288,512]{2,1,0:T(8,128)(2,1)S(1)} %collective-permute-done.lt.refs_1_, bf16[512,2048]{1,0:T(8,128)(2,1)S(1)} %bitcast.39, ...), custom_call_target="tpu_custom_call" | custom-call | flops 150994944 | bytes 3473408 | tf_op jit(solution)/shard_map/pallas_call | solution.py:286
  129.4 4.0 %shard_map.133 = (f32[288,2048]{1,0:T(8,128)}, f32[288,2048]{1,0:T(8,128)}, f32[288,2048]{1,0:T(8,128)}) custom-call(bf16[6,288,512]{2,1,0:T(8,128)(2,1)S(1)} %get-tuple-element.27.lo.refs_0_, bf16[6,288,512]{2,1,0:T(8,128)(2,1)S(1)} %collective-permute-done.lt.refs_1_, ...), custom_call_target="tpu_custom_call", output_to_operand_aliasing={{0}: (10, {}), {1}: (11, {}), {2}: (12, {})} | custom-call | flops 301989888 | bytes 6356992 | tf_op jit(solution)/shard_map/pallas_call | solution.py:286
  133.4 4.6 %shard_map.134 = (f32[288,2048]{1,0:T(8,128)}, f32[288,2048]{1,0:T(8,128)}, f32[288,2048]{1,0:T(8,128)}) custom-call(bf16[6,288,512]{2,1,0:T(8,128)(2,1)S(1)} %get-tuple-element.27.lo.refs_0_, bf16[6,288,512]{2,1,0:T(8,128)(2,1)S(1)} %collective-permute-done.lt.refs_1_, ...), custom_call_target="tpu_custom_call", output_to_operand_aliasing={{0}: (10, {}), {1}: (11, {}), {2}: (12, {})} | custom-call | flops 377487360 | bytes 7798784 | tf_op jit(solution)/shard_map/pallas_call | solution.py:286
  138.1 4.6 %shard_map.135 = (f32[288,2048]{1,0:T(8,128)}, f32[288,2048]{1,0:T(8,128)}, f32[288,2048]{1,0:T(8,128)}) custom-call(bf16[6,288,512]{2,1,0:T(8,128)(2,1)S(1)} %get-tuple-element.27.lo.refs_0_, bf16[6,288,512]{2,1,0:T(8,128)(2,1)S(1)} %collective-permute-done.lt.refs_1_, ...), custom_call_target="tpu_custom_call", output_to_operand_aliasing={{0}: (10, {}), {1}: (11, {}), {2}: (12, {})} | custom-call | flops 377487360 | bytes 7798784 | tf_op jit(solution)/shard_map/pallas_call | solution.py:286
  (78 shorter events, 37.7 us)
Async XLA Ops:
  0.6 42.6 %collective-permute-start.1 = (bf16[512,2048]{1,0:T(8,128)(2,1)}, bf16[512,2048]{1,0:T(8,128)(2,1)S(1)}, u32[]{:S(2)}, u32[]{:S(2)}) collective-permute-start(bf16[512,2048]{1,0:T(8,128)(2,1)} %bitcast.19), channel_id=1, source_target_pairs={{0,1},{1,0},{2,3},{3,2},{4,5},{5,4},{6,7},{7,6},{8,9},{9,8},{10,11... | collective-permute-start | bytes 6291464 | tf_op jit(solution)/shard_map/ppermute | solution.py:50
  3.6 18.1 %collective-permute-start.10 = (f32[2,288,256]{2,1,0:T(8,128)S(1)}, f32[2,288,256]{2,1,0:T(8,128)S(1)}, u32[]{:S(2)}, u32[]{:S(2)}) collective-permute-start(f32[2,288,256]{2,1,0:T(8,128)S(1)} %get-tuple-element.31), channel_id=1, source_target_pairs={{0,16},{16,32},{32,48},{48,0},{64,80},{80,96},{96,112},{112,64},{1... | collective-permute-start | bytes 1769480 | tf_op jit(solution)/shard_map/ppermute | solution.py:54
  8.9 53.4 %collective-permute-start = (bf16[6,288,512]{2,1,0:T(8,128)(2,1)}, bf16[6,288,512]{2,1,0:T(8,128)(2,1)S(1)}, u32[]{:S(2)}, u32[]{:S(2)}) collective-permute-start(bf16[6,288,512]{2,1,0:T(8,128)(2,1)} %get-tuple-element.28), channel_id=1, source_target_pairs={{0,1},{1,0},{2,3},{3,2},{4,5},{5,4},{6,7},{7,6},{8,9},{9,8},{10,11... | collective-permute-start | bytes 5308424 | tf_op jit(solution)/shard_map/ppermute | solution.py:50
  9.1 26.4 %collective-permute-start.11 = (f32[2,288,256]{2,1,0:T(8,128)S(1)}, f32[2,288,256]{2,1,0:T(8,128)S(1)}, u32[]{:S(2)}, u32[]{:S(2)}) collective-permute-start(f32[2,288,256]{2,1,0:T(8,128)S(1)} %get-tuple-element.32), channel_id=1, source_target_pairs={{0,32},{16,48},{32,0},{48,16},{64,96},{80,112},{96,64},{112,80},{1... | collective-permute-start | bytes 1769480 | tf_op jit(solution)/shard_map/ppermute | solution.py:54
  12.7 26.9 %collective-permute-start.12 = (f32[2,288,256]{2,1,0:T(8,128)S(1)}, f32[2,288,256]{2,1,0:T(8,128)S(1)}, u32[]{:S(2)}, u32[]{:S(2)}) collective-permute-start(f32[2,288,256]{2,1,0:T(8,128)S(1)} %get-tuple-element.33), channel_id=1, source_target_pairs={{0,48},{16,0},{32,16},{48,32},{64,112},{80,64},{96,80},{112,96},{1... | collective-permute-start | bytes 1769480 | tf_op jit(solution)/shard_map/ppermute | solution.py:54
  21.7 21.6 %collective-permute-start.3 = (bf16[2,288,512]{2,1,0:T(8,128)(2,1)S(1)}, bf16[2,288,512]{2,1,0:T(8,128)(2,1)S(1)}, u32[]{:S(2)}, u32[]{:S(2)}) collective-permute-start(bf16[2,288,512]{2,1,0:T(8,128)(2,1)S(1)} %get-tuple-element.30), channel_id=1, source_target_pairs={{0,1},{1,0},{2,3},{3,2},{4,5},{5,4},{6,7},{7,6},{8,9},{9,8},{10,11... | collective-permute-start | bytes 1769480 | tf_op jit(solution)/shard_map/ppermute | solution.py:50
  40.2 9.7 %collective-permute-start.13 = (f32[288,256]{1,0:T(8,128)S(1)}, f32[288,256]{1,0:T(8,128)S(1)}, u32[]{:S(2)}, u32[]{:S(2)}) collective-permute-start(f32[288,256]{1,0:T(8,128)S(1)} %shard_map.120), channel_id=1, source_target_pairs={{0,64},{16,80},{32,96},{48,112},{64,0},{80,16},{96,32},{112,48},{1... | collective-permute-start | bytes 884744 | tf_op jit(solution)/shard_map/ppermute | solution.py:54
  44.8 23.6 %collective-permute-start.6 = (bf16[2,288,640]{2,1,0:T(8,128)(2,1)S(1)}, bf16[2,288,640]{2,1,0:T(8,128)(2,1)S(1)}, u32[]{:S(2)}, u32[]{:S(2)}) collective-permute-start(bf16[2,288,640]{2,1,0:T(8,128)(2,1)S(1)} %shard_map.115), channel_id=1, source_target_pairs={{0,4},{1,5},{2,6},{3,7},{4,8},{5,9},{6,10},{7,11},{8,12},{9,13},{1... | collective-permute-start | bytes 2211848 | tf_op jit(solution)/shard_map/ppermute | solution.py:50
  47.9 22.3 %collective-permute-start.4 = (bf16[2,288,640]{2,1,0:T(8,128)(2,1)S(1)}, bf16[2,288,640]{2,1,0:T(8,128)(2,1)S(1)}, u32[]{:S(2)}, u32[]{:S(2)}) collective-permute-start(bf16[2,288,640]{2,1,0:T(8,128)(2,1)S(1)} %shard_map.113), channel_id=1, source_target_pairs={{0,12},{1,13},{2,14},{3,15},{4,0},{5,1},{6,2},{7,3},{8,4},{9,5},{1... | collective-permute-start | bytes 2211848 | tf_op jit(solution)/shard_map/ppermute | solution.py:50
  58.1 14.4 %collective-permute-start.15 = (bf16[2,288,256]{2,1,0:T(8,128)(2,1)S(1)}, bf16[2,288,256]{2,1,0:T(8,128)(2,1)S(1)}, u32[]{:S(2)}, u32[]{:S(2)}) collective-permute-start(bf16[2,288,256]{2,1,0:T(8,128)(2,1)S(1)} %pad_maximum_fusion.refs_0_), channel_id=1, source_target_pairs={{0,16},{16,32},{32,48},{48,0},{64,80},{80,96},{96,112},{112,64},{1... | collective-permute-start | bytes 884744 | tf_op jit(solution)/shard_map/ppermute | solution.py:54
  60.8 16.1 %collective-permute-start.21 = (bf16[1,288,768]{2,1,0:T(8,128)(2,1)S(1)}, bf16[1,288,768]{2,1,0:T(8,128)(2,1)S(1)}, u32[]{:S(2)}, u32[]{:S(2)}) collective-permute-start(bf16[1,288,768]{2,1,0:T(8,128)(2,1)S(1)} %shard_map.126), channel_id=1, source_target_pairs={{0,2},{1,3},{2,0},{3,1},{4,6},{5,7},{6,4},{7,5},{8,10},{9,11},{10,... | collective-permute-start | bytes 1327112 | tf_op jit(solution)/shard_map/ppermute | solution.py:50
  63.8 20.0 %collective-permute-start.8 = (bf16[2,288,640]{2,1,0:T(8,128)(2,1)S(1)}, bf16[2,288,640]{2,1,0:T(8,128)(2,1)S(1)}, u32[]{:S(2)}, u32[]{:S(2)}) collective-permute-start(bf16[2,288,640]{2,1,0:T(8,128)(2,1)S(1)} %shard_map.117), channel_id=1, source_target_pairs={{0,12},{1,13},{2,14},{3,15},{4,0},{5,1},{6,2},{7,3},{8,4},{9,5},{1... | collective-permute-start | bytes 2211848 | tf_op jit(solution)/shard_map/ppermute | solution.py:50
  68.3 20.7 %collective-permute-start.2 = (bf16[2,288,640]{2,1,0:T(8,128)(2,1)S(1)}, bf16[2,288,640]{2,1,0:T(8,128)(2,1)S(1)}, u32[]{:S(2)}, u32[]{:S(2)}) collective-permute-start(bf16[2,288,640]{2,1,0:T(8,128)(2,1)S(1)} %shard_map.111), channel_id=1, source_target_pairs={{0,4},{1,5},{2,6},{3,7},{4,8},{5,9},{6,10},{7,11},{8,12},{9,13},{1... | collective-permute-start | bytes 2211848 | tf_op jit(solution)/shard_map/ppermute | solution.py:50
  70.2 31.1 %collective-permute-start.7 = (bf16[2,288,640]{2,1,0:T(8,128)(2,1)S(1)}, bf16[2,288,640]{2,1,0:T(8,128)(2,1)S(1)}, u32[]{:S(2)}, u32[]{:S(2)}) collective-permute-start(bf16[2,288,640]{2,1,0:T(8,128)(2,1)S(1)} %shard_map.116), channel_id=1, source_target_pairs={{0,4},{1,5},{2,6},{3,7},{4,8},{5,9},{6,10},{7,11},{8,12},{9,13},{1... | collective-permute-start | bytes 2211848 | tf_op jit(solution)/shard_map/ppermute | solution.py:50
  72.5 31.2 %collective-permute-start.5 = (bf16[2,288,640]{2,1,0:T(8,128)(2,1)S(1)}, bf16[2,288,640]{2,1,0:T(8,128)(2,1)S(1)}, u32[]{:S(2)}, u32[]{:S(2)}) collective-permute-start(bf16[2,288,640]{2,1,0:T(8,128)(2,1)S(1)} %shard_map.114), channel_id=1, source_target_pairs={{0,12},{1,13},{2,14},{3,15},{4,0},{5,1},{6,2},{7,3},{8,4},{9,5},{1... | collective-permute-start | bytes 2211848 | tf_op jit(solution)/shard_map/ppermute | solution.py:50
  76.9 35.3 %collective-permute-start.19 = (bf16[2,288,768]{2,1,0:T(8,128)(2,1)S(1)}, bf16[2,288,768]{2,1,0:T(8,128)(2,1)S(1)}, u32[]{:S(2)}, u32[]{:S(2)}) collective-permute-start(bf16[2,288,768]{2,1,0:T(8,128)(2,1)S(1)} %shard_map.124), channel_id=1, source_target_pairs={{0,2},{1,3},{2,0},{3,1},{4,6},{5,7},{6,4},{7,5},{8,10},{9,11},{10,... | collective-permute-start | bytes 2654216 | tf_op jit(solution)/shard_map/ppermute | solution.py:50
  83.8 22.9 %collective-permute-start.16 = (bf16[2,288,256]{2,1,0:T(8,128)(2,1)S(1)}, bf16[2,288,256]{2,1,0:T(8,128)(2,1)S(1)}, u32[]{:S(2)}, u32[]{:S(2)}) collective-permute-start(bf16[2,288,256]{2,1,0:T(8,128)(2,1)S(1)} %pad_maximum_fusion.refs_0_), channel_id=1, source_target_pairs={{0,32},{16,48},{32,0},{48,16},{64,96},{80,112},{96,64},{112,80},{1... | collective-permute-start | bytes 884744 | tf_op jit(solution)/shard_map/ppermute | solution.py:54
  89.0 26.9 %collective-permute-start.18 = (bf16[1,288,768]{2,1,0:T(8,128)(2,1)S(1)}, bf16[1,288,768]{2,1,0:T(8,128)(2,1)S(1)}, u32[]{:S(2)}, u32[]{:S(2)}) collective-permute-start(bf16[1,288,768]{2,1,0:T(8,128)(2,1)S(1)} %shard_map.123), channel_id=1, source_target_pairs={{0,2},{1,3},{2,0},{3,1},{4,6},{5,7},{6,4},{7,5},{8,10},{9,11},{10,... | collective-permute-start | bytes 1327112 | tf_op jit(solution)/shard_map/ppermute | solution.py:50
  101.3 6.7 %collective-permute-start.17 = (bf16[2,288,256]{2,1,0:T(8,128)(2,1)S(1)}, bf16[2,288,256]{2,1,0:T(8,128)(2,1)S(1)}, u32[]{:S(2)}, u32[]{:S(2)}) collective-permute-start(bf16[2,288,256]{2,1,0:T(8,128)(2,1)S(1)} %pad_maximum_fusion.refs_0_), channel_id=1, source_target_pairs={{0,48},{16,0},{32,16},{48,32},{64,112},{80,64},{96,80},{112,96},{1... | collective-permute-start | bytes 884744 | tf_op jit(solution)/shard_map/ppermute | solution.py:54
  103.7 8.6 %collective-permute-start.22 = (bf16[288,512]{1,0:T(8,128)(2,1)S(1)}, bf16[288,512]{1,0:T(8,128)(2,1)S(1)}, u32[]{:S(2)}, u32[]{:S(2)}) collective-permute-start(bf16[288,512]{1,0:T(8,128)(2,1)S(1)} %shard_map.127), channel_id=1, source_target_pairs={{0,12},{1,13},{2,14},{3,15},{4,0},{5,1},{6,2},{7,3},{8,4},{9,5},{1... | collective-permute-start | bytes 884744 | tf_op jit(solution)/shard_map/ppermute | solution.py:50
  106.7 26.7 %collective-permute-start.9 = (bf16[288,1280]{1,0:T(8,128)(2,1)S(1)}, bf16[288,1280]{1,0:T(8,128)(2,1)S(1)}, u32[]{:S(2)}, u32[]{:S(2)}) collective-permute-start(bf16[288,1280]{1,0:T(8,128)(2,1)S(1)} %shard_map.118), channel_id=1, source_target_pairs={{0,2},{1,3},{2,0},{3,1},{4,6},{5,7},{6,4},{7,5},{8,10},{9,11},{10,... | collective-permute-start | bytes 2211848 | tf_op jit(solution)/shard_map/ppermute | solution.py:50
  111.1 8.0 %collective-permute-start.24 = (bf16[288,256]{1,0:T(8,128)(2,1)S(1)}, bf16[288,256]{1,0:T(8,128)(2,1)S(1)}, u32[]{:S(2)}, u32[]{:S(2)}) collective-permute-start(bf16[288,256]{1,0:T(8,128)(2,1)S(1)} %shard_map.129), channel_id=1, source_target_pairs={{0,4},{1,5},{2,6},{3,7},{4,8},{5,9},{6,10},{7,11},{8,12},{9,13},{1... | collective-permute-start | bytes 442376 | tf_op jit(solution)/shard_map/ppermute | solution.py:50
  113.0 16.4 %collective-permute-start.23 = (bf16[288,512]{1,0:T(8,128)(2,1)S(1)}, bf16[288,512]{1,0:T(8,128)(2,1)S(1)}, u32[]{:S(2)}, u32[]{:S(2)}) collective-permute-start(bf16[288,512]{1,0:T(8,128)(2,1)S(1)} %shard_map.128), channel_id=1, source_target_pairs={{0,12},{1,13},{2,14},{3,15},{4,0},{5,1},{6,2},{7,3},{8,4},{9,5},{1... | collective-permute-start | bytes 884744 | tf_op jit(solution)/shard_map/ppermute | solution.py:50
  115.9 13.5 %collective-permute-start.20 = (bf16[288,512]{1,0:T(8,128)(2,1)S(1)}, bf16[288,512]{1,0:T(8,128)(2,1)S(1)}, u32[]{:S(2)}, u32[]{:S(2)}) collective-permute-start(bf16[288,512]{1,0:T(8,128)(2,1)S(1)} %shard_map.125), channel_id=1, source_target_pairs={{0,4},{1,5},{2,6},{3,7},{4,8},{5,9},{6,10},{7,11},{8,12},{9,13},{1... | collective-permute-start | bytes 884744 | tf_op jit(solution)/shard_map/ppermute | solution.py:50
  (12 other events, 103.0 us)

commit v2 on v0

v2 whole, which is shorter than its diff:
```python
import jax
import jax.numpy as jnp
from jax import lax
from jax.experimental import pallas as pl
from jax.experimental.pallas import tpu as pltpu
from jax.sharding import PartitionSpec as P

outer_rate = 0.7
outer_decay = 0.9
mix_share = 0.5
beta_one = 0.9
beta_two = 0.95
inner_rate = 0.05
weight_decay = 0.1
epsilon = 1e-08
step_count = 200.0
corr_one = 1.0 - beta_one**step_count
corr_two = 1.0 - beta_two**step_count

NY, NX, NC, NZ, NH = 4, 2, 2, 4, 2
BLOCK = 256
A1, A2, B1, B2 = (0, 3), (3, 3), (6, 1), (7, 1)
A, B, ALL = (0, 6), (6, 2), (0, 8)
VMEM = 16 * 2**20


def along_fsdp(move):
    where = [(y, x, c) for y in range(NY) for x in range(NX) for c in range(NC)]
    number = lambda y, x, c: ((y % NY) * NX + x) * NC + c
    return [(number(*place), number(*move(*place))) for place in where]


def along_replica(move):
    where = [(h, z) for h in range(NH) for z in range(NZ)]
    number = lambda h, z: h * NZ + z % NZ
    return [(number(*place), number(*move(*place))) for place in where]


UP = along_fsdp(lambda y, x, c: (y + 1, x, c))
DOWN = along_fsdp(lambda y, x, c: (y - 1, x, c))
ACROSS = along_fsdp(lambda y, x, c: (y, 1 - x, c))
TWIN = along_fsdp(lambda y, x, c: (y, x, 1 - c))
FAR = along_replica(lambda h, z: (1 - h, z))
AHEAD = [along_replica(lambda h, z, k=k: (h, z + k)) for k in range(NZ)]


def on_fsdp(value, pairs):
    return lax.ppermute(value, "fsdp", pairs)


def on_replica(value, pairs):
    return lax.ppermute(value, "replica", pairs)


def coded(value):
    return (value * jnp.abs(value) * (value * value)).astype(jnp.bfloat16)


def decoded(code):
    code = code.astype(jnp.float32)
    root = lax.rsqrt(lax.rsqrt(jnp.abs(code)))
    return jnp.where(code < 0.0, -root, root)


def coded_outer(value):
    value = value * 4096.0
    square = value * value
    fourth = square * square
    return (value * jnp.abs(value) * square * fourth).astype(jnp.bfloat16)


def decoded_outer(code):
    code = code.astype(jnp.float32)
    root = jnp.sqrt(lax.rsqrt(lax.rsqrt(jnp.abs(code)))) * (1.0 / 4096.0)
    return jnp.where(code < 0.0, -root, root)


def run(kernel, grid, ins, outs, after=(), prefetch=(), scratch=(), aliases=None):
    read, late = len(prefetch) + len(ins), len(after)

    def body(*refs):
        kernel(*refs[:read], *refs[read + late :])

    arrays = [array for array, _ in ins]
    shapes = tuple(shape for shape, _ in outs)
    result = pl.pallas_call(
        body,
        out_shape=shapes,
        grid_spec=pltpu.PrefetchScalarGridSpec(
            num_scalar_prefetch=len(prefetch),
            grid=grid,
            in_specs=[spec for _, spec in ins] + [pl.BlockSpec(memory_space=pl.ANY)] * late,
            out_specs=tuple(spec for _, spec in outs),
            scratch_shapes=list(scratch),
        ),
        input_output_aliases=aliases or {},
        compiler_params=pltpu.CompilerParams(vmem_limit_bytes=VMEM),
        cost_estimate=pl.CostEstimate(flops=1, bytes_accessed=1, transcendentals=0),
    )(*prefetch, *arrays, *after)
    return result[0] if len(outs) == 1 else result


def prepare(place, activations, first, count, after=()):
    tokens, width = activations.shape
    quarter = width // NY
    rows = quarter // (NX * NC)

    def distance(i):
        step = first + i
        return jnp.where(step == 0, 2, jnp.where(step == 1, 1, jnp.where(step == 2, 3, 0)))

    def kernel(place_ref, a_ref, own_ref, send_ref, turned):
        turned[...] = a_ref[...].T
        x, core = place_ref[1], place_ref[2]
        for dx in range(NX):
            column = (x + dx) % NX
            own = pl.multiple_of((column * NC + core) * rows, 16)
            other = pl.multiple_of((column * NC + 1 - core) * rows, 16)
            own_ref[dx, 0] = turned[pl.ds(own, rows), :]
            send_ref[dx, 0] = turned[pl.ds(other, rows), :]

    out = (
        jax.ShapeDtypeStruct((NX, count, rows, tokens), jnp.bfloat16),
        pl.BlockSpec((NX, 1, rows, tokens), lambda i, s: (0, i, 0, 0)),
    )
    source = pl.BlockSpec((tokens, quarter), lambda i, s: (0, (s[0] + distance(i)) % NY))
    own, send = run(
        kernel, (count,), [(activations, source)], [out, out], after, (place,),
        [pltpu.VMEM((quarter, tokens), jnp.bfloat16)],
    )
    return own.reshape(NX * count, rows, tokens), send.reshape(NX * count, rows, tokens)


def run_whole(kernel, arrays, shape, after=()):
    count = len(arrays)
    vmem = pl.BlockSpec(memory_space=pltpu.VMEM)

    def body(*refs):
        kernel(*refs[:count], refs[-1])

    return pl.pallas_call(
        body,
        out_shape=shape,
        in_specs=[vmem] * count + [pl.BlockSpec(memory_space=pl.ANY)] * len(after),
        out_specs=vmem,
        compiler_params=pltpu.CompilerParams(vmem_limit_bytes=VMEM),
    )(*arrays, *after)


def block_columns(j):
    start = j * BLOCK
    return pl.ds(start if isinstance(start, int) else pl.multiple_of(start, BLOCK), BLOCK)


def dots(lefts, rights, blocks, j):
    start, count = blocks
    total = None
    for left, right in zip(lefts, rights):
        rows, depth = left.shape[1:]
        part = left[start : start + count].reshape(count * rows, depth)
        part = jnp.dot(part, right[:, block_columns(j)], preferred_element_type=jnp.float32)
        total = part if total is None else total + part
    return total.reshape(count, rows, BLOCK)


def regions(number, received):
    cuts = {0, number}
    for _, _, span, _ in received:
        cuts |= {span[0], span[0] + span[1]}
    cuts = sorted(cuts)
    found = []
    for low, high in zip(cuts, cuts[1:]):
        which = [i for i, (_, _, span, _) in enumerate(received) if span[0] <= low < span[0] + span[1]]
        found.append((low, high, which))
    return found


def product(lefts, rights, blocks, columns, received=(), after=(), kind=jnp.bfloat16):
    first, number = columns
    count, rows = blocks[1], lefts[0].shape[1]

    def kernel(lo, lt, ro, rt, *rest):
        out = rest[-1]

        def step(j, which):
            total = dots((lo, lt), (ro, rt), blocks, first + j)
            for i in which:
                _, block, span, offset = received[i]
                total = total + decoded(rest[i][block : block + count, :, block_columns(offset + j - span[0])])
            out[:, :, block_columns(j)] = coded(total) if kind == jnp.bfloat16 else total

        for low, high, which in regions(number, received):
            pl.loop(low, high)(lambda j, which=which: step(j, which))

    shape = jax.ShapeDtypeStruct((count, rows, number * BLOCK), kind)
    return run_whole(kernel, [*lefts, *rights, *(array for array, *_ in received)], shape, after)


def product_pair(lefts, rights, block, columns, lefts_last, block_last, column_last, codes, after=()):
    first, number = columns
    rows = lefts[0].shape[1]

    def kernel(lo, lt, lo2, lt2, ro, rt, code, out):
        @pl.loop(0, number)
        def _(j):
            out[:, :, block_columns(j)] = coded(dots((lo, lt), (ro, rt), (block, 1), first + j))

        total = dots((lo2, lt2), (ro, rt), (block_last, 1), column_last)
        total = total + decoded(code[:, :, block_columns(column_last - B[0])])
        out[:, :, block_columns(number)] = coded(total)

    shape = jax.ShapeDtypeStruct((1, rows, (number + 1) * BLOCK), jnp.bfloat16)
    return run_whole(kernel, [*lefts, *lefts_last, *rights, codes], shape, after)


def finish(base, down, across, states, after=()):
    rows, width = states[0].shape
    wide = 2 * BLOCK

    def kernel(base_ref, down_ref, across_ref, blended_ref, first_ref, second_ref, inner_out, first_out, second_out):
        def store(total):
            first_next = beta_one * first_ref[...] + (1.0 - beta_one) * total
            second_next = beta_two * second_ref[...] + (1.0 - beta_two) * total * total
            scaled = second_next * (1.0 / corr_two)
            update = first_next * (1.0 / corr_one) / (scaled * lax.rsqrt(scaled) + epsilon)
            blended = blended_ref[...]
            inner_out[...] = blended - inner_rate * (update + weight_decay * blended)
            first_out[...] = first_next
            second_out[...] = second_next

        step = pl.program_id(0)

        @pl.when(step < A[1] // 2)
        def _():
            store(base_ref[0] + decoded(down_ref[0]) + decoded(across_ref[0]))

        @pl.when(step >= A[1] // 2)
        def _():
            store(base_ref[0] + decoded(down_ref[0]))

    whole = pl.BlockSpec((1, rows, wide), lambda j: (0, 0, j))
    part = pl.BlockSpec((1, rows, wide), lambda j: (0, 0, jnp.minimum(j, A[1] // 2 - 1)))
    state = pl.BlockSpec((rows, wide), lambda j: (0, j))
    out = (jax.ShapeDtypeStruct((rows, width), jnp.float32), state)
    ins = [(base, whole), (down, whole), (across, part)] + [(array, state) for array in states]
    return run(kernel, (width // wide,), ins, [out] * 3, after)


def scatter_blocks(place, inner, places, after=()):
    rows = inner.shape[0]
    n = len(places)

    def kernel(place_ref, *refs):
        for source, target in zip(refs[:n], refs[n:]):
            target[0] = source[...]

    ins = []
    for k in places:
        def source(i, s, k=k):
            return (0, ((s[4] + i) % NH) * NZ + (s[3] + k) % NZ)

        ins.append((inner, pl.BlockSpec((rows, BLOCK), source)))
    out = (
        jax.ShapeDtypeStruct((NH, rows, BLOCK), jnp.float32),
        pl.BlockSpec((1, rows, BLOCK), lambda i, s: (i, 0, 0)),
    )
    return run(kernel, (NH,), ins, [out] * n, after, (place,))


def sum_far(place, inner, arrived, after=()):
    rows = inner.shape[0]

    def kernel(place_ref, own, a, b, c, out):
        out[...] = own[...] + a[0] + b[0] + c[0]

    part = pl.BlockSpec((1, rows, BLOCK), lambda i, s: (1, 0, 0))
    own = pl.BlockSpec((rows, BLOCK), lambda i, s: (0, ((s[4] + 1) % NH) * NZ + s[3]))
    out = (jax.ShapeDtypeStruct((rows, BLOCK), jnp.float32), pl.BlockSpec((rows, BLOCK), lambda i, s: (0, 0)))
    return run(kernel, (1,), [(inner, own)] + [(a, part) for a in arrived], [out], after, (place,))


def outer_step(place, inner, arrived, far, outer_weight, outer_momentum, after=()):
    rows = inner.shape[0]

    def kernel(place_ref, own, a, b, c, far_ref, weight, momentum, next_ref, momentum_ref, code_ref):
        summed = own[...] + a[0] + b[0] + c[0] + far_ref[...]
        average = weight[...] - summed / (NZ * NH)
        momentum_next = outer_decay * momentum[...] + average
        outer_next = weight[...] - outer_rate * (average + outer_decay * momentum_next)
        next_ref[...] = outer_next
        momentum_ref[...] = momentum_next
        code_ref[...] = coded_outer(outer_next)

    part = pl.BlockSpec((1, rows, BLOCK), lambda i, s: (0, 0, 0))
    own = pl.BlockSpec((rows, BLOCK), lambda i, s: (0, s[4] * NZ + s[3]))
    whole = pl.BlockSpec((rows, BLOCK), lambda i, s: (0, 0))
    shape = jax.ShapeDtypeStruct((rows, BLOCK), jnp.float32)
    return run(
        kernel,
        (1,),
        [(inner, own)] + [(a, part) for a in arrived]
        + [(array, whole) for array in (far, outer_weight, outer_momentum)],
        [(shape, whole), (shape, whole), (jax.ShapeDtypeStruct((rows, BLOCK), jnp.bfloat16), whole)],
        after,
        (place,),
    )


def paired(near, far, after=()):
    rows = near.shape[0]

    def kernel(a, b, out):
        out[0] = a[...]
        out[1] = b[...]

    whole = pl.BlockSpec((rows, BLOCK), lambda i: (0, 0))
    out = (
        jax.ShapeDtypeStruct((NH, rows, BLOCK), near.dtype),
        pl.BlockSpec((NH, rows, BLOCK), lambda i: (0, 0, 0)),
    )
    return run(kernel, (1,), [(near, whole), (far, whole)], [out], after)


def blend(place, inner, gathered, buffer=None, after=()):
    rows, width = inner.shape
    n = len(gathered)

    def column(t, s):
        back = gathered[0][0]
        for i, (k, _) in enumerate(gathered):
            back = jnp.where(t // NH == i, k, back)
        return (0, (t % NH + s[4]) % NH * NZ + (s[3] - back + NZ) % NZ)

    def kernel(place_ref, inner_ref, *refs):
        out = refs[-1]
        for i in range(n):

            @pl.when(pl.program_id(0) // NH == i)
            def _():
                out[...] = mix_share * decoded_outer(refs[i][0]) + (1.0 - mix_share) * inner_ref[...]

    code = pl.BlockSpec((1, rows, BLOCK), lambda t, s: (t % NH, 0, 0))
    state = pl.BlockSpec((rows, BLOCK), column)
    ins = [(inner, state)] + [(array, code) for _, array in gathered]
    aliases = {}
    if buffer is not None:
        aliases = {1 + len(ins): 0}
        ins.append((buffer, pl.BlockSpec(memory_space=pl.ANY)))
    out = (jax.ShapeDtypeStruct((rows, width), jnp.float32), state)
    return run(kernel, (NH * n,), ins, [out], after, (place,), aliases=aliases)


def local(
    inner_weight, first_moment, second_moment, outer_weight, outer_momentum, activations, out_grads
):
    inner, first, second = inner_weight[0], first_moment[0], second_moment[0]
    inputs, cotangents = activations[0], out_grads[0]
    replica, member = lax.axis_index("replica"), lax.axis_index("fsdp")
    core, column, row = member % NC, member // NC % NX, member // (NC * NX)
    depth, side = replica % NZ, replica // NZ
    place = jnp.stack([row, column, core, depth, side]).astype(jnp.int32)

    rights = (cotangents, on_fsdp(cotangents, TWIN))
    ahead_one, ahead_three = scatter_blocks(place, inner, (1, 3))
    from_one, from_three = on_replica(ahead_one, AHEAD[1]), on_replica(ahead_three, AHEAD[3])
    far_own, far_send = prepare(place, inputs, 0, 1, (ahead_one,))
    far_left = (far_own, on_fsdp(far_send, TWIN))
    near_own, near_send = prepare(place, inputs, 1, 3, (far_own,))
    near_left = (near_own, on_fsdp(near_send, TWIN))

    across_far_code = product(far_left, rights, (1, 1), B, after=(near_left[1],))
    across_far = on_fsdp(across_far_code, ACROSS)
    up_far_code = product(far_left, rights, (0, 2), A1, after=(across_far_code,))
    up_far = on_fsdp(up_far_code, UP)
    down_far_code = product(far_left, rights, (0, 2), A2, after=(up_far_code,))
    down_far = on_fsdp(down_far_code, DOWN)

    across_near_code = product(near_left, rights, (3, 3), B, after=(down_far_code,))
    across_near = on_fsdp(across_near_code, ACROSS)
    up_own_code = product_pair(
        near_left, rights, 3, A2, far_left, 0, B1[0], across_far, (across_near_code,)
    )
    up_own = on_fsdp(up_own_code, UP)
    ahead_two = scatter_blocks(place, inner, (2,), (up_own_code, from_one, from_three))
    from_two = on_replica(ahead_two, AHEAD[2])

    down_own_code = product_pair(
        near_left, rights, 4, A1, far_left, 0, B2[0], across_far, (ahead_two, up_far)
    )
    down_own = on_fsdp(down_own_code, DOWN)

    up_turn_code = product(
        near_left, rights, (3, 1), A1, ((up_far, 1, (0, 3), 0),), (down_own_code, down_far)
    )
    up_turn = on_fsdp(up_turn_code, UP)

    arrived = (from_one, from_two, from_three)
    far_part = sum_far(place, inner, arrived, (up_turn_code, across_near))
    far_sum = on_replica(far_part, FAR)

    down_turn_code = product(
        near_left, rights, (4, 1), A2, ((down_far, 1, (0, 3), 0),), (far_part, up_own)
    )
    down_turn = on_fsdp(down_turn_code, DOWN)

    outer_next, momentum_next, code = outer_step(
        place, inner, arrived, far_sum, outer_weight, outer_momentum, (down_turn_code, down_own)
    )
    far_code = on_replica(code, FAR)
    up_rest_code = product(
        near_left, rights, (0, 1), ALL,
        ((up_far, 0, A1, 0), (across_near, 0, B, 0), (up_own, 0, B1, A2[1])), (code,),
    )
    up_rest = on_fsdp(up_rest_code, UP)
    down_rest_code = product(
        near_left, rights, (1, 1), ALL,
        ((down_far, 0, A2, 0), (across_near, 1, B, 0), (down_own, 0, B2, A1[1])), (up_rest_code, far_code),
    )
    down_rest = on_fsdp(down_rest_code, DOWN)

    turned_code = product(
        near_left, rights, (5, 1), A,
        ((up_turn, 0, A1, 0), (down_own, 0, A1, 0), (up_own, 0, A2, 0), (down_turn, 0, A2, 0)),
        (down_rest_code,),
    )
    turned = on_fsdp(turned_code, ACROSS)

    pair = paired(code, far_code, (turned_code,))
    from_next, from_last = on_replica(pair, AHEAD[1]), on_replica(pair, AHEAD[3])
    blended = blend(place, inner, [(0, pair)])
    pair_two = paired(code, far_code, (from_next, from_last))
    from_far = on_replica(pair_two, AHEAD[2])
    blended = blend(place, inner, [(1, from_next), (3, from_last)], blended, (pair_two,))
    base = product(
        near_left, rights, (2, 1), ALL, ((across_near, 2, B, 0), (up_rest, 0, ALL, 0)), (blended,),
        jnp.float32,
    )
    blended = blend(place, inner, [(2, from_far)], blended, (base,))
    inner_next, first_next, second_next = finish(base, down_rest, turned, (blended, first, second))
    return (inner_next[None], first_next[None], second_next[None], outer_next, momentum_next)


def solution(mesh):
    in_specs = (
        P("replica", "fsdp", None),
        P("replica", "fsdp", None),
        P("replica", "fsdp", None),
        P("fsdp", "replica"),
        P("fsdp", "replica"),
        P("replica", "fsdp", None),
        P("replica", "fsdp", None),
    )
    out_specs = (
        P("replica", "fsdp", None),
        P("replica", "fsdp", None),
        P("replica", "fsdp", None),
        P("fsdp", "replica"),
        P("fsdp", "replica"),
    )
    return jax.shard_map(local, mesh=mesh, in_specs=in_specs, out_specs=out_specs, check_vma=False)
```

time: 533 us -> 101 us (0.19)
  waiting for transfers between devices: 488 us -> 21.4 us
  starting transfers between devices: 0.12 us -> 37 us
  Pallas kernels: 0 us -> 36.6 us
  matrix products: 18.1 us -> 0 us
  between operations: 15.5 us -> 0.99 us
  other arithmetic: 11.5 us -> 0 us
    reduce_scatter x2 -> x0, waiting for transfers between devices: 444 us -> none  [the longest x1 361 us: local(): lax.psum_scatter(lax.dot_general(inputs, cotangents, (((0,), (0,)), ((),...]
    all_gather x1 -> x0, waiting for transfers between devices: 43.2 us -> none  [local(): full_outer = lax.all_gather(outer_next, 'replica', axis=1, tiled=True)]
    ppermute x0 -> x22, starting transfers between devices: none -> 37 us  [the longest x8 19.2 us: on_replica(): return lax.ppermute(value, 'replica', pairs)]
    pallas_call x0 -> x24, Pallas kernels: none -> 36.6 us  [the longest x12 20.2 us: run_whole(): pl.pallas_call(body, out_shape=shape, in_specs=[vmem] * count + [pl.Block...]
    ppermute x0 -> x22, waiting for transfers between devices: none -> 21.4 us  [the longest x14 12.2 us: on_fsdp(): return lax.ppermute(value, 'fsdp', pairs)]
    dot_general x1 -> x0, matrix products: 18.1 us -> none  [local(): lax.dot_general(inputs, cotangents, (((0,), (0,)), ((), ())), preferred_e...]
    broadcast_in_dim x1 -> x0, other arithmetic: 9.65 us -> none  [local(): second_next[None]]
  transfers between devices with their start and end apart: 3 -> 22, of which waited for: 3 -> 8; matrix products, arithmetic and copies ran while one was open for 3% -> 0% of each run, Pallas kernels for 0% -> 32%
where the time goes in v2:
time: 101 us; the launch traced here: 100 us
  starting transfers between devices  37 us (37%)
  Pallas kernels  36.6 us (36%)
  waiting for transfers between devices  21.4 us (21%)
  local copies, waits for them, and re-layouts  4.38 us (4%)
    pallas_call x12, Pallas kernels, run_whole(): pl.pallas_call(body, out_shape=shape, in_specs=[vmem] * count + [pl.Block...  20.2 us
    ppermute x8, starting transfers between devices, on_replica(): return lax.ppermute(value, 'replica', pairs)  19.2 us
    ppermute x14, starting transfers between devices, on_fsdp(): return lax.ppermute(value, 'fsdp', pairs)  17.8 us
    pallas_call x12, Pallas kernels, run(): pl.pallas_call(body, out_shape=shapes, grid_spec=pltpu.PrefetchScalarGrid...  16.4 us
    ppermute x14, waiting for transfers between devices, on_fsdp(): return lax.ppermute(value, 'fsdp', pairs)  12.2 us
    ppermute x8, waiting for transfers between devices, on_replica(): return lax.ppermute(value, 'replica', pairs)  9.17 us
    unnamed x16, local copies, waits for them, and re-layouts  4.29 us
  transfers between devices with their start and end apart: 22, of which 8 were waited for; matrix products, arithmetic and copies ran while one was open for 0% of the time, Pallas kernels for 32%

profile of v2, /device:TPU:0, one launch (start us, length us, event | category | flops | bytes accessed | tf_op | source)
XLA Modules:
  0.0 100.4 jit_solution(6812372674567833868)
XLA Ops:
  0.9 1.7 %copy-done.1 = f32[1,288,2048]{2,1,0:T(8,128)S(1)} copy-done((f32[1,288,2048]{2,1,0:T(8,128)S(1)}, f32[1,288,2048]{2,1,0:T(8,128)}, u32[]{:S(2)}) %copy-start.1) | copy-done | bytes 2359320
  5.9 2.5 %shard_map.112 = (bf16[2,3,288,512]{3,2,1,0:T(8,128)(2,1)S(1)}, bf16[2,3,288,512]{3,2,1,0:T(8,128)(2,1)S(1)}) custom-call(s32[5]{0:T(128)S(1)} %stack.23.refs_0_, bf16[512,4608]{1,0:T(8,128)(2,1)S(1)} %bitcast.54, bf16[2,288,512]{2,1,0:T(8,128)(2,1)S(1)} %bitcast.47), custom_call_target="tpu_custom_call" | custom-call | flops 1 | bytes 1 | tf_op jit(solution)/shard_map/pallas_call | solution.py:86
  9.0 2.0 %collective-permute-start.7 = (f32[2,288,256]{2,1,0:T(8,128)S(1)}, f32[2,288,256]{2,1,0:T(8,128)S(1)}, u32[]{:S(2)}, u32[]{:S(2)}) collective-permute-start(f32[2,288,256]{2,1,0:T(8,128)S(1)} %get-tuple-element.17.refs_2_), channel_id=1, source_target_pairs={{0,16},{16,32},{32,48},{48,0},{64,80},{80,96},{96,112},{112,64},{1... | collective-permute-start | bytes 1769480 | tf_op jit(solution)/shard_map/ppermute | solution.py:52
  11.0 2.1 %collective-permute-start.8 = (f32[2,288,256]{2,1,0:T(8,128)S(1)}, f32[2,288,256]{2,1,0:T(8,128)S(1)}, u32[]{:S(2)}, u32[]{:S(2)}) collective-permute-start(f32[2,288,256]{2,1,0:T(8,128)S(1)} %get-tuple-element.22), channel_id=1, source_target_pairs={{0,48},{16,0},{32,16},{48,32},{64,112},{80,64},{96,80},{112,96},{1... | collective-permute-start | bytes 1769480 | tf_op jit(solution)/shard_map/ppermute | solution.py:52
  20.1 1.7 %collective-permute-start.10 = (bf16[2,288,768]{2,1,0:T(8,128)(2,1)S(1)}, bf16[2,288,768]{2,1,0:T(8,128)(2,1)S(1)}, u32[]{:S(2)}, u32[]{:S(2)}) collective-permute-start(bf16[2,288,768]{2,1,0:T(8,128)(2,1)S(1)} %shard_map.115.refs_4_), channel_id=1, source_target_pairs={{0,12},{1,13},{2,14},{3,15},{4,0},{5,1},{6,2},{7,3},{8,4},{9,5},{1... | collective-permute-start | bytes 2654216 | tf_op jit(solution)/shard_map/ppermute | solution.py:48
  27.8 3.0 %collective-permute-start.9 = (f32[2,288,256]{2,1,0:T(8,128)S(1)}, f32[2,288,256]{2,1,0:T(8,128)S(1)}, u32[]{:S(2)}, u32[]{:S(2)}) collective-permute-start(f32[2,288,256]{2,1,0:T(8,128)S(1)} %shard_map.118.refs_7_), channel_id=1, source_target_pairs={{0,32},{16,48},{32,0},{48,16},{64,96},{80,112},{96,64},{112,80},{1... | collective-permute-start | bytes 1769480 | tf_op jit(solution)/shard_map/ppermute | solution.py:52
  32.4 8.3 %collective-permute-done.4.refs_8_.refs_4_ = bf16[2,288,768]{2,1,0:T(8,128)(2,1)S(1)} collective-permute-done((bf16[2,288,768]{2,1,0:T(8,128)(2,1)S(1)}, bf16[2,288,768]{2,1,0:T(8,128)(2,1)S(1)}, u32[]{:S(2)}, u32[]{:S(2)}) %collective-permute-start.4) | collective-permute-done | bytes 884768 | tf_op jit(solution)/shard_map/ppermute | solution.py:48
  42.0 1.9 %collective-permute-start.12 = (bf16[1,288,1024]{2,1,0:T(8,128)(2,1)S(1)}, bf16[1,288,1024]{2,1,0:T(8,128)(2,1)S(1)}, u32[]{:S(2)}, u32[]{:S(2)}) collective-permute-start(bf16[1,288,1024]{2,1,0:T(8,128)(2,1)S(1)} %shard_map.119.refs_5_), channel_id=1, source_target_pairs={{0,12},{1,13},{2,14},{3,15},{4,0},{5,1},{6,2},{7,3},{8,4},{9,5},{1... | collective-permute-start | bytes 1769480 | tf_op jit(solution)/shard_map/ppermute | solution.py:48
  45.6 2.8 %collective-permute-start.11 = (f32[288,256]{1,0:T(8,128)S(1)}, f32[288,256]{1,0:T(8,128)S(1)}, u32[]{:S(2)}, u32[]{:S(2)}) collective-permute-start(f32[288,256]{1,0:T(8,128)S(1)} %shard_map.121.refs_5_), channel_id=1, source_target_pairs={{0,64},{16,80},{32,96},{48,112},{64,0},{80,16},{96,32},{112,48},{1... | collective-permute-start | bytes 884744 | tf_op jit(solution)/shard_map/ppermute | solution.py:52
  49.8 3.6 %collective-permute-done.6.refs_6_ = bf16[1,288,1024]{2,1,0:T(8,128)(2,1)S(1)} collective-permute-done((bf16[1,288,1024]{2,1,0:T(8,128)(2,1)S(1)}, bf16[1,288,1024]{2,1,0:T(8,128)(2,1)S(1)}, u32[]{:S(2)}, u32[]{:S(2)}) %collective-permute-start.6) | collective-permute-done | bytes 589856 | tf_op jit(solution)/shard_map/ppermute | solution.py:48
  54.4 1.9 %collective-permute-start.16 = (bf16[1,288,768]{2,1,0:T(8,128)(2,1)S(1)}, bf16[1,288,768]{2,1,0:T(8,128)(2,1)S(1)}, u32[]{:S(2)}, u32[]{:S(2)}) collective-permute-start(bf16[1,288,768]{2,1,0:T(8,128)(2,1)S(1)} %shard_map.122.refs_8_), channel_id=1, source_target_pairs={{0,12},{1,13},{2,14},{3,15},{4,0},{5,1},{6,2},{7,3},{8,4},{9,5},{1... | collective-permute-start | bytes 1327112 | tf_op jit(solution)/shard_map/ppermute | solution.py:48
  57.8 2.7 %collective-permute-start.14 = (bf16[288,256]{1,0:T(8,128)(2,1)S(1)}, bf16[288,256]{1,0:T(8,128)(2,1)S(1)}, u32[]{:S(2)}, u32[]{:S(2)}) collective-permute-start(bf16[288,256]{1,0:T(8,128)(2,1)S(1)} %get-tuple-element.23.refs_7_.refs_0_), channel_id=1, source_target_pairs={{0,64},{16,80},{32,96},{48,112},{64,0},{80,16},{96,32},{112,48},{1... | collective-permute-start | bytes 442376 | tf_op jit(solution)/shard_map/ppermute | solution.py:52
  60.5 2.7 %shard_map.124.refs_7_ = bf16[1,288,2048]{2,1,0:T(8,128)(2,1)S(1)} custom-call(bf16[6,288,512]{2,1,0:T(8,128)(2,1)S(1)} %bitcast.43, bf16[6,288,512]{2,1,0:T(8,128)(2,1)S(1)} %collective-permute-done.refs_4_.refs_1_, bf16[512,2048]{1,0:T(8,128)(2,1)S(1)} %bitcast.26, bf16[512,2048]{1,0:T(8,128)(2,1)S(1)} %collective-permute-done.1.refs_3_.refs_5_, ...), custom_call_target="tpu_custom_call" | custom-call | tf_op jit(solution)/shard_map/pallas_call | solution.py:141
  64.4 2.7 %shard_map.125.refs_8_ = bf16[1,288,2048]{2,1,0:T(8,128)(2,1)S(1)} custom-call(bf16[6,288,512]{2,1,0:T(8,128)(2,1)S(1)} %bitcast.44, bf16[6,288,512]{2,1,0:T(8,128)(2,1)S(1)} %collective-permute-done.refs_4_.refs_1_, bf16[512,2048]{1,0:T(8,128)(2,1)S(1)} %bitcast.27, bf16[512,2048]{1,0:T(8,128)(2,1)S(1)} %collective-permute-done.1.refs_3_.refs_5_, ...), custom_call_target="tpu_custom_call" | custom-call | tf_op jit(solution)/shard_map/pallas_call | solution.py:141
  67.1 2.8 %collective-permute-start.19 = (bf16[1,288,2048]{2,1,0:T(8,128)(2,1)S(1)}, bf16[1,288,2048]{2,1,0:T(8,128)(2,1)S(1)}, u32[]{:S(2)}, u32[]{:S(2)}) collective-permute-start(bf16[1,288,2048]{2,1,0:T(8,128)(2,1)S(1)} %shard_map.125.refs_8_), channel_id=1, source_target_pairs={{0,12},{1,13},{2,14},{3,15},{4,0},{5,1},{6,2},{7,3},{8,4},{9,5},{1... | collective-permute-start | bytes 3538952 | tf_op jit(solution)/shard_map/ppermute | solution.py:48
  69.9 2.5 %shard_map.126.refs_2_ = bf16[1,288,1536]{2,1,0:T(8,128)(2,1)S(1)} custom-call(bf16[6,288,512]{2,1,0:T(8,128)(2,1)S(1)} %bitcast.45, bf16[6,288,512]{2,1,0:T(8,128)(2,1)S(1)} %collective-permute-done.refs_4_.refs_1_, bf16[512,2048]{1,0:T(8,128)(2,1)S(1)} %bitcast.28, bf16[512,2048]{1,0:T(8,128)(2,1)S(1)} %collective-permute-done.1.refs_3_.refs_5_, ...), custom_call_target="tpu_custom_call" | custom-call | tf_op jit(solution)/shard_map/pallas_call | solution.py:141
  73.0 2.0 %collective-permute-start.17 = (bf16[2,288,256]{2,1,0:T(8,128)(2,1)S(1)}, bf16[2,288,256]{2,1,0:T(8,128)(2,1)S(1)}, u32[]{:S(2)}, u32[]{:S(2)}) collective-permute-start(bf16[2,288,256]{2,1,0:T(8,128)(2,1)S(1)} %shard_map.127.refs_2_), channel_id=1, source_target_pairs={{0,16},{16,32},{32,48},{48,0},{64,80},{80,96},{96,112},{112,64},{1... | collective-permute-start | bytes 884744 | tf_op jit(solution)/shard_map/ppermute | solution.py:52
  75.1 2.2 %collective-permute-start.18 = (bf16[2,288,256]{2,1,0:T(8,128)(2,1)S(1)}, bf16[2,288,256]{2,1,0:T(8,128)(2,1)S(1)}, u32[]{:S(2)}, u32[]{:S(2)}) collective-permute-start(bf16[2,288,256]{2,1,0:T(8,128)(2,1)S(1)} %shard_map.127.refs_2_), channel_id=1, source_target_pairs={{0,48},{16,0},{32,16},{48,32},{64,112},{80,64},{96,80},{112,96},{1... | collective-permute-start | bytes 884744 | tf_op jit(solution)/shard_map/ppermute | solution.py:52
  77.2 4.6 %collective-permute-done.17.refs_2_ = bf16[2,288,256]{2,1,0:T(8,128)(2,1)S(1)} collective-permute-done((bf16[2,288,256]{2,1,0:T(8,128)(2,1)S(1)}, bf16[2,288,256]{2,1,0:T(8,128)(2,1)S(1)}, u32[]{:S(2)}, u32[]{:S(2)}) %collective-permute-start.17) | collective-permute-done | bytes 294944 | tf_op jit(solution)/shard_map/ppermute | solution.py:52
  81.9 2.8 %collective-permute-done.18.refs_3_ = bf16[2,288,256]{2,1,0:T(8,128)(2,1)S(1)} collective-permute-done((bf16[2,288,256]{2,1,0:T(8,128)(2,1)S(1)}, bf16[2,288,256]{2,1,0:T(8,128)(2,1)S(1)}, u32[]{:S(2)}, u32[]{:S(2)}) %collective-permute-start.18) | collective-permute-done | bytes 294944 | tf_op jit(solution)/shard_map/ppermute | solution.py:52
  84.7 2.4 %collective-permute-start.21 = (bf16[2,288,256]{2,1,0:T(8,128)(2,1)S(1)}, bf16[2,288,256]{2,1,0:T(8,128)(2,1)S(1)}, u32[]{:S(2)}, u32[]{:S(2)}) collective-permute-start(bf16[2,288,256]{2,1,0:T(8,128)(2,1)S(1)} %shard_map.129.refs_5_), channel_id=1, source_target_pairs={{0,32},{16,48},{32,0},{48,16},{64,96},{80,112},{96,64},{112,80},{1... | collective-permute-start | bytes 884744 | tf_op jit(solution)/shard_map/ppermute | solution.py:52
  88.2 1.9 %shard_map.130.refs_6_.refs_3_ = f32[288,2048]{1,0:T(8,128)S(1)} custom-call(s32[5]{0:T(128)S(1)} %stack.23.refs_0_, f32[288,2048]{1,0:T(8,128)S(1)} %bitcast.36, bf16[2,288,256]{2,1,0:T(8,128)(2,1)S(1)} %collective-permute-done.17.refs_2_, bf16[2,288,256]{2,1,0:T(8,128)(2,1)S(1)} %collective-permute-done.18.refs_3_, ...), custom_call_target="tpu_custom_call", output_to_operand_aliasing={{}: (4, {})} | custom-call | flops 1 | bytes 1 | tf_op jit(solution)/shard_map/pallas_call | solution.py:86
  90.4 2.7 %shard_map.131.refs_4_.refs_0_ = f32[1,288,2048]{2,1,0:T(8,128)S(1)} custom-call(bf16[6,288,512]{2,1,0:T(8,128)(2,1)S(1)} %bitcast.46, bf16[6,288,512]{2,1,0:T(8,128)(2,1)S(1)} %collective-permute-done.refs_4_.refs_1_, bf16[512,2048]{1,0:T(8,128)(2,1)S(1)} %bitcast.29, bf16[512,2048]{1,0:T(8,128)(2,1)S(1)} %collective-permute-done.1.refs_3_.refs_5_, ...), custom_call_target="tpu_custom_call" | custom-call | tf_op jit(solution)/shard_map/pallas_call | solution.py:141
  95.5 4.9 %shard_map.133 = (f32[288,2048]{1,0:T(8,128)}, f32[288,2048]{1,0:T(8,128)}, f32[288,2048]{1,0:T(8,128)}) custom-call(f32[1,288,2048]{2,1,0:T(8,128)S(1)} %shard_map.131.refs_4_.refs_0_, bf16[1,288,2048]{2,1,0:T(8,128)(2,1)S(1)} %collective-permute-done.19.refs_1_, bf16[1,288,1536]{2,1,0:T(8,128)(2,1)S(1)} %collective-permute-done.20.refs_2_, ...), custom_call_target="tpu_custom_call" | custom-call | flops 1 | bytes 1 | tf_op jit(solution)/shard_map/pallas_call | solution.py:86
  (61 shorter events, 31.1 us)
Async XLA Ops:
  0.6 12.5 %collective-permute-start.1 = (bf16[512,2048]{1,0:T(8,128)(2,1)}, bf16[512,2048]{1,0:T(8,128)(2,1)S(1)}, u32[]{:S(2)}, u32[]{:S(2)}) collective-permute-start(bf16[512,2048]{1,0:T(8,128)(2,1)} %bitcast.17), channel_id=1, source_target_pairs={{0,1},{1,0},{2,3},{3,2},{4,5},{5,4},{6,7},{7,6},{8,9},{9,8},{10,11... | collective-permute-start | bytes 6291464 | tf_op jit(solution)/shard_map/ppermute | solution.py:48
  8.4 4.7 %collective-permute-start = (bf16[6,288,512]{2,1,0:T(8,128)(2,1)S(1)}, bf16[6,288,512]{2,1,0:T(8,128)(2,1)S(1)}, u32[]{:S(2)}, u32[]{:S(2)}) collective-permute-start(bf16[6,288,512]{2,1,0:T(8,128)(2,1)S(1)} %bitcast.57), channel_id=1, source_target_pairs={{0,1},{1,0},{2,3},{3,2},{4,5},{5,4},{6,7},{7,6},{8,9},{9,8},{10,11... | collective-permute-start | bytes 5308424 | tf_op jit(solution)/shard_map/ppermute | solution.py:48
  8.9 4.2 %collective-permute-start.2 = (bf16[2,288,512]{2,1,0:T(8,128)(2,1)S(1)}, bf16[2,288,512]{2,1,0:T(8,128)(2,1)S(1)}, u32[]{:S(2)}, u32[]{:S(2)}) collective-permute-start(bf16[2,288,512]{2,1,0:T(8,128)(2,1)S(1)} %bitcast.58), channel_id=1, source_target_pairs={{0,1},{1,0},{2,3},{3,2},{4,5},{5,4},{6,7},{7,6},{8,9},{9,8},{10,11... | collective-permute-start | bytes 1769480 | tf_op jit(solution)/shard_map/ppermute | solution.py:48
  9.0 18.0 %collective-permute-start.7 = (f32[2,288,256]{2,1,0:T(8,128)S(1)}, f32[2,288,256]{2,1,0:T(8,128)S(1)}, u32[]{:S(2)}, u32[]{:S(2)}) collective-permute-start(f32[2,288,256]{2,1,0:T(8,128)S(1)} %get-tuple-element.17.refs_2_), channel_id=1, source_target_pairs={{0,16},{16,32},{32,48},{48,0},{64,80},{80,96},{96,112},{112,64},{1... | collective-permute-start | bytes 1769480 | tf_op jit(solution)/shard_map/ppermute | solution.py:52
  11.0 16.0 %collective-permute-start.8 = (f32[2,288,256]{2,1,0:T(8,128)S(1)}, f32[2,288,256]{2,1,0:T(8,128)S(1)}, u32[]{:S(2)}, u32[]{:S(2)}) collective-permute-start(f32[2,288,256]{2,1,0:T(8,128)S(1)} %get-tuple-element.22), channel_id=1, source_target_pairs={{0,48},{16,0},{32,16},{48,32},{64,112},{80,64},{96,80},{112,96},{1... | collective-permute-start | bytes 1769480 | tf_op jit(solution)/shard_map/ppermute | solution.py:52
  13.8 9.3 %collective-permute-start.5 = (bf16[1,288,512]{2,1,0:T(8,128)(2,1)S(1)}, bf16[1,288,512]{2,1,0:T(8,128)(2,1)S(1)}, u32[]{:S(2)}, u32[]{:S(2)}) collective-permute-start(bf16[1,288,512]{2,1,0:T(8,128)(2,1)S(1)} %shard_map.113.refs_4_), channel_id=1, source_target_pairs={{0,2},{1,3},{2,0},{3,1},{4,6},{5,7},{6,4},{7,5},{8,10},{9,11},{10,... | collective-permute-start | bytes 884744 | tf_op jit(solution)/shard_map/ppermute | solution.py:48
  16.9 23.8 %collective-permute-start.4 = (bf16[2,288,768]{2,1,0:T(8,128)(2,1)S(1)}, bf16[2,288,768]{2,1,0:T(8,128)(2,1)S(1)}, u32[]{:S(2)}, u32[]{:S(2)}) collective-permute-start(bf16[2,288,768]{2,1,0:T(8,128)(2,1)S(1)} %shard_map.114.refs_4_), channel_id=1, source_target_pairs={{0,4},{1,5},{2,6},{3,7},{4,8},{5,9},{6,10},{7,11},{8,12},{9,13},{1... | collective-permute-start | bytes 2654216 | tf_op jit(solution)/shard_map/ppermute | solution.py:48
  20.1 23.8 %collective-permute-start.10 = (bf16[2,288,768]{2,1,0:T(8,128)(2,1)S(1)}, bf16[2,288,768]{2,1,0:T(8,128)(2,1)S(1)}, u32[]{:S(2)}, u32[]{:S(2)}) collective-permute-start(bf16[2,288,768]{2,1,0:T(8,128)(2,1)S(1)} %shard_map.115.refs_4_), channel_id=1, source_target_pairs={{0,12},{1,13},{2,14},{3,15},{4,0},{5,1},{6,2},{7,3},{8,4},{9,5},{1... | collective-permute-start | bytes 2654216 | tf_op jit(solution)/shard_map/ppermute | solution.py:48
  23.1 21.8 %collective-permute-start.3 = (bf16[3,288,512]{2,1,0:T(8,128)(2,1)S(1)}, bf16[3,288,512]{2,1,0:T(8,128)(2,1)S(1)}, u32[]{:S(2)}, u32[]{:S(2)}) collective-permute-start(bf16[3,288,512]{2,1,0:T(8,128)(2,1)S(1)} %shard_map.116.refs_7_), channel_id=1, source_target_pairs={{0,2},{1,3},{2,0},{3,1},{4,6},{5,7},{6,4},{7,5},{8,10},{9,11},{10,... | collective-permute-start | bytes 2654216 | tf_op jit(solution)/shard_map/ppermute | solution.py:48
  27.8 17.1 %collective-permute-start.9 = (f32[2,288,256]{2,1,0:T(8,128)S(1)}, f32[2,288,256]{2,1,0:T(8,128)S(1)}, u32[]{:S(2)}, u32[]{:S(2)}) collective-permute-start(f32[2,288,256]{2,1,0:T(8,128)S(1)} %shard_map.118.refs_7_), channel_id=1, source_target_pairs={{0,32},{16,48},{32,0},{48,16},{64,96},{80,112},{96,64},{112,80},{1... | collective-permute-start | bytes 1769480 | tf_op jit(solution)/shard_map/ppermute | solution.py:52
  30.8 22.5 %collective-permute-start.6 = (bf16[1,288,1024]{2,1,0:T(8,128)(2,1)S(1)}, bf16[1,288,1024]{2,1,0:T(8,128)(2,1)S(1)}, u32[]{:S(2)}, u32[]{:S(2)}) collective-permute-start(bf16[1,288,1024]{2,1,0:T(8,128)(2,1)S(1)} %shard_map.117.refs_2_), channel_id=1, source_target_pairs={{0,4},{1,5},{2,6},{3,7},{4,8},{5,9},{6,10},{7,11},{8,12},{9,13},{1... | collective-permute-start | bytes 1769480 | tf_op jit(solution)/shard_map/ppermute | solution.py:48
  42.0 14.2 %collective-permute-start.12 = (bf16[1,288,1024]{2,1,0:T(8,128)(2,1)S(1)}, bf16[1,288,1024]{2,1,0:T(8,128)(2,1)S(1)}, u32[]{:S(2)}, u32[]{:S(2)}) collective-permute-start(bf16[1,288,1024]{2,1,0:T(8,128)(2,1)S(1)} %shard_map.119.refs_5_), channel_id=1, source_target_pairs={{0,12},{1,13},{2,14},{3,15},{4,0},{5,1},{6,2},{7,3},{8,4},{9,5},{1... | collective-permute-start | bytes 1769480 | tf_op jit(solution)/shard_map/ppermute | solution.py:48
  45.6 10.7 %copy-start.6 = (f32[288,256]{1,0:T(8,128)S(1)}, f32[288,256]{1,0:T(8,128)}, u32[]{:S(2)}) copy-start(f32[288,256]{1,0:T(8,128)} %refs_6_.1) | copy-start | bytes 884740
  45.6 10.7 %copy-start.7 = (f32[288,256]{1,0:T(8,128)S(1)}, f32[288,256]{1,0:T(8,128)}, u32[]{:S(2)}) copy-start(f32[288,256]{1,0:T(8,128)} %refs_7_.1) | copy-start | bytes 884740
  45.6 10.7 %collective-permute-start.11 = (f32[288,256]{1,0:T(8,128)S(1)}, f32[288,256]{1,0:T(8,128)S(1)}, u32[]{:S(2)}, u32[]{:S(2)}) collective-permute-start(f32[288,256]{1,0:T(8,128)S(1)} %shard_map.121.refs_5_), channel_id=1, source_target_pairs={{0,64},{16,80},{32,96},{48,112},{64,0},{80,16},{96,32},{112,48},{1... | collective-permute-start | bytes 884744 | tf_op jit(solution)/shard_map/ppermute | solution.py:52
  48.4 21.5 %collective-permute-start.15 = (bf16[1,288,768]{2,1,0:T(8,128)(2,1)S(1)}, bf16[1,288,768]{2,1,0:T(8,128)(2,1)S(1)}, u32[]{:S(2)}, u32[]{:S(2)}) collective-permute-start(bf16[1,288,768]{2,1,0:T(8,128)(2,1)S(1)} %shard_map.120.refs_5_), channel_id=1, source_target_pairs={{0,4},{1,5},{2,6},{3,7},{4,8},{5,9},{6,10},{7,11},{8,12},{9,13},{1... | collective-permute-start | bytes 1327112 | tf_op jit(solution)/shard_map/ppermute | solution.py:48
  54.4 15.5 %collective-permute-start.16 = (bf16[1,288,768]{2,1,0:T(8,128)(2,1)S(1)}, bf16[1,288,768]{2,1,0:T(8,128)(2,1)S(1)}, u32[]{:S(2)}, u32[]{:S(2)}) collective-permute-start(bf16[1,288,768]{2,1,0:T(8,128)(2,1)S(1)} %shard_map.122.refs_8_), channel_id=1, source_target_pairs={{0,12},{1,13},{2,14},{3,15},{4,0},{5,1},{6,2},{7,3},{8,4},{9,5},{1... | collective-permute-start | bytes 1327112 | tf_op jit(solution)/shard_map/ppermute | solution.py:48
  57.8 6.6 %collective-permute-start.14 = (bf16[288,256]{1,0:T(8,128)(2,1)S(1)}, bf16[288,256]{1,0:T(8,128)(2,1)S(1)}, u32[]{:S(2)}, u32[]{:S(2)}) collective-permute-start(bf16[288,256]{1,0:T(8,128)(2,1)S(1)} %get-tuple-element.23.refs_7_.refs_0_), channel_id=1, source_target_pairs={{0,64},{16,80},{32,96},{48,112},{64,0},{80,16},{96,32},{112,48},{1... | collective-permute-start | bytes 442376 | tf_op jit(solution)/shard_map/ppermute | solution.py:52
  63.2 27.1 %collective-permute-start.13 = (bf16[1,288,2048]{2,1,0:T(8,128)(2,1)S(1)}, bf16[1,288,2048]{2,1,0:T(8,128)(2,1)S(1)}, u32[]{:S(2)}, u32[]{:S(2)}) collective-permute-start(bf16[1,288,2048]{2,1,0:T(8,128)(2,1)S(1)} %shard_map.124.refs_7_), channel_id=1, source_target_pairs={{0,4},{1,5},{2,6},{3,7},{4,8},{5,9},{6,10},{7,11},{8,12},{9,13},{1... | collective-permute-start | bytes 3538952 | tf_op jit(solution)/shard_map/ppermute | solution.py:48
  67.1 27.2 %collective-permute-start.19 = (bf16[1,288,2048]{2,1,0:T(8,128)(2,1)S(1)}, bf16[1,288,2048]{2,1,0:T(8,128)(2,1)S(1)}, u32[]{:S(2)}, u32[]{:S(2)}) collective-permute-start(bf16[1,288,2048]{2,1,0:T(8,128)(2,1)S(1)} %shard_map.125.refs_8_), channel_id=1, source_target_pairs={{0,12},{1,13},{2,14},{3,15},{4,0},{5,1},{6,2},{7,3},{8,4},{9,5},{1... | collective-permute-start | bytes 3538952 | tf_op jit(solution)/shard_map/ppermute | solution.py:48
  72.4 21.9 %collective-permute-start.20 = (bf16[1,288,1536]{2,1,0:T(8,128)(2,1)S(1)}, bf16[1,288,1536]{2,1,0:T(8,128)(2,1)S(1)}, u32[]{:S(2)}, u32[]{:S(2)}) collective-permute-start(bf16[1,288,1536]{2,1,0:T(8,128)(2,1)S(1)} %shard_map.126.refs_2_), channel_id=1, source_target_pairs={{0,2},{1,3},{2,0},{3,1},{4,6},{5,7},{6,4},{7,5},{8,10},{9,11},{10,... | collective-permute-start | bytes 2654216 | tf_op jit(solution)/shard_map/ppermute | solution.py:48
  73.0 8.8 %collective-permute-start.17 = (bf16[2,288,256]{2,1,0:T(8,128)(2,1)S(1)}, bf16[2,288,256]{2,1,0:T(8,128)(2,1)S(1)}, u32[]{:S(2)}, u32[]{:S(2)}) collective-permute-start(bf16[2,288,256]{2,1,0:T(8,128)(2,1)S(1)} %shard_map.127.refs_2_), channel_id=1, source_target_pairs={{0,16},{16,32},{32,48},{48,0},{64,80},{80,96},{96,112},{112,64},{1... | collective-permute-start | bytes 884744 | tf_op jit(solution)/shard_map/ppermute | solution.py:52
  75.1 9.6 %collective-permute-start.18 = (bf16[2,288,256]{2,1,0:T(8,128)(2,1)S(1)}, bf16[2,288,256]{2,1,0:T(8,128)(2,1)S(1)}, u32[]{:S(2)}, u32[]{:S(2)}) collective-permute-start(bf16[2,288,256]{2,1,0:T(8,128)(2,1)S(1)} %shard_map.127.refs_2_), channel_id=1, source_target_pairs={{0,48},{16,0},{32,16},{48,32},{64,112},{80,64},{96,80},{112,96},{1... | collective-permute-start | bytes 884744 | tf_op jit(solution)/shard_map/ppermute | solution.py:52
  84.7 8.4 %collective-permute-start.21 = (bf16[2,288,256]{2,1,0:T(8,128)(2,1)S(1)}, bf16[2,288,256]{2,1,0:T(8,128)(2,1)S(1)}, u32[]{:S(2)}, u32[]{:S(2)}) collective-permute-start(bf16[2,288,256]{2,1,0:T(8,128)(2,1)S(1)} %shard_map.129.refs_5_), channel_id=1, source_target_pairs={{0,32},{16,48},{32,0},{48,16},{64,96},{80,112},{96,64},{112,80},{1... | collective-permute-start | bytes 884744 | tf_op jit(solution)/shard_map/ppermute | solution.py:52
  (6 other events, 19.3 us)

commit v3 on v2

--- a/solution.py
+++ b/solution.py
@@ -136,13 +136,13 @@
     vmem = pl.BlockSpec(memory_space=pltpu.VMEM)
 
     def body(*refs):
-        kernel(*refs[:count], refs[-1])
+        kernel(*refs[:count], *refs[count + len(after) :])
 
     return pl.pallas_call(
         body,
         out_shape=shape,
         in_specs=[vmem] * count + [pl.BlockSpec(memory_space=pl.ANY)] * len(after),
-        out_specs=vmem,
+        out_specs=jax.tree.map(lambda _: vmem, shape),
         compiler_params=pltpu.CompilerParams(vmem_limit_bytes=VMEM),
     )(*arrays, *after)
 
@@ -196,8 +196,30 @@
     return run_whole(kernel, [*lefts, *rights, *(array for array, *_ in received)], shape, after)
 
 
-def product_pair(lefts, rights, block, columns, lefts_last, block_last, column_last, codes, after=()):
+def combined(partial, block, columns, received, after=()):
     first, number = columns
+    rows = partial.shape[1]
+
+    def kernel(values, *rest):
+        out = rest[-1]
+
+        def step(j, which):
+            total = values[block : block + 1, :, block_columns(first + j)]
+            for i in which:
+                _, row, span, offset = received[i]
+                total = total + decoded(rest[i][row : row + 1, :, block_columns(offset + j - span[0])])
+            out[:, :, block_columns(j)] = coded(total)
+
+        for low, high, which in regions(number, received):
+            pl.loop(low, high)(lambda j, which=which: step(j, which))
+
+    shape = jax.ShapeDtypeStruct((1, rows, number * BLOCK), jnp.bfloat16)
+    return run_whole(kernel, [partial, *(array for array, *_ in received)], shape, after)
+
+
+def product_pair(lefts, rights, block, columns, lefts_last, block_last, columns_last, codes, after=()):
+    first, number = columns
+    first_last, number_last = columns_last
     rows = lefts[0].shape[1]
 
     def kernel(lo, lt, lo2, lt2, ro, rt, code, out):
@@ -205,22 +227,46 @@
         def _(j):
             out[:, :, block_columns(j)] = coded(dots((lo, lt), (ro, rt), (block, 1), first + j))
 
-        total = dots((lo2, lt2), (ro, rt), (block_last, 1), column_last)
-        total = total + decoded(code[:, :, block_columns(column_last - B[0])])
-        out[:, :, block_columns(number)] = coded(total)
-
-    shape = jax.ShapeDtypeStruct((1, rows, (number + 1) * BLOCK), jnp.bfloat16)
+        @pl.loop(0, number_last)
+        def _(j):
+            total = dots((lo2, lt2), (ro, rt), (block_last, 1), first_last + j)
+            total = total + decoded(code[:, :, block_columns(first_last - B[0] + j)])
+            out[:, :, block_columns(number + j)] = coded(total)
+
+    shape = jax.ShapeDtypeStruct((1, rows, (number + number_last) * BLOCK), jnp.bfloat16)
     return run_whole(kernel, [*lefts, *lefts_last, *rights, codes], shape, after)
 
 
-def finish(base, down, across, states, after=()):
-    rows, width = states[0].shape
+def prepare_finish(partial, block, received, up, first, second, after=()):
+    rows = partial.shape[1]
+
+    def kernel(values, code, up_ref, first_ref, second_ref, base, first_out, second_out):
+        def step(j, with_code):
+            columns = block_columns(j)
+            total = values[block, :, columns] + decoded(up_ref[0, :, columns])
+            if with_code:
+                total = total + decoded(code[received[1], :, block_columns(j - B[0])])
+            base[:, columns] = total
+            first_out[:, columns] = beta_one * first_ref[:, columns] + (1.0 - beta_one) * total
+            second_out[:, columns] = beta_two * second_ref[:, columns]
+
+        pl.loop(0, B[0])(lambda j: step(j, False))
+        pl.loop(B[0], ALL[1])(lambda j: step(j, True))
+
+    shape = (jax.ShapeDtypeStruct((rows, ALL[1] * BLOCK), jnp.float32),) * 3
+    return run_whole(kernel, [partial, received[0], up, first, second], shape, after)
+
+
+def finish(base, first_part, second_part, blended, down, across, after=()):
+    rows, width = base.shape
     wide = 2 * BLOCK
-
-    def kernel(base_ref, down_ref, across_ref, blended_ref, first_ref, second_ref, inner_out, first_out, second_out):
-        def store(total):
-            first_next = beta_one * first_ref[...] + (1.0 - beta_one) * total
-            second_next = beta_two * second_ref[...] + (1.0 - beta_two) * total * total
+    cut = A[1] // 2
+
+    def kernel(base_ref, first_ref, second_ref, blended_ref, down_ref, across_ref, inner_out, first_out, second_out):
+        def store(rest):
+            total = base_ref[...] + rest
+            first_next = first_ref[...] + (1.0 - beta_one) * rest
+            second_next = second_ref[...] + (1.0 - beta_two) * total * total
             scaled = second_next * (1.0 / corr_two)
             update = first_next * (1.0 / corr_one) / (scaled * lax.rsqrt(scaled) + epsilon)
             blended = blended_ref[...]
@@ -230,19 +276,20 @@
 
         step = pl.program_id(0)
 
-        @pl.when(step < A[1] // 2)
+        @pl.when(step < cut)
         def _():
-            store(base_ref[0] + decoded(down_ref[0]) + decoded(across_ref[0]))
-
-        @pl.when(step >= A[1] // 2)
+            store(decoded(down_ref[0]) + decoded(across_ref[0]))
+
+        @pl.when(step >= cut)
         def _():
-            store(base_ref[0] + decoded(down_ref[0]))
+            store(decoded(down_ref[0]))
 
     whole = pl.BlockSpec((1, rows, wide), lambda j: (0, 0, j))
-    part = pl.BlockSpec((1, rows, wide), lambda j: (0, 0, jnp.minimum(j, A[1] // 2 - 1)))
+    part = pl.BlockSpec((1, rows, wide), lambda j: (0, 0, jnp.minimum(j, cut - 1)))
     state = pl.BlockSpec((rows, wide), lambda j: (0, j))
     out = (jax.ShapeDtypeStruct((rows, width), jnp.float32), state)
-    ins = [(base, whole), (down, whole), (across, part)] + [(array, state) for array in states]
+    ins = [(array, state) for array in (base, first_part, second_part, blended)]
+    ins += [(down, whole), (across, part)]
     return run(kernel, (width // wide,), ins, [out] * 3, after)
 
 
@@ -267,31 +314,52 @@
     return run(kernel, (NH,), ins, [out] * n, after, (place,))
 
 
-def sum_far(place, inner, arrived, after=()):
+outer_share = 1.0 - outer_rate * (1.0 + outer_decay)
+sum_share = outer_rate * (1.0 + outer_decay) / (NZ * NH)
+momentum_share = -outer_rate * outer_decay * outer_decay
+
+
+def sum_line(place, inner, arrived, outer_weight, outer_momentum, after=()):
     rows = inner.shape[0]
 
-    def kernel(place_ref, own, a, b, c, out):
-        out[...] = own[...] + a[0] + b[0] + c[0]
-
-    part = pl.BlockSpec((1, rows, BLOCK), lambda i, s: (1, 0, 0))
-    own = pl.BlockSpec((rows, BLOCK), lambda i, s: (0, ((s[4] + 1) % NH) * NZ + s[3]))
-    out = (jax.ShapeDtypeStruct((rows, BLOCK), jnp.float32), pl.BlockSpec((rows, BLOCK), lambda i, s: (0, 0)))
-    return run(kernel, (1,), [(inner, own)] + [(a, part) for a in arrived], [out], after, (place,))
-
-
-def outer_step(place, inner, arrived, far, outer_weight, outer_momentum, after=()):
+    def kernel(place_ref, near, far, *rest):
+        here, there, weight, momentum, out = rest[:3], rest[3:6], rest[6], rest[7], rest[8]
+        out[0] = far[...] + there[0][0] + there[1][0] + there[2][0]
+        summed = near[...] + here[0][0] + here[1][0] + here[2][0]
+        out[1] = outer_share * weight[...] + momentum_share * momentum[...] + sum_share * summed
+
+    def own(d):
+        return pl.BlockSpec((rows, BLOCK), lambda i, s: (0, ((s[4] + d) % NH) * NZ + s[3]))
+
+    def part(d):
+        return pl.BlockSpec((1, rows, BLOCK), lambda i, s: (d, 0, 0))
+
+    whole = pl.BlockSpec((rows, BLOCK), lambda i, s: (0, 0))
+    ins = [(inner, own(0)), (inner, own(1))]
+    ins += [(a, part(0)) for a in arrived] + [(a, part(1)) for a in arrived]
+    ins += [(outer_weight, whole), (outer_momentum, whole)]
+    out = (
+        jax.ShapeDtypeStruct((NH, rows, BLOCK), jnp.float32),
+        pl.BlockSpec((NH, rows, BLOCK), lambda i, s: (0, 0, 0)),
+    )
+    return run(kernel, (1,), ins, [out], after, (place,))
+
+
+def outer_step(place, inner, arrived, line, far, outer_weight, outer_momentum, after=()):
     rows = inner.shape[0]
 
-    def kernel(place_ref, own, a, b, c, far_ref, weight, momentum, next_ref, momentum_ref, code_ref):
-        summed = own[...] + a[0] + b[0] + c[0] + far_ref[...]
+    def kernel(place_ref, own, a, b, c, line_ref, far_ref, weight, momentum, next_ref, momentum_ref, code_ref):
+        summed = own[...] + a[0] + b[0] + c[0] + far_ref[0]
         average = weight[...] - summed / (NZ * NH)
         momentum_next = outer_decay * momentum[...] + average
         outer_next = weight[...] - outer_rate * (average + outer_decay * momentum_next)
         next_ref[...] = outer_next
         momentum_ref[...] = momentum_next
-        code_ref[...] = coded_outer(outer_next)
+        code_ref[0] = coded_outer(outer_next)
+        code_ref[1] = coded_outer(far_ref[1] + sum_share * line_ref[0])
 
     part = pl.BlockSpec((1, rows, BLOCK), lambda i, s: (0, 0, 0))
+    both = pl.BlockSpec((NH, rows, BLOCK), lambda i, s: (0, 0, 0))
     own = pl.BlockSpec((rows, BLOCK), lambda i, s: (0, s[4] * NZ + s[3]))
     whole = pl.BlockSpec((rows, BLOCK), lambda i, s: (0, 0))
     shape = jax.ShapeDtypeStruct((rows, BLOCK), jnp.float32)
@@ -299,31 +367,25 @@
         kernel,
         (1,),
         [(inner, own)] + [(a, part) for a in arrived]
-        + [(array, whole) for array in (far, outer_weight, outer_momentum)],
-        [(shape, whole), (shape, whole), (jax.ShapeDtypeStruct((rows, BLOCK), jnp.bfloat16), whole)],
+        + [(line, part), (far, both), (outer_weight, whole), (outer_momentum, whole)],
+        [(shape, whole), (shape, whole), (jax.ShapeDtypeStruct((NH, rows, BLOCK), jnp.bfloat16), both)],
         after,
         (place,),
     )
 
 
-def paired(near, far, after=()):
-    rows = near.shape[0]
-
-    def kernel(a, b, out):
-        out[0] = a[...]
-        out[1] = b[...]
-
-    whole = pl.BlockSpec((rows, BLOCK), lambda i: (0, 0))
-    out = (
-        jax.ShapeDtypeStruct((NH, rows, BLOCK), near.dtype),
-        pl.BlockSpec((NH, rows, BLOCK), lambda i: (0, 0, 0)),
-    )
-    return run(kernel, (1,), [(near, whole), (far, whole)], [out], after)
+def copied(array, after=()):
+    def kernel(source, out):
+        out[...] = source[...]
+
+    return run_whole(kernel, [array], jax.ShapeDtypeStruct(array.shape, array.dtype), after)
 
 
 def blend(place, inner, gathered, buffer=None, after=()):
     rows, width = inner.shape
     n = len(gathered)
+    held = [i for i in range(n) if gathered[i][1] is not None]
+    known = {i: place for place, i in enumerate(held)}
 
     def column(t, s):
         back = gathered[0][0]
@@ -337,11 +399,14 @@
 
             @pl.when(pl.program_id(0) // NH == i)
             def _():
-                out[...] = mix_share * decoded_outer(refs[i][0]) + (1.0 - mix_share) * inner_ref[...]
+                half = (1.0 - mix_share) * inner_ref[...]
+                if gathered[i][1] is not None:
+                    half = mix_share * decoded_outer(refs[known[i]][0]) + half
+                out[...] = half
 
     code = pl.BlockSpec((1, rows, BLOCK), lambda t, s: (t % NH, 0, 0))
     state = pl.BlockSpec((rows, BLOCK), column)
-    ins = [(inner, state)] + [(array, code) for _, array in gathered]
+    ins = [(inner, state)] + [(gathered[i][1], code) for i in held]
     aliases = {}
     if buffer is not None:
         aliases = {1 + len(ins): 0}
@@ -378,65 +443,69 @@
     across_near_code = product(near_left, rights, (3, 3), B, after=(down_far_code,))
     across_near = on_fsdp(across_near_code, ACROSS)
     up_own_code = product_pair(
-        near_left, rights, 3, A2, far_left, 0, B1[0], across_far, (across_near_code,)
+        near_left, rights, 3, A2, far_left, 0, B1, across_far, (across_near_code,)
     )
     up_own = on_fsdp(up_own_code, UP)
     ahead_two = scatter_blocks(place, inner, (2,), (up_own_code, from_one, from_three))
     from_two = on_replica(ahead_two, AHEAD[2])
 
+    partial = product(near_left, rights, (0, 3), ALL, after=(ahead_two,), kind=jnp.float32)
+    partial_turn = product(near_left, rights, (5, 1), A, after=(partial,), kind=jnp.float32)
+
     down_own_code = product_pair(
-        near_left, rights, 4, A1, far_left, 0, B2[0], across_far, (ahead_two, up_far)
+        near_left, rights, 4, A1, far_left, 0, B2, across_far, (partial_turn, up_far)
     )
     down_own = on_fsdp(down_own_code, DOWN)
 
     up_turn_code = product(
-        near_left, rights, (3, 1), A1, ((up_far, 1, (0, 3), 0),), (down_own_code, down_far)
+        near_left, rights, (3, 1), A1, ((up_far, 1, A1, 0),), (down_own_code, down_far)
     )
     up_turn = on_fsdp(up_turn_code, UP)
 
     arrived = (from_one, from_two, from_three)
-    far_part = sum_far(place, inner, arrived, (up_turn_code, across_near))
-    far_sum = on_replica(far_part, FAR)
+    line = sum_line(
+        place, inner, arrived, outer_weight, outer_momentum, (up_turn_code, across_near)
+    )
+    far_line = on_replica(line, FAR)
 
     down_turn_code = product(
-        near_left, rights, (4, 1), A2, ((down_far, 1, (0, 3), 0),), (far_part, up_own)
+        near_left, rights, (4, 1), A2, ((down_far, 1, (0, A2[1]), 0),), (line, up_own)
     )
     down_turn = on_fsdp(down_turn_code, DOWN)
 
-    outer_next, momentum_next, code = outer_step(
-        place, inner, arrived, far_sum, outer_weight, outer_momentum, (down_turn_code, down_own)
-    )
-    far_code = on_replica(code, FAR)
-    up_rest_code = product(
-        near_left, rights, (0, 1), ALL,
-        ((up_far, 0, A1, 0), (across_near, 0, B, 0), (up_own, 0, B1, A2[1])), (code,),
+    up_rest_code = combined(
+        partial, 0, ALL,
+        ((up_far, 0, A1, 0), (across_near, 0, B, 0), (up_own, 0, B1, A2[1])), (down_turn_code,),
     )
     up_rest = on_fsdp(up_rest_code, UP)
-    down_rest_code = product(
-        near_left, rights, (1, 1), ALL,
-        ((down_far, 0, A2, 0), (across_near, 1, B, 0), (down_own, 0, B2, A1[1])), (up_rest_code, far_code),
+    down_rest_code = combined(
+        partial, 1, ALL,
+        ((down_far, 0, A2, 0), (across_near, 1, B, 0), (down_own, 0, B2, A1[1])), (up_rest_code,),
     )
     down_rest = on_fsdp(down_rest_code, DOWN)
 
-    turned_code = product(
-        near_left, rights, (5, 1), A,
+    outer_next, momentum_next, pair = outer_step(
+        place, inner, arrived, line, far_line, outer_weight, outer_momentum, (down_rest_code, up_turn)
+    )
+    turned_code = combined(
+        partial_turn, 0, A,
         ((up_turn, 0, A1, 0), (down_own, 0, A1, 0), (up_own, 0, A2, 0), (down_turn, 0, A2, 0)),
-        (down_rest_code,),
+        (pair,),
     )
     turned = on_fsdp(turned_code, ACROSS)
 
-    pair = paired(code, far_code, (turned_code,))
     from_next, from_last = on_replica(pair, AHEAD[1]), on_replica(pair, AHEAD[3])
-    blended = blend(place, inner, [(0, pair)])
-    pair_two = paired(code, far_code, (from_next, from_last))
+    blended = blend(place, inner, [(0, pair)], None, (turned_code,))
+    pair_two = copied(pair, (blended, from_next, from_last))
     from_far = on_replica(pair_two, AHEAD[2])
-    blended = blend(place, inner, [(1, from_next), (3, from_last)], blended, (pair_two,))
-    base = product(
-        near_left, rights, (2, 1), ALL, ((across_near, 2, B, 0), (up_rest, 0, ALL, 0)), (blended,),
-        jnp.float32,
+    blended = blend(place, inner, [(3, from_last), (1, from_next)], blended, (pair_two,))
+    base, first_part, second_part = prepare_finish(
+        partial, 2, (across_near, 2), up_rest, first, second, (blended,)
     )
     blended = blend(place, inner, [(2, from_far)], blended, (base,))
-    inner_next, first_next, second_next = finish(base, down_rest, turned, (blended, first, second))
+    inner_next, first_next, second_next = finish(
+        base, first_part, second_part, blended, down_rest, turned
+    )
     return (inner_next[None], first_next[None], second_next[None], outer_next, momentum_next)
 
 

time: 101 us -> 95.7 us (0.948)
  waiting for transfers between devices: 21.4 us -> 18.3 us
  starting transfers between devices: 37 us -> 35.5 us
  local copies, waits for them, and re-layouts: 4.38 us -> 3.25 us
    ppermute x8 -> x7, starting transfers between devices: 19.2 us -> 17.4 us  [on_replica(): return lax.ppermute(value, 'replica', pairs)]
    ppermute x14, waiting for transfers between devices: 12.2 us -> 10.5 us  [on_fsdp(): return lax.ppermute(value, 'fsdp', pairs)]
    ppermute x8 -> x7, waiting for transfers between devices: 9.17 us -> 7.74 us  [on_replica(): return lax.ppermute(value, 'replica', pairs)]
    unnamed x16, local copies, waits for them, and re-layouts: 4.29 us -> 3.16 us
    pallas_call x12 -> x15, Pallas kernels: 20.2 us -> 21.1 us  [run_whole(): pl.pallas_call(body, out_shape=shape, in_specs=[vmem] * count + [pl.Block...]
    pallas_call x12 -> x10, Pallas kernels: 16.4 us -> 16.4 us  [run(): pl.pallas_call(body, out_shape=shapes, grid_spec=pltpu.PrefetchScalarGrid...]
  transfers between devices with their start and end apart: 22 -> 21, of which waited for: 8 -> 12; matrix products, arithmetic and copies ran while one was open for 0% -> 0% of each run, Pallas kernels for 32% -> 34%
where the time goes in v3:
time: 95.7 us; the launch traced here: 95.5 us
  Pallas kernels  37.5 us (39%)
  starting transfers between devices  35.5 us (37%)
  waiting for transfers between devices  18.3 us (19%)
  local copies, waits for them, and re-layouts  3.25 us (3%)
  between operations  0.98 us (1%)
    pallas_call x15, Pallas kernels, run_whole(): pl.pallas_call(body, out_shape=shape, in_specs=[vmem] * count + [pl.Block...  21.1 us
    ppermute x14, starting transfers between devices, on_fsdp(): return lax.ppermute(value, 'fsdp', pairs)  18.1 us
    ppermute x7, starting transfers between devices, on_replica(): return lax.ppermute(value, 'replica', pairs)  17.4 us
    pallas_call x10, Pallas kernels, run(): pl.pallas_call(body, out_shape=shapes, grid_spec=pltpu.PrefetchScalarGrid...  16.4 us
    ppermute x14, waiting for transfers between devices, on_fsdp(): return lax.ppermute(value, 'fsdp', pairs)  10.5 us
    ppermute x7, waiting for transfers between devices, on_replica(): return lax.ppermute(value, 'replica', pairs)  7.74 us
    unnamed x16, local copies, waits for them, and re-layouts  3.16 us
  transfers between devices with their start and end apart: 21, of which 12 were waited for; matrix products, arithmetic and copies ran while one was open for 0% of the time, Pallas kernels for 34%

profile of v3, /device:TPU:0, one launch (start us, length us, event | category | flops | bytes accessed | tf_op | source)
XLA Modules:
  0.0 95.5 jit_solution(3301484288024837242)
XLA Ops:
  0.9 1.7 %copy-done.1 = f32[1,288,2048]{2,1,0:T(8,128)S(1)} copy-done((f32[1,288,2048]{2,1,0:T(8,128)S(1)}, f32[1,288,2048]{2,1,0:T(8,128)}, u32[]{:S(2)}) %copy-start.1) | copy-done | bytes 2359320
  5.9 2.5 %shard_map.112 = (bf16[2,3,288,512]{3,2,1,0:T(8,128)(2,1)S(1)}, bf16[2,3,288,512]{3,2,1,0:T(8,128)(2,1)S(1)}) custom-call(s32[5]{0:T(128)S(1)} %stack.23.refs_0_, bf16[512,4608]{1,0:T(8,128)(2,1)S(1)} %bitcast.51, bf16[2,288,512]{2,1,0:T(8,128)(2,1)S(1)} %bitcast.44), custom_call_target="tpu_custom_call" | custom-call | flops 1 | bytes 1 | tf_op jit(solution)/shard_map/pallas_call | solution.py:86
  9.0 2.0 %collective-permute-start.4 = (f32[2,288,256]{2,1,0:T(8,128)S(1)}, f32[2,288,256]{2,1,0:T(8,128)S(1)}, u32[]{:S(2)}, u32[]{:S(2)}) collective-permute-start(f32[2,288,256]{2,1,0:T(8,128)S(1)} %get-tuple-element.20.refs_2_), channel_id=1, source_target_pairs={{0,16},{16,32},{32,48},{48,0},{64,80},{80,96},{96,112},{112,64},{1... | collective-permute-start | bytes 1769480 | tf_op jit(solution)/shard_map/ppermute | solution.py:52
  11.0 2.1 %collective-permute-start.5 = (f32[2,288,256]{2,1,0:T(8,128)S(1)}, f32[2,288,256]{2,1,0:T(8,128)S(1)}, u32[]{:S(2)}, u32[]{:S(2)}) collective-permute-start(f32[2,288,256]{2,1,0:T(8,128)S(1)} %get-tuple-element.25), channel_id=1, source_target_pairs={{0,48},{16,0},{32,16},{48,32},{64,112},{80,64},{96,80},{112,96},{1... | collective-permute-start | bytes 1769480 | tf_op jit(solution)/shard_map/ppermute | solution.py:52
  13.8 1.6 %collective-permute-start.3 = (bf16[1,288,512]{2,1,0:T(8,128)(2,1)S(1)}, bf16[1,288,512]{2,1,0:T(8,128)(2,1)S(1)}, u32[]{:S(2)}, u32[]{:S(2)}) collective-permute-start(bf16[1,288,512]{2,1,0:T(8,128)(2,1)S(1)} %shard_map.113.refs_4_), channel_id=1, source_target_pairs={{0,2},{1,3},{2,0},{3,1},{4,6},{5,7},{6,4},{7,5},{8,10},{9,11},{10,... | collective-permute-start | bytes 884744 | tf_op jit(solution)/shard_map/ppermute | solution.py:48
  16.9 1.7 %collective-permute-start.7 = (bf16[2,288,768]{2,1,0:T(8,128)(2,1)S(1)}, bf16[2,288,768]{2,1,0:T(8,128)(2,1)S(1)}, u32[]{:S(2)}, u32[]{:S(2)}) collective-permute-start(bf16[2,288,768]{2,1,0:T(8,128)(2,1)S(1)} %shard_map.114.refs_4_), channel_id=1, source_target_pairs={{0,4},{1,5},{2,6},{3,7},{4,8},{5,9},{6,10},{7,11},{8,12},{9,13},{1... | collective-permute-start | bytes 2654216 | tf_op jit(solution)/shard_map/ppermute | solution.py:48
  20.1 1.7 %collective-permute-start.9 = (bf16[2,288,768]{2,1,0:T(8,128)(2,1)S(1)}, bf16[2,288,768]{2,1,0:T(8,128)(2,1)S(1)}, u32[]{:S(2)}, u32[]{:S(2)}) collective-permute-start(bf16[2,288,768]{2,1,0:T(8,128)(2,1)S(1)} %shard_map.115.refs_4_), channel_id=1, source_target_pairs={{0,12},{1,13},{2,14},{3,15},{4,0},{5,1},{6,2},{7,3},{8,4},{9,5},{1... | collective-permute-start | bytes 2654216 | tf_op jit(solution)/shard_map/ppermute | solution.py:48
  27.8 3.0 %collective-permute-start.10 = (f32[2,288,256]{2,1,0:T(8,128)S(1)}, f32[2,288,256]{2,1,0:T(8,128)S(1)}, u32[]{:S(2)}, u32[]{:S(2)}) collective-permute-start(f32[2,288,256]{2,1,0:T(8,128)S(1)} %shard_map.118.refs_4_), channel_id=1, source_target_pairs={{0,32},{16,48},{32,0},{48,16},{64,96},{80,112},{96,64},{112,80},{1... | collective-permute-start | bytes 1769480 | tf_op jit(solution)/shard_map/ppermute | solution.py:52
  30.8 1.6 %collective-permute-start.8 = (bf16[1,288,1024]{2,1,0:T(8,128)(2,1)S(1)}, bf16[1,288,1024]{2,1,0:T(8,128)(2,1)S(1)}, u32[]{:S(2)}, u32[]{:S(2)}) collective-permute-start(bf16[1,288,1024]{2,1,0:T(8,128)(2,1)S(1)} %shard_map.117.refs_2_), channel_id=1, source_target_pairs={{0,4},{1,5},{2,6},{3,7},{4,8},{5,9},{6,10},{7,11},{8,12},{9,13},{1... | collective-permute-start | bytes 1769480 | tf_op jit(solution)/shard_map/ppermute | solution.py:48
  32.4 5.1 %shard_map.119.refs_4_.refs_0_ = f32[3,288,2048]{2,1,0:T(8,128)S(1)} custom-call(bf16[6,288,512]{2,1,0:T(8,128)(2,1)S(1)} %bitcast.39, bf16[6,288,512]{2,1,0:T(8,128)(2,1)S(1)} %collective-permute-done.refs_4_.refs_1_, bf16[512,2048]{1,0:T(8,128)(2,1)S(1)} %bitcast.23, bf16[512,2048]{1,0:T(8,128)(2,1)S(1)} %collective-permute-done.1.refs_3_.refs_5_, ...), custom_call_target="tpu_custom_call" | custom-call | tf_op jit(solution)/shard_map/pallas_call | solution.py:141
  37.5 2.0 %shard_map.120.refs_7_.refs_0_ = f32[1,288,1536]{2,1,0:T(8,128)S(1)} custom-call(bf16[6,288,512]{2,1,0:T(8,128)(2,1)S(1)} %bitcast.40, bf16[6,288,512]{2,1,0:T(8,128)(2,1)S(1)} %collective-permute-done.refs_4_.refs_1_, bf16[512,2048]{1,0:T(8,128)(2,1)S(1)} %bitcast.24, bf16[512,2048]{1,0:T(8,128)(2,1)S(1)} %collective-permute-done.1.refs_3_.refs_5_, ...), custom_call_target="tpu_custom_call" | custom-call | tf_op jit(solution)/shard_map/pallas_call | solution.py:141
  42.0 1.9 %collective-permute-start.13 = (bf16[1,288,1024]{2,1,0:T(8,128)(2,1)S(1)}, bf16[1,288,1024]{2,1,0:T(8,128)(2,1)S(1)}, u32[]{:S(2)}, u32[]{:S(2)}) collective-permute-start(bf16[1,288,1024]{2,1,0:T(8,128)(2,1)S(1)} %shard_map.121.refs_5_), channel_id=1, source_target_pairs={{0,12},{1,13},{2,14},{3,15},{4,0},{5,1},{6,2},{7,3},{8,4},{9,5},{1... | collective-permute-start | bytes 1769480 | tf_op jit(solution)/shard_map/ppermute | solution.py:48
  45.7 2.8 %collective-permute-start.12 = (f32[2,288,256]{2,1,0:T(8,128)S(1)}, f32[2,288,256]{2,1,0:T(8,128)S(1)}, u32[]{:S(2)}, u32[]{:S(2)}) collective-permute-start(f32[2,288,256]{2,1,0:T(8,128)S(1)} %shard_map.123.refs_5_), channel_id=1, source_target_pairs={{0,64},{16,80},{32,96},{48,112},{64,0},{80,16},{96,32},{112,48},{1... | collective-permute-start | bytes 1769480 | tf_op jit(solution)/shard_map/ppermute | solution.py:52
  49.9 3.4 %collective-permute-done.8.refs_6_.refs_3_ = bf16[1,288,1024]{2,1,0:T(8,128)(2,1)S(1)} collective-permute-done((bf16[1,288,1024]{2,1,0:T(8,128)(2,1)S(1)}, bf16[1,288,1024]{2,1,0:T(8,128)(2,1)S(1)}, u32[]{:S(2)}, u32[]{:S(2)}) %collective-permute-start.8) | collective-permute-done | bytes 589856 | tf_op jit(solution)/shard_map/ppermute | solution.py:48
  54.4 1.9 %collective-permute-start.17 = (bf16[1,288,768]{2,1,0:T(8,128)(2,1)S(1)}, bf16[1,288,768]{2,1,0:T(8,128)(2,1)S(1)}, u32[]{:S(2)}, u32[]{:S(2)}) collective-permute-start(bf16[1,288,768]{2,1,0:T(8,128)(2,1)S(1)} %shard_map.124.refs_4_), channel_id=1, source_target_pairs={{0,12},{1,13},{2,14},{3,15},{4,0},{5,1},{6,2},{7,3},{8,4},{9,5},{1... | collective-permute-start | bytes 1327112 | tf_op jit(solution)/shard_map/ppermute | solution.py:48
  58.5 3.1 %collective-permute-start.19 = (bf16[1,288,2048]{2,1,0:T(8,128)(2,1)S(1)}, bf16[1,288,2048]{2,1,0:T(8,128)(2,1)S(1)}, u32[]{:S(2)}, u32[]{:S(2)}) collective-permute-start(bf16[1,288,2048]{2,1,0:T(8,128)(2,1)S(1)} %shard_map.126.refs_9_), channel_id=1, source_target_pairs={{0,12},{1,13},{2,14},{3,15},{4,0},{5,1},{6,2},{7,3},{8,4},{9,5},{1... | collective-permute-start | bytes 3538952 | tf_op jit(solution)/shard_map/ppermute | solution.py:48
  64.3 3.2 %collective-permute-done.17.refs_4_ = bf16[1,288,768]{2,1,0:T(8,128)(2,1)S(1)} collective-permute-done((bf16[1,288,768]{2,1,0:T(8,128)(2,1)S(1)}, bf16[1,288,768]{2,1,0:T(8,128)(2,1)S(1)}, u32[]{:S(2)}, u32[]{:S(2)}) %collective-permute-start.17) | collective-permute-done | bytes 442400 | tf_op jit(solution)/shard_map/ppermute | solution.py:48
  69.4 2.0 %collective-permute-start.16 = (bf16[2,288,256]{2,1,0:T(8,128)(2,1)S(1)}, bf16[2,288,256]{2,1,0:T(8,128)(2,1)S(1)}, u32[]{:S(2)}, u32[]{:S(2)}) collective-permute-start(bf16[2,288,256]{2,1,0:T(8,128)(2,1)S(1)} %get-tuple-element.26.refs_5_.refs_2_.refs_0_), channel_id=1, source_target_pairs={{0,16},{16,32},{32,48},{48,0},{64,80},{80,96},{96,112},{112,64},{1... | collective-permute-start | bytes 884744 | tf_op jit(solution)/shard_map/ppermute | solution.py:52
  71.4 2.1 %collective-permute-start.15 = (bf16[2,288,256]{2,1,0:T(8,128)(2,1)S(1)}, bf16[2,288,256]{2,1,0:T(8,128)(2,1)S(1)}, u32[]{:S(2)}, u32[]{:S(2)}) collective-permute-start(bf16[2,288,256]{2,1,0:T(8,128)(2,1)S(1)} %get-tuple-element.26.refs_5_.refs_2_.refs_0_), channel_id=1, source_target_pairs={{0,48},{16,0},{32,16},{48,32},{64,112},{80,64},{96,80},{112,96},{1... | collective-permute-start | bytes 884744 | tf_op jit(solution)/shard_map/ppermute | solution.py:52
  74.7 4.4 %collective-permute-done.16.refs_2_.refs_3_ = bf16[2,288,256]{2,1,0:T(8,128)(2,1)S(1)} collective-permute-done((bf16[2,288,256]{2,1,0:T(8,128)(2,1)S(1)}, bf16[2,288,256]{2,1,0:T(8,128)(2,1)S(1)}, u32[]{:S(2)}, u32[]{:S(2)}) %collective-permute-start.16) | collective-permute-done | bytes 294944 | tf_op jit(solution)/shard_map/ppermute | solution.py:52
  79.1 1.8 %collective-permute-done.15.refs_3_.refs_2_ = bf16[2,288,256]{2,1,0:T(8,128)(2,1)S(1)} collective-permute-done((bf16[2,288,256]{2,1,0:T(8,128)(2,1)S(1)}, bf16[2,288,256]{2,1,0:T(8,128)(2,1)S(1)}, u32[]{:S(2)}, u32[]{:S(2)}) %collective-permute-start.15) | collective-permute-done | bytes 294944 | tf_op jit(solution)/shard_map/ppermute | solution.py:52
  81.0 3.4 %collective-permute-start.18 = (bf16[2,288,256]{2,1,0:T(8,128)(2,1)S(1)}, bf16[2,288,256]{2,1,0:T(8,128)(2,1)S(1)}, u32[]{:S(2)}, u32[]{:S(2)}) collective-permute-start(bf16[2,288,256]{2,1,0:T(8,128)(2,1)S(1)} %shard_map.130.refs_5_), channel_id=1, source_target_pairs={{0,32},{16,48},{32,0},{48,16},{64,96},{80,112},{96,64},{112,80},{1... | collective-permute-start | bytes 884744 | tf_op jit(solution)/shard_map/ppermute | solution.py:52
  84.3 1.8 %shard_map.131.refs_5_.refs_3_ = f32[288,2048]{1,0:T(8,128)S(1)} custom-call(s32[5]{0:T(128)S(1)} %stack.23.refs_0_, f32[288,2048]{1,0:T(8,128)S(1)} %bitcast.35, bf16[2,288,256]{2,1,0:T(8,128)(2,1)S(1)} %collective-permute-done.15.refs_3_.refs_2_, bf16[2,288,256]{2,1,0:T(8,128)(2,1)S(1)} %collective-permute-done.16.refs_2_.refs_3_, ...), custom_call_target="tpu_custom_call", output_to_operand_aliasing={{}: (4, {})} | custom-call | flops 1 | bytes 1 | tf_op jit(solution)/shard_map/pallas_call | solution.py:86
  90.6 4.8 %shard_map.134 = (f32[288,2048]{1,0:T(8,128)}, f32[288,2048]{1,0:T(8,128)}, f32[288,2048]{1,0:T(8,128)}) custom-call(f32[288,2048]{1,0:T(8,128)S(1)} %get-tuple-element.27.refs_4_.refs_0_, f32[288,2048]{1,0:T(8,128)S(1)} %get-tuple-element.28.refs_1_, f32[288,2048]{1,0:T(8,128)S(1)} %get-tuple-element.29.refs_2_, f32[288,2048]{1,0:T(8,128)S(1)} %shard_map.133.refs_3_, ...), custom_call_target="tpu_custom_call" | custom-call | flops 1 | bytes 1 | tf_op jit(solution)/shard_map/pallas_call | solution.py:86
  (60 shorter events, 32.8 us)
Async XLA Ops:
  0.6 12.5 %collective-permute-start.1 = (bf16[512,2048]{1,0:T(8,128)(2,1)}, bf16[512,2048]{1,0:T(8,128)(2,1)S(1)}, u32[]{:S(2)}, u32[]{:S(2)}) collective-permute-start(bf16[512,2048]{1,0:T(8,128)(2,1)} %bitcast.17), channel_id=1, source_target_pairs={{0,1},{1,0},{2,3},{3,2},{4,5},{5,4},{6,7},{7,6},{8,9},{9,8},{10,11... | collective-permute-start | bytes 6291464 | tf_op jit(solution)/shard_map/ppermute | solution.py:48
  5.9 7.3 %copy-start = (bf16[1,512,2048]{2,1,0:T(8,128)(2,1)S(1)}, bf16[1,512,2048]{2,1,0:T(8,128)(2,1)}, u32[]{:S(2)}) copy-start(bf16[1,512,2048]{2,1,0:T(8,128)(2,1)} %param.13) | copy-start | bytes 6291460
  8.4 4.7 %collective-permute-start = (bf16[6,288,512]{2,1,0:T(8,128)(2,1)S(1)}, bf16[6,288,512]{2,1,0:T(8,128)(2,1)S(1)}, u32[]{:S(2)}, u32[]{:S(2)}) collective-permute-start(bf16[6,288,512]{2,1,0:T(8,128)(2,1)S(1)} %bitcast.54), channel_id=1, source_target_pairs={{0,1},{1,0},{2,3},{3,2},{4,5},{5,4},{6,7},{7,6},{8,9},{9,8},{10,11... | collective-permute-start | bytes 5308424 | tf_op jit(solution)/shard_map/ppermute | solution.py:48
  8.9 4.2 %collective-permute-start.2 = (bf16[2,288,512]{2,1,0:T(8,128)(2,1)S(1)}, bf16[2,288,512]{2,1,0:T(8,128)(2,1)S(1)}, u32[]{:S(2)}, u32[]{:S(2)}) collective-permute-start(bf16[2,288,512]{2,1,0:T(8,128)(2,1)S(1)} %bitcast.55), channel_id=1, source_target_pairs={{0,1},{1,0},{2,3},{3,2},{4,5},{5,4},{6,7},{7,6},{8,9},{9,8},{10,11... | collective-permute-start | bytes 1769480 | tf_op jit(solution)/shard_map/ppermute | solution.py:48
  9.0 18.0 %collective-permute-start.4 = (f32[2,288,256]{2,1,0:T(8,128)S(1)}, f32[2,288,256]{2,1,0:T(8,128)S(1)}, u32[]{:S(2)}, u32[]{:S(2)}) collective-permute-start(f32[2,288,256]{2,1,0:T(8,128)S(1)} %get-tuple-element.20.refs_2_), channel_id=1, source_target_pairs={{0,16},{16,32},{32,48},{48,0},{64,80},{80,96},{96,112},{112,64},{1... | collective-permute-start | bytes 1769480 | tf_op jit(solution)/shard_map/ppermute | solution.py:52
  11.0 15.6 %collective-permute-start.5 = (f32[2,288,256]{2,1,0:T(8,128)S(1)}, f32[2,288,256]{2,1,0:T(8,128)S(1)}, u32[]{:S(2)}, u32[]{:S(2)}) collective-permute-start(f32[2,288,256]{2,1,0:T(8,128)S(1)} %get-tuple-element.25), channel_id=1, source_target_pairs={{0,48},{16,0},{32,16},{48,32},{64,112},{80,64},{96,80},{112,96},{1... | collective-permute-start | bytes 1769480 | tf_op jit(solution)/shard_map/ppermute | solution.py:52
  13.8 9.3 %collective-permute-start.3 = (bf16[1,288,512]{2,1,0:T(8,128)(2,1)S(1)}, bf16[1,288,512]{2,1,0:T(8,128)(2,1)S(1)}, u32[]{:S(2)}, u32[]{:S(2)}) collective-permute-start(bf16[1,288,512]{2,1,0:T(8,128)(2,1)S(1)} %shard_map.113.refs_4_), channel_id=1, source_target_pairs={{0,2},{1,3},{2,0},{3,1},{4,6},{5,7},{6,4},{7,5},{8,10},{9,11},{10,... | collective-permute-start | bytes 884744 | tf_op jit(solution)/shard_map/ppermute | solution.py:48
  16.9 23.8 %collective-permute-start.7 = (bf16[2,288,768]{2,1,0:T(8,128)(2,1)S(1)}, bf16[2,288,768]{2,1,0:T(8,128)(2,1)S(1)}, u32[]{:S(2)}, u32[]{:S(2)}) collective-permute-start(bf16[2,288,768]{2,1,0:T(8,128)(2,1)S(1)} %shard_map.114.refs_4_), channel_id=1, source_target_pairs={{0,4},{1,5},{2,6},{3,7},{4,8},{5,9},{6,10},{7,11},{8,12},{9,13},{1... | collective-permute-start | bytes 2654216 | tf_op jit(solution)/shard_map/ppermute | solution.py:48
  20.1 23.9 %collective-permute-start.9 = (bf16[2,288,768]{2,1,0:T(8,128)(2,1)S(1)}, bf16[2,288,768]{2,1,0:T(8,128)(2,1)S(1)}, u32[]{:S(2)}, u32[]{:S(2)}) collective-permute-start(bf16[2,288,768]{2,1,0:T(8,128)(2,1)S(1)} %shard_map.115.refs_4_), channel_id=1, source_target_pairs={{0,12},{1,13},{2,14},{3,15},{4,0},{5,1},{6,2},{7,3},{8,4},{9,5},{1... | collective-permute-start | bytes 2654216 | tf_op jit(solution)/shard_map/ppermute | solution.py:48
  23.1 21.8 %collective-permute-start.6 = (bf16[3,288,512]{2,1,0:T(8,128)(2,1)S(1)}, bf16[3,288,512]{2,1,0:T(8,128)(2,1)S(1)}, u32[]{:S(2)}, u32[]{:S(2)}) collective-permute-start(bf16[3,288,512]{2,1,0:T(8,128)(2,1)S(1)} %shard_map.116.refs_7_), channel_id=1, source_target_pairs={{0,2},{1,3},{2,0},{3,1},{4,6},{5,7},{6,4},{7,5},{8,10},{9,11},{10,... | collective-permute-start | bytes 2654216 | tf_op jit(solution)/shard_map/ppermute | solution.py:48
  27.8 17.2 %collective-permute-start.10 = (f32[2,288,256]{2,1,0:T(8,128)S(1)}, f32[2,288,256]{2,1,0:T(8,128)S(1)}, u32[]{:S(2)}, u32[]{:S(2)}) collective-permute-start(f32[2,288,256]{2,1,0:T(8,128)S(1)} %shard_map.118.refs_4_), channel_id=1, source_target_pairs={{0,32},{16,48},{32,0},{48,16},{64,96},{80,112},{96,64},{112,80},{1... | collective-permute-start | bytes 1769480 | tf_op jit(solution)/shard_map/ppermute | solution.py:52
  30.8 22.5 %collective-permute-start.8 = (bf16[1,288,1024]{2,1,0:T(8,128)(2,1)S(1)}, bf16[1,288,1024]{2,1,0:T(8,128)(2,1)S(1)}, u32[]{:S(2)}, u32[]{:S(2)}) collective-permute-start(bf16[1,288,1024]{2,1,0:T(8,128)(2,1)S(1)} %shard_map.117.refs_2_), channel_id=1, source_target_pairs={{0,4},{1,5},{2,6},{3,7},{4,8},{5,9},{6,10},{7,11},{8,12},{9,13},{1... | collective-permute-start | bytes 1769480 | tf_op jit(solution)/shard_map/ppermute | solution.py:48
  42.0 15.5 %collective-permute-start.13 = (bf16[1,288,1024]{2,1,0:T(8,128)(2,1)S(1)}, bf16[1,288,1024]{2,1,0:T(8,128)(2,1)S(1)}, u32[]{:S(2)}, u32[]{:S(2)}) collective-permute-start(bf16[1,288,1024]{2,1,0:T(8,128)(2,1)S(1)} %shard_map.121.refs_5_), channel_id=1, source_target_pairs={{0,12},{1,13},{2,14},{3,15},{4,0},{5,1},{6,2},{7,3},{8,4},{9,5},{1... | collective-permute-start | bytes 1769480 | tf_op jit(solution)/shard_map/ppermute | solution.py:48
  45.7 17.1 %collective-permute-start.12 = (f32[2,288,256]{2,1,0:T(8,128)S(1)}, f32[2,288,256]{2,1,0:T(8,128)S(1)}, u32[]{:S(2)}, u32[]{:S(2)}) collective-permute-start(f32[2,288,256]{2,1,0:T(8,128)S(1)} %shard_map.123.refs_5_), channel_id=1, source_target_pairs={{0,64},{16,80},{32,96},{48,112},{64,0},{80,16},{96,32},{112,48},{1... | collective-permute-start | bytes 1769480 | tf_op jit(solution)/shard_map/ppermute | solution.py:52
  48.5 14.3 %collective-permute-start.14 = (bf16[1,288,768]{2,1,0:T(8,128)(2,1)S(1)}, bf16[1,288,768]{2,1,0:T(8,128)(2,1)S(1)}, u32[]{:S(2)}, u32[]{:S(2)}) collective-permute-start(bf16[1,288,768]{2,1,0:T(8,128)(2,1)S(1)} %shard_map.122.refs_11_), channel_id=1, source_target_pairs={{0,4},{1,5},{2,6},{3,7},{4,8},{5,9},{6,10},{7,11},{8,12},{9,13},{1... | collective-permute-start | bytes 1327112 | tf_op jit(solution)/shard_map/ppermute | solution.py:48
  54.4 13.2 %collective-permute-start.17 = (bf16[1,288,768]{2,1,0:T(8,128)(2,1)S(1)}, bf16[1,288,768]{2,1,0:T(8,128)(2,1)S(1)}, u32[]{:S(2)}, u32[]{:S(2)}) collective-permute-start(bf16[1,288,768]{2,1,0:T(8,128)(2,1)S(1)} %shard_map.124.refs_4_), channel_id=1, source_target_pairs={{0,12},{1,13},{2,14},{3,15},{4,0},{5,1},{6,2},{7,3},{8,4},{9,5},{1... | collective-permute-start | bytes 1327112 | tf_op jit(solution)/shard_map/ppermute | solution.py:48
  57.1 30.2 %collective-permute-start.11 = (bf16[1,288,2048]{2,1,0:T(8,128)(2,1)S(1)}, bf16[1,288,2048]{2,1,0:T(8,128)(2,1)S(1)}, u32[]{:S(2)}, u32[]{:S(2)}) collective-permute-start(bf16[1,288,2048]{2,1,0:T(8,128)(2,1)S(1)} %shard_map.125.refs_4_), channel_id=1, source_target_pairs={{0,4},{1,5},{2,6},{3,7},{4,8},{5,9},{6,10},{7,11},{8,12},{9,13},{1... | collective-permute-start | bytes 3538952 | tf_op jit(solution)/shard_map/ppermute | solution.py:48
  58.5 32.2 %collective-permute-start.19 = (bf16[1,288,2048]{2,1,0:T(8,128)(2,1)S(1)}, bf16[1,288,2048]{2,1,0:T(8,128)(2,1)S(1)}, u32[]{:S(2)}, u32[]{:S(2)}) collective-permute-start(bf16[1,288,2048]{2,1,0:T(8,128)(2,1)S(1)} %shard_map.126.refs_9_), channel_id=1, source_target_pairs={{0,12},{1,13},{2,14},{3,15},{4,0},{5,1},{6,2},{7,3},{8,4},{9,5},{1... | collective-permute-start | bytes 3538952 | tf_op jit(solution)/shard_map/ppermute | solution.py:48
  68.8 21.6 %collective-permute-start.20 = (bf16[1,288,1536]{2,1,0:T(8,128)(2,1)S(1)}, bf16[1,288,1536]{2,1,0:T(8,128)(2,1)S(1)}, u32[]{:S(2)}, u32[]{:S(2)}) collective-permute-start(bf16[1,288,1536]{2,1,0:T(8,128)(2,1)S(1)} %shard_map.128.refs_3_), channel_id=1, source_target_pairs={{0,2},{1,3},{2,0},{3,1},{4,6},{5,7},{6,4},{7,5},{8,10},{9,11},{10,... | collective-permute-start | bytes 2654216 | tf_op jit(solution)/shard_map/ppermute | solution.py:48
  69.4 9.7 %collective-permute-start.16 = (bf16[2,288,256]{2,1,0:T(8,128)(2,1)S(1)}, bf16[2,288,256]{2,1,0:T(8,128)(2,1)S(1)}, u32[]{:S(2)}, u32[]{:S(2)}) collective-permute-start(bf16[2,288,256]{2,1,0:T(8,128)(2,1)S(1)} %get-tuple-element.26.refs_5_.refs_2_.refs_0_), channel_id=1, source_target_pairs={{0,16},{16,32},{32,48},{48,0},{64,80},{80,96},{96,112},{112,64},{1... | collective-permute-start | bytes 884744 | tf_op jit(solution)/shard_map/ppermute | solution.py:52
  71.4 9.6 %collective-permute-start.15 = (bf16[2,288,256]{2,1,0:T(8,128)(2,1)S(1)}, bf16[2,288,256]{2,1,0:T(8,128)(2,1)S(1)}, u32[]{:S(2)}, u32[]{:S(2)}) collective-permute-start(bf16[2,288,256]{2,1,0:T(8,128)(2,1)S(1)} %get-tuple-element.26.refs_5_.refs_2_.refs_0_), channel_id=1, source_target_pairs={{0,48},{16,0},{32,16},{48,32},{64,112},{80,64},{96,80},{112,96},{1... | collective-permute-start | bytes 884744 | tf_op jit(solution)/shard_map/ppermute | solution.py:52
  80.9 6.4 %copy-start.4 = (f32[1,288,2048]{2,1,0:T(8,128)S(1)}, f32[1,288,2048]{2,1,0:T(8,128)}, u32[]{:S(2)}) copy-start(f32[1,288,2048]{2,1,0:T(8,128)} %param.8) | copy-start | bytes 7077892
  81.0 6.3 %copy-start.5 = (f32[1,288,2048]{2,1,0:T(8,128)S(1)}, f32[1,288,2048]{2,1,0:T(8,128)}, u32[]{:S(2)}) copy-start(f32[1,288,2048]{2,1,0:T(8,128)} %param.9) | copy-start | bytes 7077892
  81.0 8.3 %collective-permute-start.18 = (bf16[2,288,256]{2,1,0:T(8,128)(2,1)S(1)}, bf16[2,288,256]{2,1,0:T(8,128)(2,1)S(1)}, u32[]{:S(2)}, u32[]{:S(2)}) collective-permute-start(bf16[2,288,256]{2,1,0:T(8,128)(2,1)S(1)} %shard_map.130.refs_5_), channel_id=1, source_target_pairs={{0,32},{16,48},{32,0},{48,16},{64,96},{80,112},{96,64},{112,80},{1... | collective-permute-start | bytes 884744 | tf_op jit(solution)/shard_map/ppermute | solution.py:52
  (5 other events, 13.9 us)

commit v4 on v3

--- a/solution.py
+++ b/solution.py
@@ -100,35 +100,41 @@
     return result[0] if len(outs) == 1 else result
 
 
-def prepare(place, activations, first, count, after=()):
+def prepare(place, activations, after=()):
     tokens, width = activations.shape
     quarter = width // NY
     rows = quarter // (NX * NC)
 
     def distance(i):
-        step = first + i
-        return jnp.where(step == 0, 2, jnp.where(step == 1, 1, jnp.where(step == 2, 3, 0)))
-
-    def kernel(place_ref, a_ref, own_ref, send_ref, turned):
+        return jnp.where(i == 0, 2, jnp.where(i == 1, 1, jnp.where(i == 2, 3, 0)))
+
+    def kernel(place_ref, a_ref, far_own, far_send, near_own, near_send, turned):
         turned[...] = a_ref[...].T
         x, core = place_ref[1], place_ref[2]
-        for dx in range(NX):
-            column = (x + dx) % NX
-            own = pl.multiple_of((column * NC + core) * rows, 16)
-            other = pl.multiple_of((column * NC + 1 - core) * rows, 16)
-            own_ref[dx, 0] = turned[pl.ds(own, rows), :]
-            send_ref[dx, 0] = turned[pl.ds(other, rows), :]
-
-    out = (
-        jax.ShapeDtypeStruct((NX, count, rows, tokens), jnp.bfloat16),
-        pl.BlockSpec((NX, 1, rows, tokens), lambda i, s: (0, i, 0, 0)),
-    )
+
+        def write(own_ref, send_ref):
+            for dx in range(NX):
+                column = (x + dx) % NX
+                own = pl.multiple_of((column * NC + core) * rows, 16)
+                other = pl.multiple_of((column * NC + 1 - core) * rows, 16)
+                own_ref[dx, 0] = turned[pl.ds(own, rows), :]
+                send_ref[dx, 0] = turned[pl.ds(other, rows), :]
+
+        pl.when(pl.program_id(0) == 0)(lambda: write(far_own, far_send))
+        pl.when(pl.program_id(0) > 0)(lambda: write(near_own, near_send))
+
+    def out(count):
+        return (
+            jax.ShapeDtypeStruct((NX, count, rows, tokens), jnp.bfloat16),
+            pl.BlockSpec((NX, 1, rows, tokens), lambda i, s: (0, 0 if count == 1 else jnp.maximum(i - 1, 0), 0, 0)),
+        )
+
     source = pl.BlockSpec((tokens, quarter), lambda i, s: (0, (s[0] + distance(i)) % NY))
-    own, send = run(
-        kernel, (count,), [(activations, source)], [out, out], after, (place,),
+    results = run(
+        kernel, (NY,), [(activations, source)], [out(1), out(1), out(NY - 1), out(NY - 1)], after, (place,),
         [pltpu.VMEM((quarter, tokens), jnp.bfloat16)],
     )
-    return own.reshape(NX * count, rows, tokens), send.reshape(NX * count, rows, tokens)
+    return [array.reshape(-1, rows, tokens) for array in results]
 
 
 def run_whole(kernel, arrays, shape, after=()):
@@ -323,9 +329,10 @@
     rows = inner.shape[0]
 
     def kernel(place_ref, near, far, *rest):
-        here, there, weight, momentum, out = rest[:3], rest[3:6], rest[6], rest[7], rest[8]
+        here, there, weight, momentum, sum_out, out = rest[:3], rest[3:6], rest[6], rest[7], rest[8], rest[9]
         out[0] = far[...] + there[0][0] + there[1][0] + there[2][0]
         summed = near[...] + here[0][0] + here[1][0] + here[2][0]
+        sum_out[...] = summed
         out[1] = outer_share * weight[...] + momentum_share * momentum[...] + sum_share * summed
 
     def own(d):
@@ -338,19 +345,19 @@
     ins = [(inner, own(0)), (inner, own(1))]
     ins += [(a, part(0)) for a in arrived] + [(a, part(1)) for a in arrived]
     ins += [(outer_weight, whole), (outer_momentum, whole)]
-    out = (
-        jax.ShapeDtypeStruct((NH, rows, BLOCK), jnp.float32),
-        pl.BlockSpec((NH, rows, BLOCK), lambda i, s: (0, 0, 0)),
-    )
-    return run(kernel, (1,), ins, [out], after, (place,))
-
-
-def outer_step(place, inner, arrived, line, far, outer_weight, outer_momentum, after=()):
-    rows = inner.shape[0]
-
-    def kernel(place_ref, own, a, b, c, line_ref, far_ref, weight, momentum, next_ref, momentum_ref, code_ref):
-        summed = own[...] + a[0] + b[0] + c[0] + far_ref[0]
-        average = weight[...] - summed / (NZ * NH)
+    outs = [
+        (jax.ShapeDtypeStruct((rows, BLOCK), jnp.float32), whole),
+        (
+            jax.ShapeDtypeStruct((NH, rows, BLOCK), jnp.float32),
+            pl.BlockSpec((NH, rows, BLOCK), lambda i, s: (0, 0, 0)),
+        ),
+    ]
+    return run(kernel, (1,), ins, outs, after, (place,))
+
+
+def outer_step(line_sum, line, far, outer_weight, outer_momentum, after=()):
+    def kernel(sum_ref, line_ref, far_ref, weight, momentum, next_ref, momentum_ref, code_ref):
+        average = weight[...] - (sum_ref[...] + far_ref[0]) / (NZ * NH)
         momentum_next = outer_decay * momentum[...] + average
         outer_next = weight[...] - outer_rate * (average + outer_decay * momentum_next)
         next_ref[...] = outer_next
@@ -358,20 +365,9 @@
         code_ref[0] = coded_outer(outer_next)
         code_ref[1] = coded_outer(far_ref[1] + sum_share * line_ref[0])
 
-    part = pl.BlockSpec((1, rows, BLOCK), lambda i, s: (0, 0, 0))
-    both = pl.BlockSpec((NH, rows, BLOCK), lambda i, s: (0, 0, 0))
-    own = pl.BlockSpec((rows, BLOCK), lambda i, s: (0, s[4] * NZ + s[3]))
-    whole = pl.BlockSpec((rows, BLOCK), lambda i, s: (0, 0))
-    shape = jax.ShapeDtypeStruct((rows, BLOCK), jnp.float32)
-    return run(
-        kernel,
-        (1,),
-        [(inner, own)] + [(a, part) for a in arrived]
-        + [(line, part), (far, both), (outer_weight, whole), (outer_momentum, whole)],
-        [(shape, whole), (shape, whole), (jax.ShapeDtypeStruct((NH, rows, BLOCK), jnp.bfloat16), both)],
-        after,
-        (place,),
-    )
+    shape = jax.ShapeDtypeStruct(line_sum.shape, jnp.float32)
+    shapes = (shape, shape, jax.ShapeDtypeStruct(line.shape, jnp.bfloat16))
+    return run_whole(kernel, [line_sum, line, far, outer_weight, outer_momentum], shapes, after)
 
 
 def copied(array, after=()):
@@ -382,37 +378,32 @@
 
 
 def blend(place, inner, gathered, buffer=None, after=()):
-    rows, width = inner.shape
-    n = len(gathered)
-    held = [i for i in range(n) if gathered[i][1] is not None]
-    known = {i: place for place, i in enumerate(held)}
-
-    def column(t, s):
-        back = gathered[0][0]
-        for i, (k, _) in enumerate(gathered):
-            back = jnp.where(t // NH == i, k, back)
-        return (0, (t % NH + s[4]) % NH * NZ + (s[3] - back + NZ) % NZ)
-
-    def kernel(place_ref, inner_ref, *refs):
-        out = refs[-1]
-        for i in range(n):
-
-            @pl.when(pl.program_id(0) // NH == i)
-            def _():
-                half = (1.0 - mix_share) * inner_ref[...]
-                if gathered[i][1] is not None:
-                    half = mix_share * decoded_outer(refs[known[i]][0]) + half
-                out[...] = half
-
-    code = pl.BlockSpec((1, rows, BLOCK), lambda t, s: (t % NH, 0, 0))
-    state = pl.BlockSpec((rows, BLOCK), column)
-    ins = [(inner, state)] + [(gathered[i][1], code) for i in held]
+    count = len(gathered)
+
+    def kernel(place_ref, inner_ref, *rest):
+        out = rest[-1]
+        for (back, _), code in zip(gathered, rest):
+            for d in range(NH):
+                column = (d + place_ref[4]) % NH * NZ + (place_ref[3] - back + NZ) % NZ
+                half = (1.0 - mix_share) * inner_ref[:, block_columns(column)]
+                out[:, block_columns(column)] = mix_share * decoded_outer(code[d]) + half
+
+    vmem = pl.BlockSpec(memory_space=pltpu.VMEM)
+    operands = [place, inner, *(codes for _, codes in gathered)]
+    specs = [pl.BlockSpec(memory_space=pltpu.SMEM)] + [vmem] * (1 + count)
     aliases = {}
     if buffer is not None:
-        aliases = {1 + len(ins): 0}
-        ins.append((buffer, pl.BlockSpec(memory_space=pl.ANY)))
-    out = (jax.ShapeDtypeStruct((rows, width), jnp.float32), state)
-    return run(kernel, (NH * n,), ins, [out], after, (place,), aliases=aliases)
+        aliases = {len(operands): 0}
+        operands.append(buffer)
+        specs.append(vmem)
+    return pl.pallas_call(
+        kernel,
+        out_shape=jax.ShapeDtypeStruct(inner.shape, jnp.float32),
+        in_specs=specs + [pl.BlockSpec(memory_space=pl.ANY)] * len(after),
+        out_specs=vmem,
+        input_output_aliases=aliases,
+        compiler_params=pltpu.CompilerParams(vmem_limit_bytes=VMEM),
+    )(*operands, *after)
 
 
 def local(
@@ -426,12 +417,11 @@
     place = jnp.stack([row, column, core, depth, side]).astype(jnp.int32)
 
     rights = (cotangents, on_fsdp(cotangents, TWIN))
-    ahead_one, ahead_three = scatter_blocks(place, inner, (1, 3))
+    far_own, far_send, near_own, near_send = prepare(place, inputs)
+    far_left = (far_own, on_fsdp(far_send, TWIN))
+    near_left = (near_own, on_fsdp(near_send, TWIN))
+    ahead_one, ahead_three = scatter_blocks(place, inner, (1, 3), (far_own,))
     from_one, from_three = on_replica(ahead_one, AHEAD[1]), on_replica(ahead_three, AHEAD[3])
-    far_own, far_send = prepare(place, inputs, 0, 1, (ahead_one,))
-    far_left = (far_own, on_fsdp(far_send, TWIN))
-    near_own, near_send = prepare(place, inputs, 1, 3, (far_own,))
-    near_left = (near_own, on_fsdp(near_send, TWIN))
 
     across_far_code = product(far_left, rights, (1, 1), B, after=(near_left[1],))
     across_far = on_fsdp(across_far_code, ACROSS)
@@ -463,7 +453,7 @@
     up_turn = on_fsdp(up_turn_code, UP)
 
     arrived = (from_one, from_two, from_three)
-    line = sum_line(
+    line_sum, line = sum_line(
         place, inner, arrived, outer_weight, outer_momentum, (up_turn_code, across_near)
     )
     far_line = on_replica(line, FAR)
@@ -485,7 +475,7 @@
     down_rest = on_fsdp(down_rest_code, DOWN)
 
     outer_next, momentum_next, pair = outer_step(
-        place, inner, arrived, line, far_line, outer_weight, outer_momentum, (down_rest_code, up_turn)
+        line_sum, line, far_line, outer_weight, outer_momentum, (down_rest_code, up_turn)
     )
     turned_code = combined(
         partial_turn, 0, A,

time: 95.7 us -> 94.1 us (0.983)
  waiting for transfers between devices: 18.3 us -> 20.7 us
  Pallas kernels: 37.5 us -> 35.5 us
  starting transfers between devices: 35.5 us -> 34.4 us
    pallas_call x10 -> x5, Pallas kernels: 16.4 us -> 10.4 us  [run(): pl.pallas_call(body, out_shape=shapes, grid_spec=pltpu.PrefetchScalarGrid...]
    pallas_call x0 -> x3, Pallas kernels: none -> 3.06 us  [blend(): pl.pallas_call(kernel, out_shape=jax.ShapeDtypeStruct(inner.shape, jnp.fl...]
    ppermute x14, waiting for transfers between devices: 10.5 us -> 13.1 us  [on_fsdp(): return lax.ppermute(value, 'fsdp', pairs)]
    pallas_call x15 -> x16, Pallas kernels: 21.1 us -> 22 us  [run_whole(): pl.pallas_call(body, out_shape=shape, in_specs=[vmem] * count + [pl.Block...]
    unnamed x16 -> x14, local copies, waits for them, and re-layouts: 3.16 us -> 2.37 us
  transfers between devices with their start and end apart: 21 -> 21, of which waited for: 12 -> 9; matrix products, arithmetic and copies ran while one was open for 0% -> 0% of each run, Pallas kernels for 34% -> 33%
where the time goes in v4:
time: 94.1 us; the launch traced here: 94 us
  Pallas kernels  35.5 us (38%)
  starting transfers between devices  34.4 us (37%)
  waiting for transfers between devices  20.7 us (22%)
  local copies, waits for them, and re-layouts  2.46 us (3%)
  between operations  0.96 us (1%)
    pallas_call x16, Pallas kernels, run_whole(): pl.pallas_call(body, out_shape=shape, in_specs=[vmem] * count + [pl.Block...  22 us
    ppermute x14, starting transfers between devices, on_fsdp(): return lax.ppermute(value, 'fsdp', pairs)  17.8 us
    ppermute x7, starting transfers between devices, on_replica(): return lax.ppermute(value, 'replica', pairs)  16.6 us
    ppermute x14, waiting for transfers between devices, on_fsdp(): return lax.ppermute(value, 'fsdp', pairs)  13.1 us
    pallas_call x5, Pallas kernels, run(): pl.pallas_call(body, out_shape=shapes, grid_spec=pltpu.PrefetchScalarGrid...  10.4 us
    ppermute x7, waiting for transfers between devices, on_replica(): return lax.ppermute(value, 'replica', pairs)  7.66 us
    pallas_call x3, Pallas kernels, blend(): pl.pallas_call(kernel, out_shape=jax.ShapeDtypeStruct(inner.shape, jnp.fl...  3.06 us
    unnamed x14, local copies, waits for them, and re-layouts  2.37 us
  transfers between devices with their start and end apart: 21, of which 9 were waited for; matrix products, arithmetic and copies ran while one was open for 0% of the time, Pallas kernels for 33%

profile of v4, /device:TPU:0, one launch (start us, length us, event | category | flops | bytes accessed | tf_op | source)
XLA Modules:
  0.0 94.0 jit_solution(6943993043973501340)
XLA Ops:
  0.9 2.3 %copy-done.2 = bf16[1,512,4608]{2,1,0:T(8,128)(2,1)S(1)} copy-done((bf16[1,512,4608]{2,1,0:T(8,128)(2,1)S(1)}, bf16[1,512,4608]{2,1,0:T(8,128)(2,1)}, u32[]{:S(2)}) %copy-start.2) | copy-done | bytes 4718616
  3.2 3.1 %shard_map.110 = (bf16[2,1,288,512]{3,2,1,0:T(8,128)(2,1)S(1)}, bf16[2,1,288,512]{3,2,1,0:T(8,128)(2,1)S(1)}, bf16[2,3,288,512]{3,2,1,0:T(8,128)(2,1)S(1)}, bf16[2,3,288,512]{3,2,1,0:T(8,128)(2,1)S(1)}) custom-call(s32[5]{0:T(128)S(1)} %stack.23.refs_0_.place_ref, bf16[512,4608]{1,0:T(8,128)(2,1)S(1)} %bitcast.49), custom_call_target="tpu_custom_call" | custom-call | flops 1 | bytes 1 | tf_op jit(solution)/shard_map/pallas_call | solution.py:86
  7.8 2.1 %collective-permute-start.4 = (f32[2,288,256]{2,1,0:T(8,128)S(1)}, f32[2,288,256]{2,1,0:T(8,128)S(1)}, u32[]{:S(2)}, u32[]{:S(2)}) collective-permute-start(f32[2,288,256]{2,1,0:T(8,128)S(1)} %get-tuple-element.26), channel_id=1, source_target_pairs={{0,16},{16,32},{32,48},{48,0},{64,80},{80,96},{96,112},{112,64},{1... | collective-permute-start | bytes 1769480 | tf_op jit(solution)/shard_map/ppermute | solution.py:52
  9.9 2.2 %collective-permute-start.5 = (f32[2,288,256]{2,1,0:T(8,128)S(1)}, f32[2,288,256]{2,1,0:T(8,128)S(1)}, u32[]{:S(2)}, u32[]{:S(2)}) collective-permute-start(f32[2,288,256]{2,1,0:T(8,128)S(1)} %get-tuple-element.27), channel_id=1, source_target_pairs={{0,48},{16,0},{32,16},{48,32},{64,112},{80,64},{96,80},{112,96},{1... | collective-permute-start | bytes 1769480 | tf_op jit(solution)/shard_map/ppermute | solution.py:52
  12.8 1.6 %collective-permute-start.3 = (bf16[1,288,512]{2,1,0:T(8,128)(2,1)S(1)}, bf16[1,288,512]{2,1,0:T(8,128)(2,1)S(1)}, u32[]{:S(2)}, u32[]{:S(2)}) collective-permute-start(bf16[1,288,512]{2,1,0:T(8,128)(2,1)S(1)} %shard_map.111.refs_4_), channel_id=1, source_target_pairs={{0,2},{1,3},{2,0},{3,1},{4,6},{5,7},{6,4},{7,5},{8,10},{9,11},{10,... | collective-permute-start | bytes 884744 | tf_op jit(solution)/shard_map/ppermute | solution.py:48
  14.4 1.5 %shard_map.112.refs_4_ = bf16[2,288,768]{2,1,0:T(8,128)(2,1)S(1)} custom-call(bf16[2,288,512]{2,1,0:T(8,128)(2,1)S(1)} %bitcast.45, bf16[2,288,512]{2,1,0:T(8,128)(2,1)S(1)} %collective-permute-done.2.refs_1_.refs_3_, bf16[512,2048]{1,0:T(8,128)(2,1)S(1)} %bitcast.19, bf16[512,2048]{1,0:T(8,128)(2,1)S(1)} %collective-permute-done.1.refs_3_.refs_5_, ...), custom_call_target="tpu_custom_call" | custom-call | tf_op jit(solution)/shard_map/pallas_call | solution.py:147
  15.9 1.6 %collective-permute-start.7 = (bf16[2,288,768]{2,1,0:T(8,128)(2,1)S(1)}, bf16[2,288,768]{2,1,0:T(8,128)(2,1)S(1)}, u32[]{:S(2)}, u32[]{:S(2)}) collective-permute-start(bf16[2,288,768]{2,1,0:T(8,128)(2,1)S(1)} %shard_map.112.refs_4_), channel_id=1, source_target_pairs={{0,4},{1,5},{2,6},{3,7},{4,8},{5,9},{6,10},{7,11},{8,12},{9,13},{1... | collective-permute-start | bytes 2654216 | tf_op jit(solution)/shard_map/ppermute | solution.py:48
  19.0 1.7 %collective-permute-start.9 = (bf16[2,288,768]{2,1,0:T(8,128)(2,1)S(1)}, bf16[2,288,768]{2,1,0:T(8,128)(2,1)S(1)}, u32[]{:S(2)}, u32[]{:S(2)}) collective-permute-start(bf16[2,288,768]{2,1,0:T(8,128)(2,1)S(1)} %shard_map.113.refs_4_), channel_id=1, source_target_pairs={{0,12},{1,13},{2,14},{3,15},{4,0},{5,1},{6,2},{7,3},{8,4},{9,5},{1... | collective-permute-start | bytes 2654216 | tf_op jit(solution)/shard_map/ppermute | solution.py:48
  26.7 3.0 %collective-permute-start.10 = (f32[2,288,256]{2,1,0:T(8,128)S(1)}, f32[2,288,256]{2,1,0:T(8,128)S(1)}, u32[]{:S(2)}, u32[]{:S(2)}) collective-permute-start(f32[2,288,256]{2,1,0:T(8,128)S(1)} %shard_map.117.refs_4_), channel_id=1, source_target_pairs={{0,32},{16,48},{32,0},{48,16},{64,96},{80,112},{96,64},{112,80},{1... | collective-permute-start | bytes 1769480 | tf_op jit(solution)/shard_map/ppermute | solution.py:52
  29.7 1.6 %collective-permute-start.8 = (bf16[1,288,1024]{2,1,0:T(8,128)(2,1)S(1)}, bf16[1,288,1024]{2,1,0:T(8,128)(2,1)S(1)}, u32[]{:S(2)}, u32[]{:S(2)}) collective-permute-start(bf16[1,288,1024]{2,1,0:T(8,128)(2,1)S(1)} %shard_map.115.refs_2_), channel_id=1, source_target_pairs={{0,4},{1,5},{2,6},{3,7},{4,8},{5,9},{6,10},{7,11},{8,12},{9,13},{1... | collective-permute-start | bytes 1769480 | tf_op jit(solution)/shard_map/ppermute | solution.py:48
  31.3 5.1 %shard_map.118.refs_4_.refs_0_ = f32[3,288,2048]{2,1,0:T(8,128)S(1)} custom-call(bf16[6,288,512]{2,1,0:T(8,128)(2,1)S(1)} %bitcast.38, bf16[6,288,512]{2,1,0:T(8,128)(2,1)S(1)} %collective-permute-done.refs_4_.refs_1_, bf16[512,2048]{1,0:T(8,128)(2,1)S(1)} %bitcast.23, bf16[512,2048]{1,0:T(8,128)(2,1)S(1)} %collective-permute-done.1.refs_3_.refs_5_, ...), custom_call_target="tpu_custom_call" | custom-call | tf_op jit(solution)/shard_map/pallas_call | solution.py:147
  36.4 2.0 %shard_map.119.refs_7_.refs_0_ = f32[1,288,1536]{2,1,0:T(8,128)S(1)} custom-call(bf16[6,288,512]{2,1,0:T(8,128)(2,1)S(1)} %bitcast.39, bf16[6,288,512]{2,1,0:T(8,128)(2,1)S(1)} %collective-permute-done.refs_4_.refs_1_, bf16[512,2048]{1,0:T(8,128)(2,1)S(1)} %bitcast.24, bf16[512,2048]{1,0:T(8,128)(2,1)S(1)} %collective-permute-done.1.refs_3_.refs_5_, ...), custom_call_target="tpu_custom_call" | custom-call | tf_op jit(solution)/shard_map/pallas_call | solution.py:147
  41.0 1.9 %collective-permute-start.13 = (bf16[1,288,1024]{2,1,0:T(8,128)(2,1)S(1)}, bf16[1,288,1024]{2,1,0:T(8,128)(2,1)S(1)}, u32[]{:S(2)}, u32[]{:S(2)}) collective-permute-start(bf16[1,288,1024]{2,1,0:T(8,128)(2,1)S(1)} %shard_map.120.refs_5_), channel_id=1, source_target_pairs={{0,12},{1,13},{2,14},{3,15},{4,0},{5,1},{6,2},{7,3},{8,4},{9,5},{1... | collective-permute-start | bytes 1769480 | tf_op jit(solution)/shard_map/ppermute | solution.py:48
  44.7 2.8 %collective-permute-start.12 = (f32[2,288,256]{2,1,0:T(8,128)S(1)}, f32[2,288,256]{2,1,0:T(8,128)S(1)}, u32[]{:S(2)}, u32[]{:S(2)}) collective-permute-start(f32[2,288,256]{2,1,0:T(8,128)S(1)} %get-tuple-element.28.refs_5_.refs_1_), channel_id=1, source_target_pairs={{0,64},{16,80},{32,96},{48,112},{64,0},{80,16},{96,32},{112,48},{1... | collective-permute-start | bytes 1769480 | tf_op jit(solution)/shard_map/ppermute | solution.py:52
  48.8 3.5 %collective-permute-done.8.refs_6_.refs_3_ = bf16[1,288,1024]{2,1,0:T(8,128)(2,1)S(1)} collective-permute-done((bf16[1,288,1024]{2,1,0:T(8,128)(2,1)S(1)}, bf16[1,288,1024]{2,1,0:T(8,128)(2,1)S(1)}, u32[]{:S(2)}, u32[]{:S(2)}) %collective-permute-start.8) | collective-permute-done | bytes 589856 | tf_op jit(solution)/shard_map/ppermute | solution.py:48
  53.4 1.9 %collective-permute-start.17 = (bf16[1,288,768]{2,1,0:T(8,128)(2,1)S(1)}, bf16[1,288,768]{2,1,0:T(8,128)(2,1)S(1)}, u32[]{:S(2)}, u32[]{:S(2)}) collective-permute-start(bf16[1,288,768]{2,1,0:T(8,128)(2,1)S(1)} %shard_map.123.refs_4_), channel_id=1, source_target_pairs={{0,12},{1,13},{2,14},{3,15},{4,0},{5,1},{6,2},{7,3},{8,4},{9,5},{1... | collective-permute-start | bytes 1327112 | tf_op jit(solution)/shard_map/ppermute | solution.py:48
  57.3 3.3 %collective-permute-start.19 = (bf16[1,288,2048]{2,1,0:T(8,128)(2,1)S(1)}, bf16[1,288,2048]{2,1,0:T(8,128)(2,1)S(1)}, u32[]{:S(2)}, u32[]{:S(2)}) collective-permute-start(bf16[1,288,2048]{2,1,0:T(8,128)(2,1)S(1)} %shard_map.125.refs_5_), channel_id=1, source_target_pairs={{0,12},{1,13},{2,14},{3,15},{4,0},{5,1},{6,2},{7,3},{8,4},{9,5},{1... | collective-permute-start | bytes 3538952 | tf_op jit(solution)/shard_map/ppermute | solution.py:48
  62.7 3.8 %collective-permute-done.17.refs_4_ = bf16[1,288,768]{2,1,0:T(8,128)(2,1)S(1)} collective-permute-done((bf16[1,288,768]{2,1,0:T(8,128)(2,1)S(1)}, bf16[1,288,768]{2,1,0:T(8,128)(2,1)S(1)}, u32[]{:S(2)}, u32[]{:S(2)}) %collective-permute-start.17) | collective-permute-done | bytes 442400 | tf_op jit(solution)/shard_map/ppermute | solution.py:48
  69.3 2.3 %collective-permute-start.15 = (bf16[2,288,256]{2,1,0:T(8,128)(2,1)S(1)}, bf16[2,288,256]{2,1,0:T(8,128)(2,1)S(1)}, u32[]{:S(2)}, u32[]{:S(2)}) collective-permute-start(bf16[2,288,256]{2,1,0:T(8,128)(2,1)S(1)} %get-tuple-element.30.refs_5_.rest_0_.refs_0_), channel_id=1, source_target_pairs={{0,48},{16,0},{32,16},{48,32},{64,112},{80,64},{96,80},{112,96},{1... | collective-permute-start | bytes 884744 | tf_op jit(solution)/shard_map/ppermute | solution.py:52
  72.6 4.9 %collective-permute-done.16.refs_2_.rest_1_ = bf16[2,288,256]{2,1,0:T(8,128)(2,1)S(1)} collective-permute-done((bf16[2,288,256]{2,1,0:T(8,128)(2,1)S(1)}, bf16[2,288,256]{2,1,0:T(8,128)(2,1)S(1)}, u32[]{:S(2)}, u32[]{:S(2)}) %collective-permute-start.16) | collective-permute-done | bytes 294944 | tf_op jit(solution)/shard_map/ppermute | solution.py:52
  77.5 1.6 %collective-permute-done.15.refs_3_.rest_0_ = bf16[2,288,256]{2,1,0:T(8,128)(2,1)S(1)} collective-permute-done((bf16[2,288,256]{2,1,0:T(8,128)(2,1)S(1)}, bf16[2,288,256]{2,1,0:T(8,128)(2,1)S(1)}, u32[]{:S(2)}, u32[]{:S(2)}) %collective-permute-start.15) | collective-permute-done | bytes 294944 | tf_op jit(solution)/shard_map/ppermute | solution.py:52
  79.1 3.2 %collective-permute-start.18 = (bf16[2,288,256]{2,1,0:T(8,128)(2,1)S(1)}, bf16[2,288,256]{2,1,0:T(8,128)(2,1)S(1)}, u32[]{:S(2)}, u32[]{:S(2)}) collective-permute-start(bf16[2,288,256]{2,1,0:T(8,128)(2,1)S(1)} %shard_map.129.rest_3_), channel_id=1, source_target_pairs={{0,32},{16,48},{32,0},{48,16},{64,96},{80,112},{96,64},{112,80},{1... | collective-permute-start | bytes 884744 | tf_op jit(solution)/shard_map/ppermute | solution.py:52
  83.6 2.4 %collective-permute-done.11.refs_2_ = bf16[1,288,2048]{2,1,0:T(8,128)(2,1)S(1)} collective-permute-done((bf16[1,288,2048]{2,1,0:T(8,128)(2,1)S(1)}, bf16[1,288,2048]{2,1,0:T(8,128)(2,1)S(1)}, u32[]{:S(2)}, u32[]{:S(2)}) %collective-permute-start.11) | collective-permute-done | bytes 1179680 | tf_op jit(solution)/shard_map/ppermute | solution.py:48
  89.1 4.8 %shard_map.133 = (f32[288,2048]{1,0:T(8,128)}, f32[288,2048]{1,0:T(8,128)}, f32[288,2048]{1,0:T(8,128)}) custom-call(f32[288,2048]{1,0:T(8,128)S(1)} %get-tuple-element.31.rest_2_.refs_0_, f32[288,2048]{1,0:T(8,128)S(1)} %get-tuple-element.32.refs_1_, f32[288,2048]{1,0:T(8,128)S(1)} %get-tuple-element.33.refs_2_, f32[288,2048]{1,0:T(8,128)S(1)} %shard_map.132.refs_3_, ...), custom_call_target="tpu_custom_call" | custom-call | flops 1 | bytes 1 | tf_op jit(solution)/shard_map/pallas_call | solution.py:86
  (57 shorter events, 28.7 us)
Async XLA Ops:
  0.6 11.5 %collective-permute-start.1 = (bf16[512,2048]{1,0:T(8,128)(2,1)}, bf16[512,2048]{1,0:T(8,128)(2,1)S(1)}, u32[]{:S(2)}, u32[]{:S(2)}) collective-permute-start(bf16[512,2048]{1,0:T(8,128)(2,1)} %bitcast.17), channel_id=1, source_target_pairs={{0,1},{1,0},{2,3},{3,2},{4,5},{5,4},{6,7},{7,6},{8,9},{9,8},{10,11... | collective-permute-start | bytes 6291464 | tf_op jit(solution)/shard_map/ppermute | solution.py:48
  6.4 5.8 %collective-permute-start = (bf16[6,288,512]{2,1,0:T(8,128)(2,1)S(1)}, bf16[6,288,512]{2,1,0:T(8,128)(2,1)S(1)}, u32[]{:S(2)}, u32[]{:S(2)}) collective-permute-start(bf16[6,288,512]{2,1,0:T(8,128)(2,1)S(1)} %bitcast.52), channel_id=1, source_target_pairs={{0,1},{1,0},{2,3},{3,2},{4,5},{5,4},{6,7},{7,6},{8,9},{9,8},{10,11... | collective-permute-start | bytes 5308424 | tf_op jit(solution)/shard_map/ppermute | solution.py:48
  6.9 5.2 %collective-permute-start.2 = (bf16[2,288,512]{2,1,0:T(8,128)(2,1)S(1)}, bf16[2,288,512]{2,1,0:T(8,128)(2,1)S(1)}, u32[]{:S(2)}, u32[]{:S(2)}) collective-permute-start(bf16[2,288,512]{2,1,0:T(8,128)(2,1)S(1)} %bitcast.53), channel_id=1, source_target_pairs={{0,1},{1,0},{2,3},{3,2},{4,5},{5,4},{6,7},{7,6},{8,9},{9,8},{10,11... | collective-permute-start | bytes 1769480 | tf_op jit(solution)/shard_map/ppermute | solution.py:48
  7.0 5.2 %copy-start = (bf16[1,512,2048]{2,1,0:T(8,128)(2,1)S(1)}, bf16[1,512,2048]{2,1,0:T(8,128)(2,1)}, u32[]{:S(2)}) copy-start(bf16[1,512,2048]{2,1,0:T(8,128)(2,1)} %param.13) | copy-start | bytes 6291460
  7.8 18.1 %collective-permute-start.4 = (f32[2,288,256]{2,1,0:T(8,128)S(1)}, f32[2,288,256]{2,1,0:T(8,128)S(1)}, u32[]{:S(2)}, u32[]{:S(2)}) collective-permute-start(f32[2,288,256]{2,1,0:T(8,128)S(1)} %get-tuple-element.26), channel_id=1, source_target_pairs={{0,16},{16,32},{32,48},{48,0},{64,80},{80,96},{96,112},{112,64},{1... | collective-permute-start | bytes 1769480 | tf_op jit(solution)/shard_map/ppermute | solution.py:52
  9.9 16.0 %collective-permute-start.5 = (f32[2,288,256]{2,1,0:T(8,128)S(1)}, f32[2,288,256]{2,1,0:T(8,128)S(1)}, u32[]{:S(2)}, u32[]{:S(2)}) collective-permute-start(f32[2,288,256]{2,1,0:T(8,128)S(1)} %get-tuple-element.27), channel_id=1, source_target_pairs={{0,48},{16,0},{32,16},{48,32},{64,112},{80,64},{96,80},{112,96},{1... | collective-permute-start | bytes 1769480 | tf_op jit(solution)/shard_map/ppermute | solution.py:52
  12.8 9.2 %collective-permute-start.3 = (bf16[1,288,512]{2,1,0:T(8,128)(2,1)S(1)}, bf16[1,288,512]{2,1,0:T(8,128)(2,1)S(1)}, u32[]{:S(2)}, u32[]{:S(2)}) collective-permute-start(bf16[1,288,512]{2,1,0:T(8,128)(2,1)S(1)} %shard_map.111.refs_4_), channel_id=1, source_target_pairs={{0,2},{1,3},{2,0},{3,1},{4,6},{5,7},{6,4},{7,5},{8,10},{9,11},{10,... | collective-permute-start | bytes 884744 | tf_op jit(solution)/shard_map/ppermute | solution.py:48
  15.9 23.8 %collective-permute-start.7 = (bf16[2,288,768]{2,1,0:T(8,128)(2,1)S(1)}, bf16[2,288,768]{2,1,0:T(8,128)(2,1)S(1)}, u32[]{:S(2)}, u32[]{:S(2)}) collective-permute-start(bf16[2,288,768]{2,1,0:T(8,128)(2,1)S(1)} %shard_map.112.refs_4_), channel_id=1, source_target_pairs={{0,4},{1,5},{2,6},{3,7},{4,8},{5,9},{6,10},{7,11},{8,12},{9,13},{1... | collective-permute-start | bytes 2654216 | tf_op jit(solution)/shard_map/ppermute | solution.py:48
  19.0 23.9 %collective-permute-start.9 = (bf16[2,288,768]{2,1,0:T(8,128)(2,1)S(1)}, bf16[2,288,768]{2,1,0:T(8,128)(2,1)S(1)}, u32[]{:S(2)}, u32[]{:S(2)}) collective-permute-start(bf16[2,288,768]{2,1,0:T(8,128)(2,1)S(1)} %shard_map.113.refs_4_), channel_id=1, source_target_pairs={{0,12},{1,13},{2,14},{3,15},{4,0},{5,1},{6,2},{7,3},{8,4},{9,5},{1... | collective-permute-start | bytes 2654216 | tf_op jit(solution)/shard_map/ppermute | solution.py:48
  22.0 21.9 %collective-permute-start.6 = (bf16[3,288,512]{2,1,0:T(8,128)(2,1)S(1)}, bf16[3,288,512]{2,1,0:T(8,128)(2,1)S(1)}, u32[]{:S(2)}, u32[]{:S(2)}) collective-permute-start(bf16[3,288,512]{2,1,0:T(8,128)(2,1)S(1)} %shard_map.114.refs_7_), channel_id=1, source_target_pairs={{0,2},{1,3},{2,0},{3,1},{4,6},{5,7},{6,4},{7,5},{8,10},{9,11},{10,... | collective-permute-start | bytes 2654216 | tf_op jit(solution)/shard_map/ppermute | solution.py:48
  26.7 17.2 %collective-permute-start.10 = (f32[2,288,256]{2,1,0:T(8,128)S(1)}, f32[2,288,256]{2,1,0:T(8,128)S(1)}, u32[]{:S(2)}, u32[]{:S(2)}) collective-permute-start(f32[2,288,256]{2,1,0:T(8,128)S(1)} %shard_map.117.refs_4_), channel_id=1, source_target_pairs={{0,32},{16,48},{32,0},{48,16},{64,96},{80,112},{96,64},{112,80},{1... | collective-permute-start | bytes 1769480 | tf_op jit(solution)/shard_map/ppermute | solution.py:52
  29.7 22.6 %collective-permute-start.8 = (bf16[1,288,1024]{2,1,0:T(8,128)(2,1)S(1)}, bf16[1,288,1024]{2,1,0:T(8,128)(2,1)S(1)}, u32[]{:S(2)}, u32[]{:S(2)}) collective-permute-start(bf16[1,288,1024]{2,1,0:T(8,128)(2,1)S(1)} %shard_map.115.refs_2_), channel_id=1, source_target_pairs={{0,4},{1,5},{2,6},{3,7},{4,8},{5,9},{6,10},{7,11},{8,12},{9,13},{1... | collective-permute-start | bytes 1769480 | tf_op jit(solution)/shard_map/ppermute | solution.py:48
  41.0 15.4 %collective-permute-start.13 = (bf16[1,288,1024]{2,1,0:T(8,128)(2,1)S(1)}, bf16[1,288,1024]{2,1,0:T(8,128)(2,1)S(1)}, u32[]{:S(2)}, u32[]{:S(2)}) collective-permute-start(bf16[1,288,1024]{2,1,0:T(8,128)(2,1)S(1)} %shard_map.120.refs_5_), channel_id=1, source_target_pairs={{0,12},{1,13},{2,14},{3,15},{4,0},{5,1},{6,2},{7,3},{8,4},{9,5},{1... | collective-permute-start | bytes 1769480 | tf_op jit(solution)/shard_map/ppermute | solution.py:48
  44.7 17.1 %collective-permute-start.12 = (f32[2,288,256]{2,1,0:T(8,128)S(1)}, f32[2,288,256]{2,1,0:T(8,128)S(1)}, u32[]{:S(2)}, u32[]{:S(2)}) collective-permute-start(f32[2,288,256]{2,1,0:T(8,128)S(1)} %get-tuple-element.28.refs_5_.refs_1_), channel_id=1, source_target_pairs={{0,64},{16,80},{32,96},{48,112},{64,0},{80,16},{96,32},{112,48},{1... | collective-permute-start | bytes 1769480 | tf_op jit(solution)/shard_map/ppermute | solution.py:52
  47.5 14.3 %collective-permute-start.14 = (bf16[1,288,768]{2,1,0:T(8,128)(2,1)S(1)}, bf16[1,288,768]{2,1,0:T(8,128)(2,1)S(1)}, u32[]{:S(2)}, u32[]{:S(2)}) collective-permute-start(bf16[1,288,768]{2,1,0:T(8,128)(2,1)S(1)} %shard_map.121.refs_11_), channel_id=1, source_target_pairs={{0,4},{1,5},{2,6},{3,7},{4,8},{5,9},{6,10},{7,11},{8,12},{9,13},{1... | collective-permute-start | bytes 1327112 | tf_op jit(solution)/shard_map/ppermute | solution.py:48
  53.4 13.2 %collective-permute-start.17 = (bf16[1,288,768]{2,1,0:T(8,128)(2,1)S(1)}, bf16[1,288,768]{2,1,0:T(8,128)(2,1)S(1)}, u32[]{:S(2)}, u32[]{:S(2)}) collective-permute-start(bf16[1,288,768]{2,1,0:T(8,128)(2,1)S(1)} %shard_map.123.refs_4_), channel_id=1, source_target_pairs={{0,12},{1,13},{2,14},{3,15},{4,0},{5,1},{6,2},{7,3},{8,4},{9,5},{1... | collective-permute-start | bytes 1327112 | tf_op jit(solution)/shard_map/ppermute | solution.py:48
  56.1 29.9 %collective-permute-start.11 = (bf16[1,288,2048]{2,1,0:T(8,128)(2,1)S(1)}, bf16[1,288,2048]{2,1,0:T(8,128)(2,1)S(1)}, u32[]{:S(2)}, u32[]{:S(2)}) collective-permute-start(bf16[1,288,2048]{2,1,0:T(8,128)(2,1)S(1)} %shard_map.124.refs_4_), channel_id=1, source_target_pairs={{0,4},{1,5},{2,6},{3,7},{4,8},{5,9},{6,10},{7,11},{8,12},{9,13},{1... | collective-permute-start | bytes 3538952 | tf_op jit(solution)/shard_map/ppermute | solution.py:48
  57.3 31.8 %collective-permute-start.19 = (bf16[1,288,2048]{2,1,0:T(8,128)(2,1)S(1)}, bf16[1,288,2048]{2,1,0:T(8,128)(2,1)S(1)}, u32[]{:S(2)}, u32[]{:S(2)}) collective-permute-start(bf16[1,288,2048]{2,1,0:T(8,128)(2,1)S(1)} %shard_map.125.refs_5_), channel_id=1, source_target_pairs={{0,12},{1,13},{2,14},{3,15},{4,0},{5,1},{6,2},{7,3},{8,4},{9,5},{1... | collective-permute-start | bytes 3538952 | tf_op jit(solution)/shard_map/ppermute | solution.py:48
  67.8 20.6 %collective-permute-start.20 = (bf16[1,288,1536]{2,1,0:T(8,128)(2,1)S(1)}, bf16[1,288,1536]{2,1,0:T(8,128)(2,1)S(1)}, u32[]{:S(2)}, u32[]{:S(2)}) collective-permute-start(bf16[1,288,1536]{2,1,0:T(8,128)(2,1)S(1)} %shard_map.127.rest_1_), channel_id=1, source_target_pairs={{0,2},{1,3},{2,0},{3,1},{4,6},{5,7},{6,4},{7,5},{8,10},{9,11},{10,... | collective-permute-start | bytes 2654216 | tf_op jit(solution)/shard_map/ppermute | solution.py:48
  68.4 9.1 %collective-permute-start.16 = (bf16[2,288,256]{2,1,0:T(8,128)(2,1)S(1)}, bf16[2,288,256]{2,1,0:T(8,128)(2,1)S(1)}, u32[]{:S(2)}, u32[]{:S(2)}) collective-permute-start(bf16[2,288,256]{2,1,0:T(8,128)(2,1)S(1)} %get-tuple-element.30.refs_5_.rest_0_.refs_0_), channel_id=1, source_target_pairs={{0,16},{16,32},{32,48},{48,0},{64,80},{80,96},{96,112},{112,64},{1... | collective-permute-start | bytes 884744 | tf_op jit(solution)/shard_map/ppermute | solution.py:52
  69.3 9.8 %collective-permute-start.15 = (bf16[2,288,256]{2,1,0:T(8,128)(2,1)S(1)}, bf16[2,288,256]{2,1,0:T(8,128)(2,1)S(1)}, u32[]{:S(2)}, u32[]{:S(2)}) collective-permute-start(bf16[2,288,256]{2,1,0:T(8,128)(2,1)S(1)} %get-tuple-element.30.refs_5_.rest_0_.refs_0_), channel_id=1, source_target_pairs={{0,48},{16,0},{32,16},{48,32},{64,112},{80,64},{96,80},{112,96},{1... | collective-permute-start | bytes 884744 | tf_op jit(solution)/shard_map/ppermute | solution.py:52
  79.1 6.9 %copy-start.3 = (f32[1,288,2048]{2,1,0:T(8,128)S(1)}, f32[1,288,2048]{2,1,0:T(8,128)}, u32[]{:S(2)}) copy-start(f32[1,288,2048]{2,1,0:T(8,128)} %param.8) | copy-start | bytes 7077892
  79.1 6.9 %copy-start.4 = (f32[1,288,2048]{2,1,0:T(8,128)S(1)}, f32[1,288,2048]{2,1,0:T(8,128)}, u32[]{:S(2)}) copy-start(f32[1,288,2048]{2,1,0:T(8,128)} %param.9) | copy-start | bytes 7077892
  79.1 8.4 %collective-permute-start.18 = (bf16[2,288,256]{2,1,0:T(8,128)(2,1)S(1)}, bf16[2,288,256]{2,1,0:T(8,128)(2,1)S(1)}, u32[]{:S(2)}, u32[]{:S(2)}) collective-permute-start(bf16[2,288,256]{2,1,0:T(8,128)(2,1)S(1)} %shard_map.129.rest_3_), channel_id=1, source_target_pairs={{0,32},{16,48},{32,0},{48,16},{64,96},{80,112},{96,64},{112,80},{1... | collective-permute-start | bytes 884744 | tf_op jit(solution)/shard_map/ppermute | solution.py:52
  (4 other events, 12.0 us)

commit v5 on v4

--- a/solution.py
+++ b/solution.py
@@ -14,6 +14,7 @@
 weight_decay = 0.1
 epsilon = 1e-08
 step_count = 200.0
+kept_share = 1.0 - inner_rate * weight_decay
 corr_one = 1.0 - beta_one**step_count
 corr_two = 1.0 - beta_two**step_count
 
@@ -274,9 +275,8 @@
             first_next = first_ref[...] + (1.0 - beta_one) * rest
             second_next = second_ref[...] + (1.0 - beta_two) * total * total
             scaled = second_next * (1.0 / corr_two)
-            update = first_next * (1.0 / corr_one) / (scaled * lax.rsqrt(scaled) + epsilon)
-            blended = blended_ref[...]
-            inner_out[...] = blended - inner_rate * (update + weight_decay * blended)
+            update = first_next * (inner_rate / corr_one) / (scaled * lax.rsqrt(scaled) + epsilon)
+            inner_out[...] = blended_ref[...] - update
             first_out[...] = first_next
             second_out[...] = second_next
 
@@ -300,24 +300,23 @@
 
 
 def scatter_blocks(place, inner, places, after=()):
-    rows = inner.shape[0]
     n = len(places)
 
-    def kernel(place_ref, *refs):
-        for source, target in zip(refs[:n], refs[n:]):
-            target[0] = source[...]
-
-    ins = []
-    for k in places:
-        def source(i, s, k=k):
-            return (0, ((s[4] + i) % NH) * NZ + (s[3] + k) % NZ)
-
-        ins.append((inner, pl.BlockSpec((rows, BLOCK), source)))
-    out = (
-        jax.ShapeDtypeStruct((NH, rows, BLOCK), jnp.float32),
-        pl.BlockSpec((1, rows, BLOCK), lambda i, s: (i, 0, 0)),
-    )
-    return run(kernel, (NH,), ins, [out] * n, after, (place,))
+    def kernel(place_ref, inner_ref, *rest):
+        for k, out in zip(places, rest[len(after) :]):
+            for d in range(NH):
+                column = (d + place_ref[4]) % NH * NZ + (place_ref[3] + k) % NZ
+                out[d] = inner_ref[:, block_columns(column)]
+
+    vmem = pl.BlockSpec(memory_space=pltpu.VMEM)
+    result = pl.pallas_call(
+        kernel,
+        out_shape=(jax.ShapeDtypeStruct((NH, inner.shape[0], BLOCK), jnp.float32),) * n,
+        in_specs=[pl.BlockSpec(memory_space=pltpu.SMEM), vmem] + [pl.BlockSpec(memory_space=pl.ANY)] * len(after),
+        out_specs=(vmem,) * n,
+        compiler_params=pltpu.CompilerParams(vmem_limit_bytes=VMEM),
+    )(place, inner, *after)
+    return result[0] if n == 1 else result
 
 
 outer_share = 1.0 - outer_rate * (1.0 + outer_decay)
@@ -385,8 +384,8 @@
         for (back, _), code in zip(gathered, rest):
             for d in range(NH):
                 column = (d + place_ref[4]) % NH * NZ + (place_ref[3] - back + NZ) % NZ
-                half = (1.0 - mix_share) * inner_ref[:, block_columns(column)]
-                out[:, block_columns(column)] = mix_share * decoded_outer(code[d]) + half
+                half = kept_share * (1.0 - mix_share) * inner_ref[:, block_columns(column)]
+                out[:, block_columns(column)] = kept_share * mix_share * decoded_outer(code[d]) + half
 
     vmem = pl.BlockSpec(memory_space=pltpu.VMEM)
     operands = [place, inner, *(codes for _, codes in gathered)]

time: 94.1 us -> 93.8 us (level)
    pallas_call x5 -> x3, Pallas kernels: 10.4 us -> 8.69 us  [run(): pl.pallas_call(body, out_shape=shapes, grid_spec=pltpu.PrefetchScalarGrid...]
    pallas_call x0 -> x2, Pallas kernels: none -> 1.23 us  [scatter_blocks(): pl.pallas_call(kernel, out_shape=(jax.ShapeDtypeStruct((NH, inner.shape[0...]
  transfers between devices with their start and end apart: 21 -> 21, of which waited for: 9 -> 9; matrix products, arithmetic and copies ran while one was open for 0% -> 0% of each run, Pallas kernels for 33% -> 32%
where the time goes in v5:
time: 93.8 us; the launch traced here: 93.7 us
  Pallas kernels  35 us (37%)
  starting transfers between devices  34.6 us (37%)
  waiting for transfers between devices  20.7 us (22%)
  local copies, waits for them, and re-layouts  2.46 us (3%)
  between operations  0.97 us (1%)
    pallas_call x16, Pallas kernels, run_whole(): pl.pallas_call(body, out_shape=shape, in_specs=[vmem] * count + [pl.Block...  22 us
    ppermute x14, starting transfers between devices, on_fsdp(): return lax.ppermute(value, 'fsdp', pairs)  17.7 us
    ppermute x7, starting transfers between devices, on_replica(): return lax.ppermute(value, 'replica', pairs)  16.9 us
    ppermute x14, waiting for transfers between devices, on_fsdp(): return lax.ppermute(value, 'fsdp', pairs)  13 us
    pallas_call x3, Pallas kernels, run(): pl.pallas_call(body, out_shape=shapes, grid_spec=pltpu.PrefetchScalarGrid...  8.69 us
    ppermute x7, waiting for transfers between devices, on_replica(): return lax.ppermute(value, 'replica', pairs)  7.65 us
    pallas_call x3, Pallas kernels, blend(): pl.pallas_call(kernel, out_shape=jax.ShapeDtypeStruct(inner.shape, jnp.fl...  3.05 us
    unnamed x14, local copies, waits for them, and re-layouts  2.37 us
  transfers between devices with their start and end apart: 21, of which 9 were waited for; matrix products, arithmetic and copies ran while one was open for 0% of the time, Pallas kernels for 32%

profile of v5, /device:TPU:0, one launch (start us, length us, event | category | flops | bytes accessed | tf_op | source)
XLA Modules:
  0.0 93.7 jit_solution(3295386780756829936)
XLA Ops:
  0.9 2.3 %copy-done.2 = bf16[1,512,4608]{2,1,0:T(8,128)(2,1)S(1)} copy-done((bf16[1,512,4608]{2,1,0:T(8,128)(2,1)S(1)}, bf16[1,512,4608]{2,1,0:T(8,128)(2,1)}, u32[]{:S(2)}) %copy-start.2) | copy-done | bytes 4718616
  3.2 3.1 %shard_map.110 = (bf16[2,1,288,512]{3,2,1,0:T(8,128)(2,1)S(1)}, bf16[2,1,288,512]{3,2,1,0:T(8,128)(2,1)S(1)}, bf16[2,3,288,512]{3,2,1,0:T(8,128)(2,1)S(1)}, bf16[2,3,288,512]{3,2,1,0:T(8,128)(2,1)S(1)}) custom-call(s32[5]{0:T(128)S(1)} %stack.23.refs_0_.place_ref, bf16[512,4608]{1,0:T(8,128)(2,1)S(1)} %bitcast.48), custom_call_target="tpu_custom_call" | custom-call | flops 1 | bytes 1 | tf_op jit(solution)/shard_map/pallas_call | solution.py:87
  7.6 2.1 %collective-permute-start.4 = (f32[2,288,256]{2,1,0:T(8,128)S(1)}, f32[2,288,256]{2,1,0:T(8,128)S(1)}, u32[]{:S(2)}, u32[]{:S(2)}) collective-permute-start(f32[2,288,256]{2,1,0:T(8,128)S(1)} %get-tuple-element.26), channel_id=1, source_target_pairs={{0,16},{16,32},{32,48},{48,0},{64,80},{80,96},{96,112},{112,64},{1... | collective-permute-start | bytes 1769480 | tf_op jit(solution)/shard_map/ppermute | solution.py:53
  9.7 2.2 %collective-permute-start.5 = (f32[2,288,256]{2,1,0:T(8,128)S(1)}, f32[2,288,256]{2,1,0:T(8,128)S(1)}, u32[]{:S(2)}, u32[]{:S(2)}) collective-permute-start(f32[2,288,256]{2,1,0:T(8,128)S(1)} %get-tuple-element.27), channel_id=1, source_target_pairs={{0,48},{16,0},{32,16},{48,32},{64,112},{80,64},{96,80},{112,96},{1... | collective-permute-start | bytes 1769480 | tf_op jit(solution)/shard_map/ppermute | solution.py:53
  12.6 1.6 %collective-permute-start.3 = (bf16[1,288,512]{2,1,0:T(8,128)(2,1)S(1)}, bf16[1,288,512]{2,1,0:T(8,128)(2,1)S(1)}, u32[]{:S(2)}, u32[]{:S(2)}) collective-permute-start(bf16[1,288,512]{2,1,0:T(8,128)(2,1)S(1)} %shard_map.111.refs_4_), channel_id=1, source_target_pairs={{0,2},{1,3},{2,0},{3,1},{4,6},{5,7},{6,4},{7,5},{8,10},{9,11},{10,... | collective-permute-start | bytes 884744 | tf_op jit(solution)/shard_map/ppermute | solution.py:49
  15.7 1.7 %collective-permute-start.7 = (bf16[2,288,768]{2,1,0:T(8,128)(2,1)S(1)}, bf16[2,288,768]{2,1,0:T(8,128)(2,1)S(1)}, u32[]{:S(2)}, u32[]{:S(2)}) collective-permute-start(bf16[2,288,768]{2,1,0:T(8,128)(2,1)S(1)} %shard_map.112.refs_4_), channel_id=1, source_target_pairs={{0,4},{1,5},{2,6},{3,7},{4,8},{5,9},{6,10},{7,11},{8,12},{9,13},{1... | collective-permute-start | bytes 2654216 | tf_op jit(solution)/shard_map/ppermute | solution.py:49
  17.3 1.5 %shard_map.113.refs_4_ = bf16[2,288,768]{2,1,0:T(8,128)(2,1)S(1)} custom-call(bf16[2,288,512]{2,1,0:T(8,128)(2,1)S(1)} %bitcast.45, bf16[2,288,512]{2,1,0:T(8,128)(2,1)S(1)} %collective-permute-done.2.refs_1_.refs_3_, bf16[512,2048]{1,0:T(8,128)(2,1)S(1)} %bitcast.20, bf16[512,2048]{1,0:T(8,128)(2,1)S(1)} %collective-permute-done.1.refs_3_.refs_5_, ...), custom_call_target="tpu_custom_call" | custom-call | tf_op jit(solution)/shard_map/pallas_call | solution.py:148
  18.8 1.7 %collective-permute-start.9 = (bf16[2,288,768]{2,1,0:T(8,128)(2,1)S(1)}, bf16[2,288,768]{2,1,0:T(8,128)(2,1)S(1)}, u32[]{:S(2)}, u32[]{:S(2)}) collective-permute-start(bf16[2,288,768]{2,1,0:T(8,128)(2,1)S(1)} %shard_map.113.refs_4_), channel_id=1, source_target_pairs={{0,12},{1,13},{2,14},{3,15},{4,0},{5,1},{6,2},{7,3},{8,4},{9,5},{1... | collective-permute-start | bytes 2654216 | tf_op jit(solution)/shard_map/ppermute | solution.py:49
  26.3 3.0 %collective-permute-start.10 = (f32[2,288,256]{2,1,0:T(8,128)S(1)}, f32[2,288,256]{2,1,0:T(8,128)S(1)}, u32[]{:S(2)}, u32[]{:S(2)}) collective-permute-start(f32[2,288,256]{2,1,0:T(8,128)S(1)} %shard_map.117.refs_4_), channel_id=1, source_target_pairs={{0,32},{16,48},{32,0},{48,16},{64,96},{80,112},{96,64},{112,80},{1... | collective-permute-start | bytes 1769480 | tf_op jit(solution)/shard_map/ppermute | solution.py:53
  29.3 1.6 %collective-permute-start.8 = (bf16[1,288,1024]{2,1,0:T(8,128)(2,1)S(1)}, bf16[1,288,1024]{2,1,0:T(8,128)(2,1)S(1)}, u32[]{:S(2)}, u32[]{:S(2)}) collective-permute-start(bf16[1,288,1024]{2,1,0:T(8,128)(2,1)S(1)} %shard_map.115.rest_0_), channel_id=1, source_target_pairs={{0,4},{1,5},{2,6},{3,7},{4,8},{5,9},{6,10},{7,11},{8,12},{9,13},{1... | collective-permute-start | bytes 1769480 | tf_op jit(solution)/shard_map/ppermute | solution.py:49
  30.9 5.1 %shard_map.118.refs_4_.refs_0_ = f32[3,288,2048]{2,1,0:T(8,128)S(1)} custom-call(bf16[6,288,512]{2,1,0:T(8,128)(2,1)S(1)} %bitcast.37, bf16[6,288,512]{2,1,0:T(8,128)(2,1)S(1)} %collective-permute-done.refs_4_.refs_1_, bf16[512,2048]{1,0:T(8,128)(2,1)S(1)} %bitcast.23, bf16[512,2048]{1,0:T(8,128)(2,1)S(1)} %collective-permute-done.1.refs_3_.refs_5_, ...), custom_call_target="tpu_custom_call" | custom-call | tf_op jit(solution)/shard_map/pallas_call | solution.py:148
  36.0 2.0 %shard_map.119.refs_7_.refs_0_ = f32[1,288,1536]{2,1,0:T(8,128)S(1)} custom-call(bf16[6,288,512]{2,1,0:T(8,128)(2,1)S(1)} %bitcast.38, bf16[6,288,512]{2,1,0:T(8,128)(2,1)S(1)} %collective-permute-done.refs_4_.refs_1_, bf16[512,2048]{1,0:T(8,128)(2,1)S(1)} %bitcast.24, bf16[512,2048]{1,0:T(8,128)(2,1)S(1)} %collective-permute-done.1.refs_3_.refs_5_, ...), custom_call_target="tpu_custom_call" | custom-call | tf_op jit(solution)/shard_map/pallas_call | solution.py:148
  40.8 1.9 %collective-permute-start.13 = (bf16[1,288,1024]{2,1,0:T(8,128)(2,1)S(1)}, bf16[1,288,1024]{2,1,0:T(8,128)(2,1)S(1)}, u32[]{:S(2)}, u32[]{:S(2)}) collective-permute-start(bf16[1,288,1024]{2,1,0:T(8,128)(2,1)S(1)} %shard_map.120.refs_5_), channel_id=1, source_target_pairs={{0,12},{1,13},{2,14},{3,15},{4,0},{5,1},{6,2},{7,3},{8,4},{9,5},{1... | collective-permute-start | bytes 1769480 | tf_op jit(solution)/shard_map/ppermute | solution.py:49
  44.5 2.8 %collective-permute-start.12 = (f32[2,288,256]{2,1,0:T(8,128)S(1)}, f32[2,288,256]{2,1,0:T(8,128)S(1)}, u32[]{:S(2)}, u32[]{:S(2)}) collective-permute-start(f32[2,288,256]{2,1,0:T(8,128)S(1)} %get-tuple-element.28.refs_5_.refs_1_), channel_id=1, source_target_pairs={{0,64},{16,80},{32,96},{48,112},{64,0},{80,16},{96,32},{112,48},{1... | collective-permute-start | bytes 1769480 | tf_op jit(solution)/shard_map/ppermute | solution.py:53
  48.5 3.6 %collective-permute-done.8.refs_6_.refs_3_ = bf16[1,288,1024]{2,1,0:T(8,128)(2,1)S(1)} collective-permute-done((bf16[1,288,1024]{2,1,0:T(8,128)(2,1)S(1)}, bf16[1,288,1024]{2,1,0:T(8,128)(2,1)S(1)}, u32[]{:S(2)}, u32[]{:S(2)}) %collective-permute-start.8) | collective-permute-done | bytes 589856 | tf_op jit(solution)/shard_map/ppermute | solution.py:49
  53.1 1.9 %collective-permute-start.17 = (bf16[1,288,768]{2,1,0:T(8,128)(2,1)S(1)}, bf16[1,288,768]{2,1,0:T(8,128)(2,1)S(1)}, u32[]{:S(2)}, u32[]{:S(2)}) collective-permute-start(bf16[1,288,768]{2,1,0:T(8,128)(2,1)S(1)} %shard_map.123.refs_4_), channel_id=1, source_target_pairs={{0,12},{1,13},{2,14},{3,15},{4,0},{5,1},{6,2},{7,3},{8,4},{9,5},{1... | collective-permute-start | bytes 1327112 | tf_op jit(solution)/shard_map/ppermute | solution.py:49
  57.1 3.3 %collective-permute-start.19 = (bf16[1,288,2048]{2,1,0:T(8,128)(2,1)S(1)}, bf16[1,288,2048]{2,1,0:T(8,128)(2,1)S(1)}, u32[]{:S(2)}, u32[]{:S(2)}) collective-permute-start(bf16[1,288,2048]{2,1,0:T(8,128)(2,1)S(1)} %shard_map.125.refs_5_), channel_id=1, source_target_pairs={{0,12},{1,13},{2,14},{3,15},{4,0},{5,1},{6,2},{7,3},{8,4},{9,5},{1... | collective-permute-start | bytes 3538952 | tf_op jit(solution)/shard_map/ppermute | solution.py:49
  62.6 3.7 %collective-permute-done.17.refs_4_ = bf16[1,288,768]{2,1,0:T(8,128)(2,1)S(1)} collective-permute-done((bf16[1,288,768]{2,1,0:T(8,128)(2,1)S(1)}, bf16[1,288,768]{2,1,0:T(8,128)(2,1)S(1)}, u32[]{:S(2)}, u32[]{:S(2)}) %collective-permute-start.17) | collective-permute-done | bytes 442400 | tf_op jit(solution)/shard_map/ppermute | solution.py:49
  69.3 2.1 %collective-permute-start.15 = (bf16[2,288,256]{2,1,0:T(8,128)(2,1)S(1)}, bf16[2,288,256]{2,1,0:T(8,128)(2,1)S(1)}, u32[]{:S(2)}, u32[]{:S(2)}) collective-permute-start(bf16[2,288,256]{2,1,0:T(8,128)(2,1)S(1)} %get-tuple-element.30.refs_5_.rest_0_.refs_0_), channel_id=1, source_target_pairs={{0,48},{16,0},{32,16},{48,32},{64,112},{80,64},{96,80},{112,96},{1... | collective-permute-start | bytes 884744 | tf_op jit(solution)/shard_map/ppermute | solution.py:53
  72.4 4.8 %collective-permute-done.16.refs_2_.rest_1_ = bf16[2,288,256]{2,1,0:T(8,128)(2,1)S(1)} collective-permute-done((bf16[2,288,256]{2,1,0:T(8,128)(2,1)S(1)}, bf16[2,288,256]{2,1,0:T(8,128)(2,1)S(1)}, u32[]{:S(2)}, u32[]{:S(2)}) %collective-permute-start.16) | collective-permute-done | bytes 294944 | tf_op jit(solution)/shard_map/ppermute | solution.py:53
  77.2 1.7 %collective-permute-done.15.refs_3_.rest_0_ = bf16[2,288,256]{2,1,0:T(8,128)(2,1)S(1)} collective-permute-done((bf16[2,288,256]{2,1,0:T(8,128)(2,1)S(1)}, bf16[2,288,256]{2,1,0:T(8,128)(2,1)S(1)}, u32[]{:S(2)}, u32[]{:S(2)}) %collective-permute-start.15) | collective-permute-done | bytes 294944 | tf_op jit(solution)/shard_map/ppermute | solution.py:53
  78.9 3.5 %collective-permute-start.18 = (bf16[2,288,256]{2,1,0:T(8,128)(2,1)S(1)}, bf16[2,288,256]{2,1,0:T(8,128)(2,1)S(1)}, u32[]{:S(2)}, u32[]{:S(2)}) collective-permute-start(bf16[2,288,256]{2,1,0:T(8,128)(2,1)S(1)} %shard_map.129.rest_3_), channel_id=1, source_target_pairs={{0,32},{16,48},{32,0},{48,16},{64,96},{80,112},{96,64},{112,80},{1... | collective-permute-start | bytes 884744 | tf_op jit(solution)/shard_map/ppermute | solution.py:53
  83.7 2.1 %collective-permute-done.11.refs_2_ = bf16[1,288,2048]{2,1,0:T(8,128)(2,1)S(1)} collective-permute-done((bf16[1,288,2048]{2,1,0:T(8,128)(2,1)S(1)}, bf16[1,288,2048]{2,1,0:T(8,128)(2,1)S(1)}, u32[]{:S(2)}, u32[]{:S(2)}) %collective-permute-start.11) | collective-permute-done | bytes 1179680 | tf_op jit(solution)/shard_map/ppermute | solution.py:49
  88.9 4.8 %shard_map.133 = (f32[288,2048]{1,0:T(8,128)}, f32[288,2048]{1,0:T(8,128)}, f32[288,2048]{1,0:T(8,128)}) custom-call(f32[288,2048]{1,0:T(8,128)S(1)} %get-tuple-element.31.rest_2_.refs_0_, f32[288,2048]{1,0:T(8,128)S(1)} %get-tuple-element.32.refs_1_, f32[288,2048]{1,0:T(8,128)S(1)} %get-tuple-element.33.refs_2_, f32[288,2048]{1,0:T(8,128)S(1)} %shard_map.132.refs_3_, ...), custom_call_target="tpu_custom_call" | custom-call | flops 1 | bytes 1 | tf_op jit(solution)/shard_map/pallas_call | solution.py:87
  (57 shorter events, 28.6 us)
Async XLA Ops:
  0.6 11.3 %collective-permute-start.1 = (bf16[512,2048]{1,0:T(8,128)(2,1)}, bf16[512,2048]{1,0:T(8,128)(2,1)S(1)}, u32[]{:S(2)}, u32[]{:S(2)}) collective-permute-start(bf16[512,2048]{1,0:T(8,128)(2,1)} %bitcast.17), channel_id=1, source_target_pairs={{0,1},{1,0},{2,3},{3,2},{4,5},{5,4},{6,7},{7,6},{8,9},{9,8},{10,11... | collective-permute-start | bytes 6291464 | tf_op jit(solution)/shard_map/ppermute | solution.py:49
  6.4 5.6 %copy-start = (bf16[1,512,2048]{2,1,0:T(8,128)(2,1)S(1)}, bf16[1,512,2048]{2,1,0:T(8,128)(2,1)}, u32[]{:S(2)}) copy-start(bf16[1,512,2048]{2,1,0:T(8,128)(2,1)} %param.13) | copy-start | bytes 6291460
  6.4 5.5 %collective-permute-start = (bf16[6,288,512]{2,1,0:T(8,128)(2,1)S(1)}, bf16[6,288,512]{2,1,0:T(8,128)(2,1)S(1)}, u32[]{:S(2)}, u32[]{:S(2)}) collective-permute-start(bf16[6,288,512]{2,1,0:T(8,128)(2,1)S(1)} %bitcast.51), channel_id=1, source_target_pairs={{0,1},{1,0},{2,3},{3,2},{4,5},{5,4},{6,7},{7,6},{8,9},{9,8},{10,11... | collective-permute-start | bytes 5308424 | tf_op jit(solution)/shard_map/ppermute | solution.py:49
  6.9 5.0 %collective-permute-start.2 = (bf16[2,288,512]{2,1,0:T(8,128)(2,1)S(1)}, bf16[2,288,512]{2,1,0:T(8,128)(2,1)S(1)}, u32[]{:S(2)}, u32[]{:S(2)}) collective-permute-start(bf16[2,288,512]{2,1,0:T(8,128)(2,1)S(1)} %bitcast.52), channel_id=1, source_target_pairs={{0,1},{1,0},{2,3},{3,2},{4,5},{5,4},{6,7},{7,6},{8,9},{9,8},{10,11... | collective-permute-start | bytes 1769480 | tf_op jit(solution)/shard_map/ppermute | solution.py:49
  7.6 18.1 %collective-permute-start.4 = (f32[2,288,256]{2,1,0:T(8,128)S(1)}, f32[2,288,256]{2,1,0:T(8,128)S(1)}, u32[]{:S(2)}, u32[]{:S(2)}) collective-permute-start(f32[2,288,256]{2,1,0:T(8,128)S(1)} %get-tuple-element.26), channel_id=1, source_target_pairs={{0,16},{16,32},{32,48},{48,0},{64,80},{80,96},{96,112},{112,64},{1... | collective-permute-start | bytes 1769480 | tf_op jit(solution)/shard_map/ppermute | solution.py:53
  9.7 16.0 %collective-permute-start.5 = (f32[2,288,256]{2,1,0:T(8,128)S(1)}, f32[2,288,256]{2,1,0:T(8,128)S(1)}, u32[]{:S(2)}, u32[]{:S(2)}) collective-permute-start(f32[2,288,256]{2,1,0:T(8,128)S(1)} %get-tuple-element.27), channel_id=1, source_target_pairs={{0,48},{16,0},{32,16},{48,32},{64,112},{80,64},{96,80},{112,96},{1... | collective-permute-start | bytes 1769480 | tf_op jit(solution)/shard_map/ppermute | solution.py:53
  12.6 9.2 %collective-permute-start.3 = (bf16[1,288,512]{2,1,0:T(8,128)(2,1)S(1)}, bf16[1,288,512]{2,1,0:T(8,128)(2,1)S(1)}, u32[]{:S(2)}, u32[]{:S(2)}) collective-permute-start(bf16[1,288,512]{2,1,0:T(8,128)(2,1)S(1)} %shard_map.111.refs_4_), channel_id=1, source_target_pairs={{0,2},{1,3},{2,0},{3,1},{4,6},{5,7},{6,4},{7,5},{8,10},{9,11},{10,... | collective-permute-start | bytes 884744 | tf_op jit(solution)/shard_map/ppermute | solution.py:49
  15.7 23.8 %collective-permute-start.7 = (bf16[2,288,768]{2,1,0:T(8,128)(2,1)S(1)}, bf16[2,288,768]{2,1,0:T(8,128)(2,1)S(1)}, u32[]{:S(2)}, u32[]{:S(2)}) collective-permute-start(bf16[2,288,768]{2,1,0:T(8,128)(2,1)S(1)} %shard_map.112.refs_4_), channel_id=1, source_target_pairs={{0,4},{1,5},{2,6},{3,7},{4,8},{5,9},{6,10},{7,11},{8,12},{9,13},{1... | collective-permute-start | bytes 2654216 | tf_op jit(solution)/shard_map/ppermute | solution.py:49
  18.8 23.9 %collective-permute-start.9 = (bf16[2,288,768]{2,1,0:T(8,128)(2,1)S(1)}, bf16[2,288,768]{2,1,0:T(8,128)(2,1)S(1)}, u32[]{:S(2)}, u32[]{:S(2)}) collective-permute-start(bf16[2,288,768]{2,1,0:T(8,128)(2,1)S(1)} %shard_map.113.refs_4_), channel_id=1, source_target_pairs={{0,12},{1,13},{2,14},{3,15},{4,0},{5,1},{6,2},{7,3},{8,4},{9,5},{1... | collective-permute-start | bytes 2654216 | tf_op jit(solution)/shard_map/ppermute | solution.py:49
  21.8 21.9 %collective-permute-start.6 = (bf16[3,288,512]{2,1,0:T(8,128)(2,1)S(1)}, bf16[3,288,512]{2,1,0:T(8,128)(2,1)S(1)}, u32[]{:S(2)}, u32[]{:S(2)}) collective-permute-start(bf16[3,288,512]{2,1,0:T(8,128)(2,1)S(1)} %shard_map.114.refs_7_), channel_id=1, source_target_pairs={{0,2},{1,3},{2,0},{3,1},{4,6},{5,7},{6,4},{7,5},{8,10},{9,11},{10,... | collective-permute-start | bytes 2654216 | tf_op jit(solution)/shard_map/ppermute | solution.py:49
  26.3 17.4 %collective-permute-start.10 = (f32[2,288,256]{2,1,0:T(8,128)S(1)}, f32[2,288,256]{2,1,0:T(8,128)S(1)}, u32[]{:S(2)}, u32[]{:S(2)}) collective-permute-start(f32[2,288,256]{2,1,0:T(8,128)S(1)} %shard_map.117.refs_4_), channel_id=1, source_target_pairs={{0,32},{16,48},{32,0},{48,16},{64,96},{80,112},{96,64},{112,80},{1... | collective-permute-start | bytes 1769480 | tf_op jit(solution)/shard_map/ppermute | solution.py:53
  29.3 22.7 %collective-permute-start.8 = (bf16[1,288,1024]{2,1,0:T(8,128)(2,1)S(1)}, bf16[1,288,1024]{2,1,0:T(8,128)(2,1)S(1)}, u32[]{:S(2)}, u32[]{:S(2)}) collective-permute-start(bf16[1,288,1024]{2,1,0:T(8,128)(2,1)S(1)} %shard_map.115.rest_0_), channel_id=1, source_target_pairs={{0,4},{1,5},{2,6},{3,7},{4,8},{5,9},{6,10},{7,11},{8,12},{9,13},{1... | collective-permute-start | bytes 1769480 | tf_op jit(solution)/shard_map/ppermute | solution.py:49
  40.8 15.4 %collective-permute-start.13 = (bf16[1,288,1024]{2,1,0:T(8,128)(2,1)S(1)}, bf16[1,288,1024]{2,1,0:T(8,128)(2,1)S(1)}, u32[]{:S(2)}, u32[]{:S(2)}) collective-permute-start(bf16[1,288,1024]{2,1,0:T(8,128)(2,1)S(1)} %shard_map.120.refs_5_), channel_id=1, source_target_pairs={{0,12},{1,13},{2,14},{3,15},{4,0},{5,1},{6,2},{7,3},{8,4},{9,5},{1... | collective-permute-start | bytes 1769480 | tf_op jit(solution)/shard_map/ppermute | solution.py:49
  44.5 17.1 %collective-permute-start.12 = (f32[2,288,256]{2,1,0:T(8,128)S(1)}, f32[2,288,256]{2,1,0:T(8,128)S(1)}, u32[]{:S(2)}, u32[]{:S(2)}) collective-permute-start(f32[2,288,256]{2,1,0:T(8,128)S(1)} %get-tuple-element.28.refs_5_.refs_1_), channel_id=1, source_target_pairs={{0,64},{16,80},{32,96},{48,112},{64,0},{80,16},{96,32},{112,48},{1... | collective-permute-start | bytes 1769480 | tf_op jit(solution)/shard_map/ppermute | solution.py:53
  47.3 14.3 %collective-permute-start.14 = (bf16[1,288,768]{2,1,0:T(8,128)(2,1)S(1)}, bf16[1,288,768]{2,1,0:T(8,128)(2,1)S(1)}, u32[]{:S(2)}, u32[]{:S(2)}) collective-permute-start(bf16[1,288,768]{2,1,0:T(8,128)(2,1)S(1)} %shard_map.121.refs_11_), channel_id=1, source_target_pairs={{0,4},{1,5},{2,6},{3,7},{4,8},{5,9},{6,10},{7,11},{8,12},{9,13},{1... | collective-permute-start | bytes 1327112 | tf_op jit(solution)/shard_map/ppermute | solution.py:49
  53.1 13.2 %collective-permute-start.17 = (bf16[1,288,768]{2,1,0:T(8,128)(2,1)S(1)}, bf16[1,288,768]{2,1,0:T(8,128)(2,1)S(1)}, u32[]{:S(2)}, u32[]{:S(2)}) collective-permute-start(bf16[1,288,768]{2,1,0:T(8,128)(2,1)S(1)} %shard_map.123.refs_4_), channel_id=1, source_target_pairs={{0,12},{1,13},{2,14},{3,15},{4,0},{5,1},{6,2},{7,3},{8,4},{9,5},{1... | collective-permute-start | bytes 1327112 | tf_op jit(solution)/shard_map/ppermute | solution.py:49
  55.9 29.9 %collective-permute-start.11 = (bf16[1,288,2048]{2,1,0:T(8,128)(2,1)S(1)}, bf16[1,288,2048]{2,1,0:T(8,128)(2,1)S(1)}, u32[]{:S(2)}, u32[]{:S(2)}) collective-permute-start(bf16[1,288,2048]{2,1,0:T(8,128)(2,1)S(1)} %shard_map.124.refs_4_), channel_id=1, source_target_pairs={{0,4},{1,5},{2,6},{3,7},{4,8},{5,9},{6,10},{7,11},{8,12},{9,13},{1... | collective-permute-start | bytes 3538952 | tf_op jit(solution)/shard_map/ppermute | solution.py:49
  57.1 31.9 %collective-permute-start.19 = (bf16[1,288,2048]{2,1,0:T(8,128)(2,1)S(1)}, bf16[1,288,2048]{2,1,0:T(8,128)(2,1)S(1)}, u32[]{:S(2)}, u32[]{:S(2)}) collective-permute-start(bf16[1,288,2048]{2,1,0:T(8,128)(2,1)S(1)} %shard_map.125.refs_5_), channel_id=1, source_target_pairs={{0,12},{1,13},{2,14},{3,15},{4,0},{5,1},{6,2},{7,3},{8,4},{9,5},{1... | collective-permute-start | bytes 3538952 | tf_op jit(solution)/shard_map/ppermute | solution.py:49
  67.6 20.6 %collective-permute-start.20 = (bf16[1,288,1536]{2,1,0:T(8,128)(2,1)S(1)}, bf16[1,288,1536]{2,1,0:T(8,128)(2,1)S(1)}, u32[]{:S(2)}, u32[]{:S(2)}) collective-permute-start(bf16[1,288,1536]{2,1,0:T(8,128)(2,1)S(1)} %shard_map.127.rest_1_), channel_id=1, source_target_pairs={{0,2},{1,3},{2,0},{3,1},{4,6},{5,7},{6,4},{7,5},{8,10},{9,11},{10,... | collective-permute-start | bytes 2654216 | tf_op jit(solution)/shard_map/ppermute | solution.py:49
  68.2 9.0 %collective-permute-start.16 = (bf16[2,288,256]{2,1,0:T(8,128)(2,1)S(1)}, bf16[2,288,256]{2,1,0:T(8,128)(2,1)S(1)}, u32[]{:S(2)}, u32[]{:S(2)}) collective-permute-start(bf16[2,288,256]{2,1,0:T(8,128)(2,1)S(1)} %get-tuple-element.30.refs_5_.rest_0_.refs_0_), channel_id=1, source_target_pairs={{0,16},{16,32},{32,48},{48,0},{64,80},{80,96},{96,112},{112,64},{1... | collective-permute-start | bytes 884744 | tf_op jit(solution)/shard_map/ppermute | solution.py:53
  69.3 9.6 %collective-permute-start.15 = (bf16[2,288,256]{2,1,0:T(8,128)(2,1)S(1)}, bf16[2,288,256]{2,1,0:T(8,128)(2,1)S(1)}, u32[]{:S(2)}, u32[]{:S(2)}) collective-permute-start(bf16[2,288,256]{2,1,0:T(8,128)(2,1)S(1)} %get-tuple-element.30.refs_5_.rest_0_.refs_0_), channel_id=1, source_target_pairs={{0,48},{16,0},{32,16},{48,32},{64,112},{80,64},{96,80},{112,96},{1... | collective-permute-start | bytes 884744 | tf_op jit(solution)/shard_map/ppermute | solution.py:53
  78.9 6.9 %copy-start.3 = (f32[1,288,2048]{2,1,0:T(8,128)S(1)}, f32[1,288,2048]{2,1,0:T(8,128)}, u32[]{:S(2)}) copy-start(f32[1,288,2048]{2,1,0:T(8,128)} %param.8) | copy-start | bytes 7077892
  78.9 6.9 %copy-start.4 = (f32[1,288,2048]{2,1,0:T(8,128)S(1)}, f32[1,288,2048]{2,1,0:T(8,128)}, u32[]{:S(2)}) copy-start(f32[1,288,2048]{2,1,0:T(8,128)} %param.9) | copy-start | bytes 7077892
  78.9 8.3 %collective-permute-start.18 = (bf16[2,288,256]{2,1,0:T(8,128)(2,1)S(1)}, bf16[2,288,256]{2,1,0:T(8,128)(2,1)S(1)}, u32[]{:S(2)}, u32[]{:S(2)}) collective-permute-start(bf16[2,288,256]{2,1,0:T(8,128)(2,1)S(1)} %shard_map.129.rest_3_), channel_id=1, source_target_pairs={{0,32},{16,48},{32,0},{48,16},{64,96},{80,112},{96,64},{112,80},{1... | collective-permute-start | bytes 884744 | tf_op jit(solution)/shard_map/ppermute | solution.py:53
  (4 other events, 12.0 us)
